TPU v7x, 256 devices: a whole 4x4x8 slice. The times are simulated.
256 devices in a mesh: dp: 32 (over y_hi, z, core), tensor: 8 (over y_lo, x).
Axes of the slice: x: 4, y: 4 (y_hi: 2, y_lo: 2; y = y_hi * 2 + y_lo), z: 8, core: 2. Of those that a mesh axis runs over, the one named last changes fastest.
Arguments:
- activations: bfloat16 [2, 8192, 14848], P(None, 'dp', 'tensor'), may hold values from -6 to 6
- cotangent: bfloat16 [2, 8192, 14848], P(None, 'dp', 'tensor'), may hold values from -6 to 6
- rewards: float32 [64], P('dp'), may hold values from -6 to 6
- group_of: int32 [64], P('dp'), may hold values from 0 to 15
- layer_owner: int32 [2], replicated, may hold values from 0 to 31
- adapter_a: bfloat16 [32, 2, 64, 14848], P('dp', None, None, 'tensor'), may hold values from -6 to 6
- adapter_b: bfloat16 [32, 2, 64, 14848], P('dp', None, None, 'tensor'), may hold values from -6 to 6
- frozen_query_part: bfloat16 [2, 2, 2048, 14848], P(None, None, 'dp', 'tensor'), may hold values from -32 to 32
- decode_in: bfloat16 [2, 2, 2048, 14848], P(None, None, 'dp', 'tensor'), may hold values from -6 to 6
- kv_cache: bfloat16 [2, 2048, 8, 96, 128], P(None, 'dp', 'tensor'), may hold values from -32 to 32
- new_kv: bfloat16 [2, 2, 2048, 8, 128], P(None, None, 'dp', 'tensor'), may hold values from -6 to 6
- lengths: int32 [2048], P('dp'), may hold values from 2 to 96, as said below
Outputs:
- new_a: bfloat16 [2, 64, 14848], P(None, None, 'tensor')
- revised_up_factors: bfloat16 [2, 64, 14848], P(None, None, 'tensor')
- attended: bfloat16 [2, 2, 2048, 14848], P(None, None, 'dp', 'tensor')
Inputs may be any that keep to these rules, and one draw needn't show every extreme that they name: `layer_owner`: index along dp of the replica whose copy of layer l's adapter is current. `lengths`: in each aligned block of 64 rows some row has all 96 slots valid.
All inputs are finite; a program needn't handle non-finite values.
Results may differ from a plain program's by a relative error of at most 0.02525.
Values may be sent and summed in bfloat16 or wider, within the bound.
No kernel may reach another device: no remote copies, remote signals or barrier semaphores. Data moves between devices by JAX's collectives and lax.ppermute only.
A program may use at most 64 MiB of HBM per device.

v0:
```python
import math

import jax
import jax.numpy as jnp
from jax import lax
from jax.sharding import PartitionSpec as P

D = 14848
R = 64


rate_a = 0.5
rate_b = 0.05


def broadcast(value, axis, root):
    mine = lax.axis_index(axis) == root
    return lax.psum(jnp.where(mine, value, jnp.zeros_like(value)), axis)


def advantage_of(rewards, group_of, groups_all):
    labels = jnp.arange(groups_all, dtype=jnp.int32)
    member = (group_of[:, None] == labels[None, :]).astype(jnp.float32)
    group_sum, group_count = lax.psum(
        (jnp.sum(member * rewards[:, None], axis=0), jnp.sum(member, axis=0)), "dp"
    )
    group_mean = group_sum / jnp.maximum(group_count, 1.0)
    return rewards - jnp.sum(member * group_mean[None, :], axis=1)


def update_factors(factor_a, factor_b, grad_a_part, grad_b_part):
    grad_a, grad_b = lax.psum((grad_a_part, grad_b_part), "dp")
    fresh_a = (factor_a.astype(jnp.float32) - rate_a * grad_a).astype(jnp.bfloat16)
    initial_up_factor = (factor_b.astype(jnp.float32) - rate_b * grad_b).astype(jnp.bfloat16)
    return (fresh_a, initial_up_factor)


def shards(
    activations,
    cotangent,
    rewards,
    group_of,
    layer_owner,
    adapter_a,
    adapter_b,
    frozen_query_part,
    decode_in,
    kv_cache,
    new_kv,
    lengths,
):
    layers = activations.shape[0]
    tokens_dev = activations.shape[1]
    scale_a = D ** (-0.5)
    up_factor_scale = R ** (-0.5)
    groups_all = lax.axis_size("dp") * rewards.shape[0] // 4
    advantage = advantage_of(rewards, group_of, groups_all)
    tok_adv = jnp.repeat(advantage, tokens_dev // rewards.shape[0])
    updated_a = []
    updated_b = []
    for layer_index in range(layers):
        stacked = jnp.stack([adapter_a[0, layer_index], adapter_b[0, layer_index]])
        current = broadcast(stacked, "dp", layer_owner[layer_index])
        factor_a = current[0]
        factor_b = current[1]
        inputs = activations[layer_index]
        weighted = (tok_adv[:, None] * cotangent[layer_index].astype(jnp.float32)).astype(
            jnp.bfloat16
        )
        low_part = jnp.einsum("td,kd->tk", inputs, factor_a, preferred_element_type=jnp.float32)
        back_part = jnp.einsum("td,kd->tk", weighted, factor_b, preferred_element_type=jnp.float32)
        low_sum, back_sum = lax.psum((low_part, back_part), "tensor")
        low_rank = (low_sum * scale_a).astype(jnp.bfloat16)
        back_rank = (back_sum * up_factor_scale).astype(jnp.bfloat16)
        grad_a_part = (
            jnp.einsum("tk,td->kd", back_rank, inputs, preferred_element_type=jnp.float32) * scale_a
        )
        grad_b_part = (
            jnp.einsum("tk,td->kd", low_rank, weighted, preferred_element_type=jnp.float32)
            * up_factor_scale
        )
        fresh_a, initial_up_factor = update_factors(factor_a, factor_b, grad_a_part, grad_b_part)
        updated_a.append(fresh_a)
        updated_b.append(initial_up_factor)
    new_a = jnp.stack(updated_a)
    revised_up_factors = jnp.stack(updated_b)
    rank_part = jnp.einsum("slrd,lkd->slrk", decode_in, new_a, preferred_element_type=jnp.float32)
    rank_sum = lax.psum(rank_part, "tensor")
    adapter_rank_size = (rank_sum * scale_a).astype(jnp.bfloat16)
    adapter_weight_change = jnp.einsum(
        "jpax,pxt->jpat", adapter_rank_size, revised_up_factors, preferred_element_type=jnp.float32
    )
    decode_query_matrix = (
        frozen_query_part.astype(jnp.float32) + up_factor_scale * adapter_weight_change
    ).astype(jnp.bfloat16)
    step_count = decode_query_matrix.shape[0]
    rows_dev = decode_query_matrix.shape[2]
    width_dev = decode_query_matrix.shape[3]
    kv_local = kv_cache.shape[2]
    cache_slot_total = kv_cache.shape[3]
    head_dim = kv_cache.shape[4] // 2
    per_kv = width_dev // (kv_local * head_dim)
    query_heads = decode_query_matrix.reshape(
        step_count, layers, rows_dev, kv_local, per_kv, head_dim
    )
    cache_keys = kv_cache[..., :head_dim]
    cache_values = kv_cache[..., head_dim:]
    fresh_keys = new_kv[..., :head_dim]
    fresh_values = new_kv[..., head_dim:]
    old_scores = jnp.einsum(
        "slrkgd,lrkpd->slrkgp", query_heads, cache_keys, preferred_element_type=jnp.float32
    ) / math.sqrt(head_dim)
    slot_valid = jnp.arange(cache_slot_total, dtype=jnp.int32)[None, :] < lengths[:, None]
    old_scores = jnp.where(slot_valid[None, None, :, None, None, :], old_scores, -jnp.inf)
    new_scores = jnp.einsum(
        "slrkgd,tlrkd->slrkgt", query_heads, fresh_keys, preferred_element_type=jnp.float32
    ) / math.sqrt(head_dim)
    causal = jnp.arange(step_count)[None, :] <= jnp.arange(step_count)[:, None]
    new_scores = jnp.where(causal[:, None, None, None, None, :], new_scores, -jnp.inf)
    peak_score = jnp.maximum(jnp.max(old_scores, axis=-1), jnp.max(new_scores, axis=-1))
    old_exp = jnp.exp(old_scores - peak_score[..., None])
    new_exp = jnp.exp(new_scores - peak_score[..., None])
    denominator = jnp.sum(old_exp, axis=-1) + jnp.sum(new_exp, axis=-1)
    old_weight = (old_exp / denominator[..., None]).astype(jnp.bfloat16)
    new_weight = (new_exp / denominator[..., None]).astype(jnp.bfloat16)
    combined = jnp.einsum(
        "slrkgp,lrkpd->slrkgd", old_weight, cache_values, preferred_element_type=jnp.float32
    )
    combined = combined + jnp.einsum(
        "slrkgt,tlrkd->slrkgd", new_weight, fresh_values, preferred_element_type=jnp.float32
    )
    attended = combined.astype(jnp.bfloat16).reshape(step_count, layers, rows_dev, width_dev)
    return (new_a, revised_up_factors, attended)


def solution(mesh):
    return jax.shard_map(
        shards,
        mesh=mesh,
        in_specs=(
            P(None, "dp", "tensor"),
            P(None, "dp", "tensor"),
            P("dp"),
            P("dp"),
            P(),
            P("dp", None, None, "tensor"),
            P("dp", None, None, "tensor"),
            P(None, None, "dp", "tensor"),
            P(None, None, "dp", "tensor"),
            P(None, "dp", "tensor", None, None),
            P(None, None, "dp", "tensor", None),
            P("dp"),
        ),
        out_specs=(P(None, None, "tensor"), P(None, None, "tensor"), P(None, None, "dp", "tensor")),
        check_vma=False,
    )
```

profile of v0, /device:TPU:1, one launch (start us, length us, event | category | flops | bytes accessed | tf_op | source)
XLA Modules:
  0.0 749.6 jit_solution(9130117386965405720)
XLA Ops:
  7.2 0.0 all-reduce.15.cloned.1.call-start
  7.2 1.3 fusion.83
  9.9 1.1 slice_bitcast_fusion.7
  11.0 1.2 slice_bitcast_fusion.6
  12.2 1.1 maximum_select_fusion
  13.3 0.0 all-reduce.15.cloned.1.call-update
  13.4 0.0 all-reduce.13.cloned.1.call-start
  13.4 0.1 convert_reduce_fusion
  13.5 69.1 %all-reduce = (f32[16]{0:T(128)S(1)}, f32[16]{0:T(128)S(1)}) all-reduce(f32[16]{0:T(128)S(1)} %get-tuple-element.7, f32[16]{0:T(128)S(1)} %get-tuple-element.6), channel_id=1, replica_groups=mesh['dp'=32,'tensor'=8] {'dp'}, use_global_device_ids=true, to_apply=%region_2.0 | all-reduce | flops 32 | bytes 256 | tf_op jit(solution)/shard_map/psum | solution.py:24
  82.7 0.2 select_reduce_fusion
  82.9 0.1 broadcast_bitcast_fusion
  82.9 199.1 %all-reduce.15.cloned.1.call-done = (bf16[2,64,1856]{2,1,0:T(8,128)(2,1)}, bf16[2,64,1856]{2,1,0:T(8,128)(2,1)}) async-done(((bf16[2,64,1856]{2,1,0:T(8,128)(2,1)}, bf16[2,64,1856]{2,1,0:T(8,128)(2,1)}), (bf16[2,64,1856]{2,1,0:T(8,128)(2,1)}, bf16[2,64,1856]{2,1,0:T(8,128)(2,1)})) %all-reduce.15.cloned.1.call-update) | async-done | bytes 950288 | tf_op jit(solution)/shard_map/psum | solution.py:18
  282.0 2.0 convolution_bitcast_fusion.1
  284.0 1.9 convolution_bitcast_fusion.2
  285.9 1.0 fusion.39
  286.9 1.0 fusion.43
  287.8 0.0 all-reduce.13.cloned.1.call-update
  287.8 0.0 all-reduce.11.cloned.1.call-start
  287.9 71.7 %all-reduce.13.cloned.1.call-done = (f32[256,64]{0,1:T(8,128)}, f32[256,64]{0,1:T(8,128)}, f32[256,64]{0,1:T(8,128)}, f32[256,64]{0,1:T(8,128)}) async-done(((f32[256,64]{0,1:T(8,128)}, f32[256,64]{0,1:T(8,128)}, f32[256,64]{0,1:T(8,128)}, f32[256,64]{0,1:T(8,128)}), (f32[256,64]{0,1:T(8,128)}, f32[256,64]{0,1:T(8,128)}, f32[256,64]{0,1:T(8,128)}, f32[256,64]{0,1:T(8,128)})) %all-reduce.13.cloned.1.call-update) | async-done | bytes 262160 | tf_op jit(solution)/shard_map/psum | solution.py:72
  359.6 2.2 convolution_multiply_fusion.3
  361.8 2.0 convolution_multiply_fusion.4
  363.9 1.2 convolution_multiply_fusion.1
  365.1 1.2 convolution_multiply_fusion.2
  366.3 0.0 all-reduce.11.cloned.1.call-update
  366.3 0.2 all-reduce.9.cloned.1.call-start
  366.6 0.1 iota_compare_fusion
  366.7 0.6 fusion.82
  367.3 272.6 %all-reduce.11.cloned.1.call-done = (f32[64,1856]{1,0:T(8,128)}, f32[64,1856]{1,0:T(8,128)}, f32[64,1856]{1,0:T(8,128)}, f32[64,1856]{1,0:T(8,128)}) async-done(((f32[64,1856]{1,0:T(8,128)}, f32[64,1856]{1,0:T(8,128)}, f32[64,1856]{1,0:T(8,128)}, f32[64,1856]{1,0:T(8,128)}), (f32[64,1856]{1,0:T(8,128)}, f32[64,1856]{1,0:T(8,128)}, f32[64,1856]{1,0:T(8,128)}, ...) | async-done | bytes 1900560 | tf_op jit(solution)/shard_map/psum | solution.py:32
  640.0 1.4 fusion.66
  641.4 0.1 copy-done.10
  641.4 0.1 fusion.65
  641.6 0.1 pad_maximum_fusion
  641.7 1.3 convolution_bitcast_fusion
  642.9 0.0 all-reduce.9.cloned.1.call-update
  643.0 0.1 pad_maximum_fusion.1
  643.0 71.6 %all-reduce.9.cloned.1.call-done = f32[2,2,64,64]{2,3,0,1:T(8,128)} async-done(((f32[2,2,64,64]{2,3,0,1:T(8,128)}), f32[2,2,64,64]{2,3,0,1:T(8,128)}) %all-reduce.9.cloned.1.call-update) | async-done | bytes 65552 | tf_op jit(solution)/shard_map/psum | solution.py:88
  714.6 1.4 fusion.11
  716.0 3.2 reshape.150
  719.2 4.6 fusion.84
  723.8 4.3 fusion.2
  728.1 0.1 max.13
  728.2 0.5 fusion.67
  728.7 2.6 fusion.1
  731.3 0.1 add.45
  731.4 6.3 fusion.3
  737.7 1.0 fusion.26
  738.7 2.1 reshape.149
  740.8 2.2 copy.50
  (44 shorter events, 0.1 us)
Async XLA Ops:
  7.2 634.5 %copy-start = (bf16[2,2,64,1856]{3,2,1,0:T(8,128)(2,1)S(1)}, bf16[2,2,64,1856]{3,2,1,0:T(8,128)(2,1)}, u32[]{:S(2)}) copy-start(bf16[2,2,64,1856]{3,2,1,0:T(8,128)(2,1)} %param.20) | copy-start | bytes 2850820
  7.2 274.8 %all-reduce.15.cloned.1.call-start = ((), (), s32[]{:S(2)}) async-start(), calls=%async_computation.3 | async-start | bytes 1966080 | tf_op jit(solution)/shard_map/psum | solution.py:18
  11.0 2.4 copy-start.14
  11.0 2.4 copy-start.15
  11.0 271.0 %copy-start.3 = (bf16[2,256,1856]{1,2,0:T(8,128)(2,1)S(1)}, bf16[2,256,1856]{1,2,0:T(8,128)(2,1)}, u32[]{:S(2)}) copy-start(bf16[2,256,1856]{1,2,0:T(8,128)(2,1)} %param.12) | copy-start | bytes 5701636
  13.4 346.3 %all-reduce.13.cloned.1.call-start = ((), (), s32[]{:S(2)}) async-start(), calls=%async_computation.2 | async-start | bytes 524288 | tf_op jit(solution)/shard_map/psum | solution.py:72
  282.0 3.9 copy-start.7
  282.0 3.9 copy-start.17
  282.0 4.9 copy-start.6
  287.8 352.1 %all-reduce.11.cloned.1.call-start = ((), (), s32[]{:S(2)}) async-start(), calls=%async_computation.1 | async-start | bytes 3932160 | tf_op jit(solution)/shard_map/psum | solution.py:32
  359.6 4.2 copy-start.18
  359.6 4.2 copy-start.20
  359.6 5.5 copy-start.19
  365.1 1.5 copy-start.13
  365.1 1.6 copy-start.11
  365.1 274.9 %copy-start.8 = (bf16[2,64,1856]{2,1,0:T(8,128)(2,1)S(1)}, bf16[2,64,1856]{2,1,0:T(8,128)(2,1)}, u32[]{:S(2)}) copy-start(bf16[2,64,1856]{2,1,0:T(8,128)(2,1)} %get-tuple-element.18) | copy-start | bytes 1425412
  366.3 348.3 %all-reduce.9.cloned.1.call-start = ((), (), s32[]{:S(2)}) async-start(), calls=%async_computation | async-start | bytes 262144 | tf_op jit(solution)/shard_map/psum | solution.py:88
  640.0 1.4 copy-start.9
  640.0 1.5 copy-start.10
  641.6 73.1 %copy-start.4 = (bf16[2,2,64,1856]{3,2,1,0:T(8,128)(2,1)S(1)}, bf16[2,2,64,1856]{3,2,1,0:T(8,128)(2,1)}, u32[]{:S(2)}) copy-start(bf16[2,2,64,1856]{3,2,1,0:T(8,128)(2,1)} %param.19) | copy-start | bytes 2850820
  641.6 1.3 copy-start.5
  643.0 76.1 %copy-start.2 = (bf16[2,64,1856]{2,1,0:T(8,128)(2,1)}, bf16[2,64,1856]{2,1,0:T(8,128)(2,1)S(1)}, u32[]{:S(2)}) copy-start(bf16[2,64,1856]{2,1,0:T(8,128)(2,1)S(1)} %pad_maximum_fusion.1) | copy-start | bytes 1425412
  716.0 3.2 copy-start.12
  719.2 4.7 copy-start.1
  728.7 2.7 copy-start.16
Sparse Core Ops, SparseCore 0:
  13.5 268.4 all-reduce.14
  288.0 71.6 all-reduce.12
  366.5 273.4 all-reduce.10
  643.2 71.3 all-reduce.8
where the time goes:
time: 754 us; the launch traced here: 750 us
  waiting for transfers between devices  615 us (82%)
  blocking collectives  69.1 us (9%)
  matrix products  31.4 us (4%)
  between operations  15.3 us (2%)
  local copies, waits for them, and re-layouts  12 us (2%)
    psum x1, waiting for transfers between devices, update_factors(): grad_a, grad_b = lax.psum((grad_a_part, grad_b_part), 'dp')  273 us
    psum x1, waiting for transfers between devices, broadcast(): return lax.psum(jnp.where(mine, value, jnp.zeros_like(value)), axis)  199 us
    psum x1, waiting for transfers between devices, shards(): low_sum, back_sum = lax.psum((low_part, back_part), 'tensor')  71.7 us
    psum x1, waiting for transfers between devices, shards(): rank_sum = lax.psum(rank_part, 'tensor')  71.6 us
    psum x1, blocking collectives, advantage_of(): lax.psum((jnp.sum(member * rewards[:, None], axis=0), jnp.sum(member, axi...  69.1 us
  transfers between devices with their start and end apart: 4, of which 4 were waited for; matrix products, arithmetic and copies ran while one was open for 0% of the time, Pallas kernels for 0%

commit v1 on v0

v1 whole, which is shorter than its diff:
```python
import math

import jax
import jax.numpy as jnp
from jax import lax
from jax.sharding import PartitionSpec as P

D = 14848
R = 64
GROUPS_PER_COMPLETION = 4

rate_a = 0.5
rate_b = 0.05

f32 = jnp.float32
bf16 = jnp.bfloat16


def pick(array, index, axis=0):
    return lax.dynamic_index_in_dim(array, index, axis, keepdims=False)


def split3(x):
    hi = lax.reduce_precision(x, 8, 7)
    mid = lax.reduce_precision(x - hi, 8, 7)
    lo = lax.reduce_precision(x - hi - mid, 8, 7)
    return hi, mid, lo


def shards(
    activations,
    cotangent,
    rewards,
    group_of,
    layer_owner,
    adapter_a,
    adapter_b,
    frozen_query_part,
    decode_in,
    kv_cache,
    new_kv,
    lengths,
):
    n_dp = lax.axis_size("dp")
    n_tensor = lax.axis_size("tensor")
    chips = n_dp // 2
    index = lax.axis_index("dp")
    core = index % 2
    chip = index // 2
    other = 1 - core
    swap = [(i, i ^ 1) for i in range(n_dp)]
    same_core = [[i for i in range(n_dp) if i % 2 == c] for c in range(2)]
    scale_a = D ** (-0.5)
    scale_b = R ** (-0.5)
    width = activations.shape[2]
    completions = rewards.shape[0]
    tokens = activations.shape[1]

    def core_swap(x):
        return lax.ppermute(x, "dp", swap)

    def across_chips(x):
        return lax.all_to_all(x, "dp", 0, 0, axis_index_groups=same_core)

    def across_tensor(x):
        return lax.all_to_all(x, "tensor", 0, 0)

    own_info = jnp.stack([rewards, group_of.astype(f32)])
    far_info = core_swap(own_info)
    own_factors = jnp.concatenate([pick(adapter_a[0], core), pick(adapter_b[0], core)])
    far_factors = core_swap(
        jnp.concatenate([pick(adapter_a[0], other), pick(adapter_b[0], other)])
    )
    far_act = core_swap(pick(activations, other))
    far_cot = core_swap(pick(cotangent, other))
    far_dec = core_swap(pick(decode_in, other, 1))
    own_act = pick(activations, core)
    own_cot = pick(cotangent, core)
    own_dec = pick(decode_in, core, 1)
    owner = pick(layer_owner, core)
    candidate = jnp.where(owner % 2 == core, own_factors, far_factors)

    info = jnp.concatenate([own_info, far_info], axis=1)
    packed = jnp.concatenate([*split3(info[0]), info[1]]).astype(bf16)
    rows = candidate.shape[0] // chips
    tail = jnp.zeros((rows, 64), bf16).at[0, : packed.shape[0]].set(packed)
    message = jnp.concatenate(
        [candidate.reshape(chips, rows, width), jnp.broadcast_to(tail, (chips, rows, 64))], axis=2
    )
    arrived = across_chips(message)
    piece = pick(arrived, owner // 2)[:, :width]
    infos = arrived[:, 0, width : width + packed.shape[0]].astype(f32)
    infos = infos.reshape(chips, 4, 2 * completions)
    all_rewards = (infos[:, 0] + infos[:, 1] + infos[:, 2]).reshape(-1)
    all_groups = infos[:, 3].reshape(-1)
    labels = jnp.arange(n_dp * completions // GROUPS_PER_COMPLETION, dtype=f32)
    member = (all_groups[:, None] == labels[None, :]).astype(f32)
    group_mean = jnp.sum(member * all_rewards[:, None], axis=0) / jnp.maximum(
        jnp.sum(member, axis=0), 1.0
    )
    mine = (info[1][:, None] == labels[None, :]).astype(f32)
    advantage = info[0] - jnp.sum(mine * group_mean[None, :], axis=1)
    tok_adv = jnp.repeat(advantage, tokens // completions)

    factors = across_chips(jnp.broadcast_to(piece, (chips, rows, width)))
    factors = factors.reshape(chips * rows, width)
    factor_a = factors[:R]
    factor_b = factors[R:]

    def project(factor, x):
        return jnp.einsum("kd,td->kt", factor, x, preferred_element_type=f32)

    low = jnp.concatenate([project(factor_a, own_act), project(factor_a, far_act)], axis=1)
    back = jnp.concatenate([project(factor_b, own_cot), project(factor_b, far_cot)], axis=1)
    parts = jnp.concatenate([low, back]).astype(bf16)
    parts = across_tensor(jnp.broadcast_to(parts, (n_tensor,) + parts.shape))
    sums = jnp.sum(parts.astype(f32), axis=0)
    low_rank = (sums[:R] * scale_a).astype(bf16)
    back_rank = (sums[R:] * (tok_adv * scale_b)[None, :]).astype(bf16)
    low_rank = (low_rank.astype(f32) * tok_adv[None, :]).astype(bf16)

    def grad(rank, own, far):
        return jnp.einsum(
            "kt,td->kd", rank[:, :tokens], own, preferred_element_type=f32
        ) + jnp.einsum("kt,td->kd", rank[:, tokens:], far, preferred_element_type=f32)

    grads = jnp.concatenate(
        [grad(back_rank, own_act, far_act), grad(low_rank, own_cot, far_cot)]
    ).astype(bf16)
    arrived = across_chips(grads.reshape(chips, rows, width))
    step = jnp.where(chip * rows < R, rate_a * scale_a, rate_b * scale_b)
    fresh = (piece.astype(f32) - step * jnp.sum(arrived.astype(f32), axis=0)).astype(bf16)
    fresh = across_chips(jnp.broadcast_to(fresh, (chips, rows, width)))
    fresh = fresh.reshape(chips * rows, width)
    far_fresh = core_swap(fresh)
    first = jnp.where(core == 0, fresh, far_fresh)
    second = jnp.where(core == 0, far_fresh, fresh)
    new_a = jnp.stack([first[:R], second[:R]])
    new_b = jnp.stack([first[R:], second[R:]])

    dec = jnp.stack([own_dec, far_dec])
    rank_part = jnp.einsum(
        "csrd,kd->csrk", dec, fresh[:R], preferred_element_type=f32
    ).astype(bf16)
    rank_part = across_tensor(jnp.broadcast_to(rank_part, (n_tensor,) + rank_part.shape))
    rank_low = (jnp.sum(rank_part.astype(f32), axis=0) * scale_a).astype(bf16)
    far_rank = core_swap(rank_low[1])
    rank_first = jnp.where(core == 0, rank_low[0], far_rank)
    rank_second = jnp.where(core == 0, far_rank, rank_low[0])
    rank_all = jnp.stack([rank_first, rank_second], axis=1)
    change = jnp.einsum("slrk,lkd->slrd", rank_all, new_b, preferred_element_type=f32)
    query = (frozen_query_part.astype(f32) + scale_b * change).astype(bf16)

    steps, layers, rows_dev, _ = query.shape
    kv_local = kv_cache.shape[2]
    slots = kv_cache.shape[3]
    head_dim = kv_cache.shape[4] // 2
    per_kv = width // (kv_local * head_dim)
    query_heads = query.reshape(steps, layers, rows_dev, kv_local, per_kv, head_dim)
    cache_keys = kv_cache[..., :head_dim]
    cache_values = kv_cache[..., head_dim:]
    fresh_keys = new_kv[..., :head_dim]
    fresh_values = new_kv[..., head_dim:]
    old_scores = jnp.einsum(
        "slrkgd,lrkpd->slrkgp", query_heads, cache_keys, preferred_element_type=f32
    ) / math.sqrt(head_dim)
    slot_valid = jnp.arange(slots, dtype=jnp.int32)[None, :] < lengths[:, None]
    old_scores = jnp.where(slot_valid[None, None, :, None, None, :], old_scores, -jnp.inf)
    new_scores = jnp.einsum(
        "slrkgd,tlrkd->slrkgt", query_heads, fresh_keys, preferred_element_type=f32
    ) / math.sqrt(head_dim)
    causal = jnp.arange(steps)[None, :] <= jnp.arange(steps)[:, None]
    new_scores = jnp.where(causal[:, None, None, None, None, :], new_scores, -jnp.inf)
    peak_score = jnp.maximum(jnp.max(old_scores, axis=-1), jnp.max(new_scores, axis=-1))
    old_exp = jnp.exp(old_scores - peak_score[..., None])
    new_exp = jnp.exp(new_scores - peak_score[..., None])
    denominator = jnp.sum(old_exp, axis=-1) + jnp.sum(new_exp, axis=-1)
    old_weight = (old_exp / denominator[..., None]).astype(bf16)
    new_weight = (new_exp / denominator[..., None]).astype(bf16)
    combined = jnp.einsum(
        "slrkgp,lrkpd->slrkgd", old_weight, cache_values, preferred_element_type=f32
    )
    combined = combined + jnp.einsum(
        "slrkgt,tlrkd->slrkgd", new_weight, fresh_values, preferred_element_type=f32
    )
    attended = combined.astype(bf16).reshape(steps, layers, rows_dev, width)
    return (new_a, new_b, attended)


def solution(mesh):
    return jax.shard_map(
        shards,
        mesh=mesh,
        in_specs=(
            P(None, "dp", "tensor"),
            P(None, "dp", "tensor"),
            P("dp"),
            P("dp"),
            P(),
            P("dp", None, None, "tensor"),
            P("dp", None, None, "tensor"),
            P(None, None, "dp", "tensor"),
            P(None, None, "dp", "tensor"),
            P(None, "dp", "tensor", None, None),
            P(None, None, "dp", "tensor", None),
            P("dp"),
        ),
        out_specs=(P(None, None, "tensor"), P(None, None, "tensor"), P(None, None, "dp", "tensor")),
        check_vma=False,
    )
```

time: 754 us -> 179 us (0.24)
  waiting for transfers between devices: 615 us -> 63.9 us
  blocking collectives: 69.1 us -> 0 us
  starting transfers between devices: 0.34 us -> 51.7 us
  between operations: 15.3 us -> 3.76 us
  local copies, waits for them, and re-layouts: 12 us -> 22.7 us
    psum x4 -> x0, waiting for transfers between devices: 615 us -> none  [the longest x1 273 us: update_factors(): grad_a, grad_b = lax.psum((grad_a_part, grad_b_part), 'dp')]
    psum x1 -> x0, blocking collectives: 69.1 us -> none  [advantage_of(): lax.psum((jnp.sum(member * rewards[:, None], axis=0), jnp.sum(member, axi...]
    all_to_all x0 -> x6, waiting for transfers between devices: none -> 61.4 us  [the longest x4 44.1 us: across_chips(): return lax.all_to_all(x, 'dp', 0, 0, axis_index_groups=same_core)]
    all_to_all x0 -> x6, starting transfers between devices: none -> 37.7 us  [the longest x4 30.1 us: across_chips(): return lax.all_to_all(x, 'dp', 0, 0, axis_index_groups=same_core)]
    ppermute x0 -> x7, starting transfers between devices: none -> 14.1 us  [core_swap(): return lax.ppermute(x, 'dp', swap)]
  transfers between devices with their start and end apart: 4 -> 13, of which waited for: 4 -> 8; matrix products, arithmetic and copies ran while one was open for 0% -> 7% of each run, Pallas kernels for 0% -> 0%
where the time goes in v1:
time: 179 us; the launch traced here: 178 us
  waiting for transfers between devices  63.9 us (36%)
  starting transfers between devices  51.7 us (29%)
  matrix products  25.9 us (14%)
  local copies, waits for them, and re-layouts  22.7 us (13%)
  other arithmetic  10.1 us (6%)
  between operations  3.76 us (2%)
    all_to_all x4, waiting for transfers between devices, across_chips(): return lax.all_to_all(x, 'dp', 0, 0, axis_index_groups=same_core)  44.1 us
    all_to_all x4, starting transfers between devices, across_chips(): return lax.all_to_all(x, 'dp', 0, 0, axis_index_groups=same_core)  30.1 us
    all_to_all x2, waiting for transfers between devices, across_tensor(): return lax.all_to_all(x, 'tensor', 0, 0)  17.3 us
    ppermute x7, starting transfers between devices, core_swap(): return lax.ppermute(x, 'dp', swap)  14.1 us
    all_to_all x2, starting transfers between devices, across_tensor(): return lax.all_to_all(x, 'tensor', 0, 0)  7.54 us
    dot_general x1, matrix products, shards(): jnp.einsum('slrkgp,lrkpd->slrkgd', old_weight, cache_values, preferred_el...  6.31 us
    reshape x2, local copies, waits for them, and re-layouts, shards(): attended = combined.astype(bf16).reshape(steps, layers, rows_dev, width)  4.74 us
    squeeze x4, local copies, waits for them, and re-layouts, pick(): return lax.dynamic_index_in_dim(array, index, axis, keepdims=False)  4.7 us
  transfers between devices with their start and end apart: 13, of which 8 were waited for; matrix products, arithmetic and copies ran while one was open for 7% of the time, Pallas kernels for 0%

profile of v1, /device:TPU:1, one launch (start us, length us, event | category | flops | bytes accessed | tf_op | source)
XLA Modules:
  0.0 178.0 jit_solution(9516154832026317537)
XLA Ops:
  0.7 1.5 dynamic-slice_bitcast_fusion.6
  2.2 3.3 %collective-permute-start = (bf16[128,1856]{1,0:T(8,128)(2,1)S(1)}, bf16[128,1856]{1,0:T(8,128)(2,1)S(1)}, u32[]{:S(2)}, u32[]{:S(2)}) collective-permute-start(bf16[128,1856]{1,0:T(8,128)(2,1)S(1)} %pad_maximum_fusion), channel_id=1, source_target_pairs={{0,8},{8,0},{16,24},{24,16},{32,40},{40,32},{48,56},{56,48},{64,72... | collective-permute-start | bytes 1425416 | tf_op jit(solution)/shard_map/ppermute | solution.py:60
  6.9 1.2 dynamic_slice.41
  10.1 0.7 pad_maximum_fusion.5
  11.1 0.9 pad_maximum_fusion.1
  11.9 9.2 %all-to-all-start = ((bf16[16,8,1920]{2,1,0:T(8,128)(2,1)}), bf16[16,8,1920]{2,1,0:T(8,128)(2,1)S(1)}, u32[]{:S(2)}, u32[]{:S(2)}) async-start(bf16[16,8,1920]{2,1,0:T(8,128)(2,1)} %pad_maximum_fusion.1), calls=%async_computation | async-start | bytes 983040 | tf_op jit(solution)/shard_map/all_to_all | solution.py:63
  21.8 13.5 %all-to-all-done = bf16[16,8,1920]{2,1,0:T(8,128)(2,1)S(1)} async-done(((bf16[16,8,1920]{2,1,0:T(8,128)(2,1)}), bf16[16,8,1920]{2,1,0:T(8,128)(2,1)S(1)}, u32[]{:S(2)}, u32[]{:S(2)}) %all-to-all-start) | async-done | bytes 491552 | tf_op jit(solution)/shard_map/all_to_all | solution.py:63
  35.3 0.9 broadcast_in_dim.58
  36.2 6.5 %all-to-all-start.1 = ((bf16[16,8,1856]{2,1,0:T(8,128)(2,1)}), bf16[16,8,1856]{2,1,0:T(8,128)(2,1)S(1)}, u32[]{:S(2)}, u32[]{:S(2)}) async-start(bf16[16,8,1856]{2,1,0:T(8,128)(2,1)} %broadcast_in_dim.58), calls=%async_computation.1 | async-start | bytes 983040 | tf_op jit(solution)/shard_map/all_to_all | solution.py:63
  42.7 2.2 %dynamic-slice_bitcast_fusion = bf16[256,1856]{0,1:T(8,128)(2,1)} fusion(bf16[2,256,1856]{1,2,0:T(8,128)(2,1)} %param.15, s32[]{:T(128)S(6)} %select_n.91), kind=kLoop, calls=%fused_computation.50 | loop fusion | bytes 1900548 | tf_op jit(solution)/shard_map/jit(dynamic_index_in_dim)/squeeze | solution.py:20
  44.9 1.3 collective-permute-start.3
  46.2 1.0 dynamic-slice_bitcast_fusion.1
  47.2 0.8 slice.143
  48.6 7.7 %all-to-all-done.1 = bf16[16,8,1856]{2,1,0:T(8,128)(2,1)S(1)} async-done(((bf16[16,8,1856]{2,1,0:T(8,128)(2,1)}), bf16[16,8,1856]{2,1,0:T(8,128)(2,1)S(1)}, u32[]{:S(2)}, u32[]{:S(2)}) %all-to-all-start.1) | async-done | bytes 475168 | tf_op jit(solution)/shard_map/all_to_all | solution.py:63
  56.3 1.5 convolution_convert_fusion.2
  58.4 1.5 convolution_convert_fusion.3
  60.0 1.1 broadcast_in_dim.59
  61.0 4.1 %all-to-all-start.2 = ((bf16[8,128,512]{2,1,0:T(8,128)(2,1)}), bf16[8,128,512]{2,1,0:T(8,128)(2,1)S(1)}, u32[]{:S(2)}, u32[]{:S(2)}) async-start(bf16[8,128,512]{2,1,0:T(8,128)(2,1)} %broadcast_in_dim.59), calls=%async_computation.2 | async-start | bytes 2097152 | tf_op jit(solution)/shard_map/all_to_all | solution.py:66
  65.5 14.6 %all-to-all-done.2 = bf16[8,128,512]{2,1,0:T(8,128)(2,1)S(1)} async-done(((bf16[8,128,512]{2,1,0:T(8,128)(2,1)}), bf16[8,128,512]{2,1,0:T(8,128)(2,1)S(1)}, u32[]{:S(2)}, u32[]{:S(2)}) %all-to-all-start.2) | async-done | bytes 1048608 | tf_op jit(solution)/shard_map/all_to_all | solution.py:66
  80.7 0.9 copy-done.1
  82.0 1.6 fusion.12
  84.1 0.8 maximum_bitcast_fusion
  84.9 7.9 %all-to-all-start.3 = ((bf16[16,8,1856]{2,1,0:T(8,128)(2,1)}), bf16[16,8,1856]{2,1,0:T(8,128)(2,1)S(1)}, u32[]{:S(2)}, u32[]{:S(2)}) async-start(bf16[16,8,1856]{2,1,0:T(8,128)(2,1)} %maximum_bitcast_fusion), calls=%async_computation.3 | async-start | bytes 983040 | tf_op jit(solution)/shard_map/all_to_all | solution.py:63
  92.8 13.7 %all-to-all-done.3 = bf16[16,8,1856]{2,1,0:T(8,128)(2,1)S(1)} async-done(((bf16[16,8,1856]{2,1,0:T(8,128)(2,1)}), bf16[16,8,1856]{2,1,0:T(8,128)(2,1)S(1)}, u32[]{:S(2)}, u32[]{:S(2)}) %all-to-all-start.3) | async-done | bytes 475168 | tf_op jit(solution)/shard_map/all_to_all | solution.py:63
  106.6 0.8 broadcast_in_dim.61
  107.5 6.6 %all-to-all-start.4 = ((bf16[16,8,1856]{2,1,0:T(8,128)(2,1)}), bf16[16,8,1856]{2,1,0:T(8,128)(2,1)S(1)}, u32[]{:S(2)}, u32[]{:S(2)}) async-start(bf16[16,8,1856]{2,1,0:T(8,128)(2,1)} %broadcast_in_dim.61), calls=%async_computation.4 | async-start | bytes 983040 | tf_op jit(solution)/shard_map/all_to_all | solution.py:63
  114.0 1.3 dynamic-slice_bitcast_fusion.3
  115.3 1.8 %collective-permute-start.5 = (bf16[2,64,1856]{2,1,0:T(8,128)(2,1)S(1)}, bf16[2,64,1856]{2,1,0:T(8,128)(2,1)}, u32[]{:S(2)}, u32[]{:S(2)}) collective-permute-start(bf16[2,64,1856]{2,1,0:T(8,128)(2,1)S(1)} %get-tuple-element.21), channel_id=1, source_target_pairs={{0,8},{8,0},{16,24},{24,16},{32,40},{40,32},{48,56},{56,48},{64,72... | collective-permute-start | bytes 1425416 | tf_op jit(solution)/shard_map/ppermute | solution.py:60
  117.1 1.6 collective-permute-done.5
  118.8 9.1 %all-to-all-done.4 = bf16[16,8,1856]{2,1,0:T(8,128)(2,1)S(1)} async-done(((bf16[16,8,1856]{2,1,0:T(8,128)(2,1)}), bf16[16,8,1856]{2,1,0:T(8,128)(2,1)S(1)}, u32[]{:S(2)}, u32[]{:S(2)}) %all-to-all-start.4) | async-done | bytes 475168 | tf_op jit(solution)/shard_map/all_to_all | solution.py:63
  127.9 1.4 convolution_convert_fusion
  129.5 1.1 reshape.247
  130.6 3.4 %all-to-all-start.5 = ((bf16[8,2,8192]{2,1,0:T(2,128)(2,1)}), bf16[8,2,8192]{2,1,0:T(2,128)(2,1)S(1)}, u32[]{:S(2)}, u32[]{:S(2)}) async-start(bf16[8,2,8192]{2,1,0:T(2,128)(2,1)} %reshape.247), calls=%async_computation.5 | async-start | bytes 524288 | tf_op jit(solution)/shard_map/all_to_all | solution.py:66
  134.2 3.1 %collective-permute-start.4 = (bf16[128,1856]{1,0:T(8,128)(2,1)S(1)}, bf16[128,1856]{1,0:T(8,128)(2,1)}, u32[]{:S(2)}, u32[]{:S(2)}) collective-permute-start(bf16[128,1856]{1,0:T(8,128)(2,1)S(1)} %bitcast.185), channel_id=1, source_target_pairs={{0,8},{8,0},{16,24},{24,16},{32,40},{40,32},{48,56},{56,48},{64,72... | collective-permute-start | bytes 1425416 | tf_op jit(solution)/shard_map/ppermute | solution.py:60
  137.3 2.7 %all-to-all-done.5 = bf16[8,2,8192]{2,1,0:T(2,128)(2,1)S(1)} async-done(((bf16[8,2,8192]{2,1,0:T(2,128)(2,1)}), bf16[8,2,8192]{2,1,0:T(2,128)(2,1)S(1)}, u32[]{:S(2)}, u32[]{:S(2)}) %all-to-all-start.5) | async-done | bytes 262176 | tf_op jit(solution)/shard_map/all_to_all | solution.py:66
  140.6 4.5 %collective-permute-start.6 = (bf16[2,64,64]{2,1,0:T(8,128)(2,1)S(1)}, bf16[2,64,64]{2,1,0:T(8,128)(2,1)S(1)}, u32[]{:S(2)}, u32[]{:S(2)}) collective-permute-start(bf16[2,64,64]{2,1,0:T(8,128)(2,1)S(1)} %slice_bitcast_fusion.12), channel_id=1, source_target_pairs={{0,8},{8,0},{16,24},{24,16},{32,40},{40,32},{48,56},{56,48},{64,72... | collective-permute-start | bytes 49160 | tf_op jit(solution)/shard_map/ppermute | solution.py:60
  145.1 0.9 collective-permute-done.6
  145.9 1.1 broadcast_select_fusion.1
  147.2 0.8 copy-done.6
  148.4 3.2 %reshape.246 = bf16[2,2,64,29,64]{4,3,2,0,1:T(8,128)(2,1)} reshape(bf16[2,2,64,1856]{3,2,0,1:T(8,128)(2,1)S(1)} %fusion.11) | data formatting | bytes 1900544 | tf_op jit(solution)/shard_map/reshape.52
  151.6 4.6 %fusion.82 = (f32[2,2,64,29]{3,0,2,1:T(2,128)S(1)}, f32[2,2,64,1,29,2]{4,5,0,2,1,3:T(2,128)S(1)}) fusion(bf16[2,2,64,1,64]{4,2,3,1,0:T(8,128)(2,1)S(1)} %get-tuple-element.37, bf16[2,2,64,29,64]{4,3,2,0,1:T(8,128)(2,1)} %reshape.246, pred[2,2]{1,0:T(4,128)(4,1)S(1)} %iota_compare_fusion.5), kind=kOutput, calls=%fused_computation.154 | convolution fusion | flops 1937664 | bytes 1072132 | tf_op jit(solution)/shard_map/slrkgd,tlrkd->slrkgt/dot_general | solution.py:169
  156.2 4.3 %fusion.2 = (f32[2,2,64,29]{3,0,2,1:T(2,128)S(1)}, f32[2,64,2,29,96]{4,3,2,1,0:T(8,128)S(1)}) fusion(pred[64,96]{1,0:T(8,128)(4,1)S(1)} %iota_compare_fusion, bf16[2,64,1,96,128]{4,3,2,1,0:T(8,128)(2,1)} %param.23, bf16[2,2,64,29,64]{4,3,2,0,1:T(8,128)(2,1)S(1)} %copy-done.4), kind=kOutput, calls=%fused_computation.6 | convolution fusion | flops 93356800 | bytes 6982656 | tf_op jit(solution)/shard_map/slrkgd,lrkpd->slrkgp/dot_general | solution.py:164
  161.2 2.6 %fusion.1 = f32[2,2,64,29]{3,0,2,1:T(2,128)S(1)} fusion(f32[2,64,2,29,96]{4,3,2,1,0:T(8,128)S(1)} %get-tuple-element.45, f32[2,2,64,29]{3,0,2,1:T(2,128)S(1)} %max.17, pred[64,96]{1,0:T(8,128)(4,1)S(1)} %iota_compare_fusion), kind=kLoop, calls=%fused_computation.5 | loop fusion | flops 2843392 | bytes 2916352 | tf_op jit(solution)/shard_map/reduce_sum | solution.py:177
  163.8 6.3 %fusion.3 = f32[2,64,2,29,64]{4,3,2,1,0:T(8,128)S(1)} fusion(bf16[2,64,1,96,128]{4,3,2,1,0:T(8,128)(2,1)S(1)} %copy-done.9, f32[2,64,2,29,96]{4,3,2,1,0:T(8,128)S(1)} %get-tuple-element.45, f32[2,2,64,29]{3,0,2,1:T(2,128)S(1)} %add.90, f32[2,2,64,29]{3,0,2,1:T(2,128)S(1)} %max.17, pred[64,96]{1,0:T(8,128)(4,1)S(1)} %iota_compare_fusion), kind=kOutput, calls=%fused_computation.7 | convolution fusion | flops 94789632 | bytes 7962624 | tf_op jit(solution)/shard_map/slrkgp,lrkpd->slrkgd/dot_general | solution.py:180
  170.1 2.3 %fusion.22 = bf16[2,2,64,1,29,64]{5,4,0,2,1,3:T(8,128)(2,1)} fusion(f32[2,64,2,29,64]{4,3,2,1,0:T(8,128)S(1)} %fusion.3, f32[2,2,64,1,29,2]{4,5,0,2,1,3:T(2,128)S(1)} %get-tuple-element.47, f32[2,2,64,29]{3,0,2,1:T(2,128)S(1)} %add.90, f32[2,2,64,29]{3,0,2,1:T(2,128)S(1)} %max.17, bf16[2,2,64,1,64]{4,2,3,1,0:T(8,128)(2,1)S(1)} %get-tuple-element.36), kind=kOutput, calls=%fused_computation.30 | convolution fusion | flops 2895360 | bytes 3002368 | tf_op jit(solution)/shard_map/slrkgt,tlrkd->slrkgd/dot_general | solution.py:183
  172.4 3.7 %reshape.245 = bf16[2,2,64,1856]{3,0,2,1:T(2,128)(2,1)S(1)} reshape(bf16[2,2,64,1,29,64]{5,4,0,2,1,3:T(8,128)(2,1)} %fusion.22) | data formatting | bytes 1900544 | tf_op jit(solution)/shard_map/reshape | solution.py:186
  176.1 1.0 copy.90
  177.2 0.8 pad_maximum_fusion.2
  (75 shorter events, 6.7 us)
Async XLA Ops:
  0.6 45.6 %copy-start = (bf16[2,256,1856]{1,2,0:T(8,128)(2,1)S(1)}, bf16[2,256,1856]{1,2,0:T(8,128)(2,1)}, u32[]{:S(2)}) copy-start(bf16[2,256,1856]{1,2,0:T(8,128)(2,1)} %param.14) | copy-start | bytes 5701636
  2.2 8.7 %collective-permute-start = (bf16[128,1856]{1,0:T(8,128)(2,1)S(1)}, bf16[128,1856]{1,0:T(8,128)(2,1)S(1)}, u32[]{:S(2)}, u32[]{:S(2)}) collective-permute-start(bf16[128,1856]{1,0:T(8,128)(2,1)S(1)} %pad_maximum_fusion), channel_id=1, source_target_pairs={{0,8},{8,0},{16,24},{24,16},{32,40},{40,32},{48,56},{56,48},{64,72... | collective-permute-start | bytes 1425416 | tf_op jit(solution)/shard_map/ppermute | solution.py:60
  6.9 3.2 %collective-permute-start.1 = (f32[2,2]{1,0:T(2,128)S(1)}, f32[2,2]{1,0:T(2,128)S(1)}, u32[]{:S(2)}, u32[]{:S(2)}) collective-permute-start(f32[2,2]{1,0:T(2,128)S(1)} %pad_maximum_fusion.4), channel_id=1, source_target_pairs={{0,8},{8,0},{16,24},{24,16},{32,40},{40,32},{48,56},{56,48},{64,72... | collective-permute-start | bytes 56 | tf_op jit(solution)/shard_map/ppermute | solution.py:60
  11.9 23.4 %all-to-all-start = ((bf16[16,8,1920]{2,1,0:T(8,128)(2,1)}), bf16[16,8,1920]{2,1,0:T(8,128)(2,1)S(1)}, u32[]{:S(2)}, u32[]{:S(2)}) async-start(bf16[16,8,1920]{2,1,0:T(8,128)(2,1)} %pad_maximum_fusion.1), calls=%async_computation | async-start | bytes 983040 | tf_op jit(solution)/shard_map/all_to_all | solution.py:63
  35.3 7.4 %copy-start.5 = (bf16[16,8,1920]{2,1,0:T(8,128)(2,1)}, bf16[16,8,1920]{2,1,0:T(8,128)(2,1)S(1)}, u32[]{:S(2)}) copy-start(bf16[16,8,1920]{2,1,0:T(8,128)(2,1)S(1)} %all-to-all-done) | copy-start | bytes 1474564
  36.2 20.1 %all-to-all-start.1 = ((bf16[16,8,1856]{2,1,0:T(8,128)(2,1)}), bf16[16,8,1856]{2,1,0:T(8,128)(2,1)S(1)}, u32[]{:S(2)}, u32[]{:S(2)}) async-start(bf16[16,8,1856]{2,1,0:T(8,128)(2,1)} %broadcast_in_dim.58), calls=%async_computation.1 | async-start | bytes 983040 | tf_op jit(solution)/shard_map/all_to_all | solution.py:63
  44.9 13.2 %collective-permute-start.3 = (bf16[256,1856]{0,1:T(8,128)(2,1)}, bf16[256,1856]{0,1:T(8,128)(2,1)S(1)}, u32[]{:S(2)}, u32[]{:S(2)}) collective-permute-start(bf16[256,1856]{0,1:T(8,128)(2,1)} %dynamic-slice_bitcast_fusion), channel_id=1, source_target_pairs={{0,8},{8,0},{16,24},{24,16},{32,40},{40,32},{48,56},{56,48},{64,72... | collective-permute-start | bytes 2850824 | tf_op jit(solution)/shard_map/ppermute | solution.py:60
  47.2 11.2 %collective-permute-start.2 = (bf16[256,1856]{0,1:T(8,128)(2,1)}, bf16[256,1856]{0,1:T(8,128)(2,1)}, u32[]{:S(2)}, u32[]{:S(2)}) collective-permute-start(bf16[256,1856]{0,1:T(8,128)(2,1)} %dynamic-slice_bitcast_fusion.1), channel_id=1, source_target_pairs={{0,8},{8,0},{16,24},{24,16},{32,40},{40,32},{48,56},{56,48},{64,72... | collective-permute-start | bytes 2850824 | tf_op jit(solution)/shard_map/ppermute | solution.py:60
  58.1 2.9 %copy-start.2 = (bf16[256,1856]{0,1:T(8,128)(2,1)}, bf16[256,1856]{0,1:T(8,128)(2,1)S(1)}, u32[]{:S(2)}) copy-start(bf16[256,1856]{0,1:T(8,128)(2,1)S(1)} %collective-permute-done.3) | copy-start | bytes 2850820
  61.0 19.1 %all-to-all-start.2 = ((bf16[8,128,512]{2,1,0:T(8,128)(2,1)}), bf16[8,128,512]{2,1,0:T(8,128)(2,1)S(1)}, u32[]{:S(2)}, u32[]{:S(2)}) async-start(bf16[8,128,512]{2,1,0:T(8,128)(2,1)} %broadcast_in_dim.59), calls=%async_computation.2 | async-start | bytes 2097152 | tf_op jit(solution)/shard_map/all_to_all | solution.py:66
  80.1 1.5 copy-start.1
  80.1 3.6 %copy-start.3 = (bf16[256,1856]{0,1:T(8,128)(2,1)S(1)}, bf16[256,1856]{0,1:T(8,128)(2,1)}, u32[]{:S(2)}) copy-start(bf16[256,1856]{0,1:T(8,128)(2,1)} %copy-done.2) | copy-start | bytes 2850820
  84.9 21.6 %all-to-all-start.3 = ((bf16[16,8,1856]{2,1,0:T(8,128)(2,1)}), bf16[16,8,1856]{2,1,0:T(8,128)(2,1)S(1)}, u32[]{:S(2)}, u32[]{:S(2)}) async-start(bf16[16,8,1856]{2,1,0:T(8,128)(2,1)} %maximum_bitcast_fusion), calls=%async_computation.3 | async-start | bytes 983040 | tf_op jit(solution)/shard_map/all_to_all | solution.py:63
  107.5 20.5 %all-to-all-start.4 = ((bf16[16,8,1856]{2,1,0:T(8,128)(2,1)}), bf16[16,8,1856]{2,1,0:T(8,128)(2,1)S(1)}, u32[]{:S(2)}, u32[]{:S(2)}) async-start(bf16[16,8,1856]{2,1,0:T(8,128)(2,1)} %broadcast_in_dim.61), calls=%async_computation.4 | async-start | bytes 983040 | tf_op jit(solution)/shard_map/all_to_all | solution.py:63
  114.0 20.0 %copy-start.8 = (s32[64]{0:T(128)S(1)}, s32[64]{0:T(128)}, u32[]{:S(2)}) copy-start(s32[64]{0:T(128)} %param.25) | copy-start | bytes 772
  114.0 20.1 %copy-start.7 = (bf16[2,2,64,1,128]{4,2,3,1,0:T(8,128)(2,1)S(1)}, bf16[2,2,64,1,128]{4,2,3,1,0:T(8,128)(2,1)}, u32[]{:S(2)}) copy-start(bf16[2,2,64,1,128]{4,2,3,1,0:T(8,128)(2,1)} %param.24) | copy-start | bytes 196612
  115.3 3.4 %collective-permute-start.5 = (bf16[2,64,1856]{2,1,0:T(8,128)(2,1)S(1)}, bf16[2,64,1856]{2,1,0:T(8,128)(2,1)}, u32[]{:S(2)}, u32[]{:S(2)}) collective-permute-start(bf16[2,64,1856]{2,1,0:T(8,128)(2,1)S(1)} %get-tuple-element.21), channel_id=1, source_target_pairs={{0,8},{8,0},{16,24},{24,16},{32,40},{40,32},{48,56},{56,48},{64,72... | collective-permute-start | bytes 1425416 | tf_op jit(solution)/shard_map/ppermute | solution.py:60
  130.6 9.5 %all-to-all-start.5 = ((bf16[8,2,8192]{2,1,0:T(2,128)(2,1)}), bf16[8,2,8192]{2,1,0:T(2,128)(2,1)S(1)}, u32[]{:S(2)}, u32[]{:S(2)}) async-start(bf16[8,2,8192]{2,1,0:T(2,128)(2,1)} %reshape.247), calls=%async_computation.5 | async-start | bytes 524288 | tf_op jit(solution)/shard_map/all_to_all | solution.py:66
  134.2 11.7 %collective-permute-start.4 = (bf16[128,1856]{1,0:T(8,128)(2,1)S(1)}, bf16[128,1856]{1,0:T(8,128)(2,1)}, u32[]{:S(2)}, u32[]{:S(2)}) collective-permute-start(bf16[128,1856]{1,0:T(8,128)(2,1)S(1)} %bitcast.185), channel_id=1, source_target_pairs={{0,8},{8,0},{16,24},{24,16},{32,40},{40,32},{48,56},{56,48},{64,72... | collective-permute-start | bytes 1425416 | tf_op jit(solution)/shard_map/ppermute | solution.py:60
  140.6 5.3 %collective-permute-start.6 = (bf16[2,64,64]{2,1,0:T(8,128)(2,1)S(1)}, bf16[2,64,64]{2,1,0:T(8,128)(2,1)S(1)}, u32[]{:S(2)}, u32[]{:S(2)}) collective-permute-start(bf16[2,64,64]{2,1,0:T(8,128)(2,1)S(1)} %slice_bitcast_fusion.12), channel_id=1, source_target_pairs={{0,8},{8,0},{16,24},{24,16},{32,40},{40,32},{48,56},{56,48},{64,72... | collective-permute-start | bytes 49160 | tf_op jit(solution)/shard_map/ppermute | solution.py:60
  145.1 2.9 %copy-start.10 = (bf16[2,2,64,1856]{3,2,1,0:T(8,128)(2,1)S(1)}, bf16[2,2,64,1856]{3,2,1,0:T(8,128)(2,1)}, u32[]{:S(2)}) copy-start(bf16[2,2,64,1856]{3,2,1,0:T(8,128)(2,1)} %param.21) | copy-start | bytes 2850820
  147.2 0.8 copy-start.6
  151.6 4.7 %copy-start.4 = (bf16[2,2,64,29,64]{4,3,2,0,1:T(8,128)(2,1)S(1)}, bf16[2,2,64,29,64]{4,3,2,0,1:T(8,128)(2,1)}, u32[]{:S(2)}) copy-start(bf16[2,2,64,29,64]{4,3,2,0,1:T(8,128)(2,1)} %reshape.246) | copy-start | bytes 2850820
  160.6 3.2 %copy-start.9 = (bf16[2,64,1,96,128]{4,3,2,1,0:T(8,128)(2,1)S(1)}, bf16[2,64,1,96,128]{4,3,2,1,0:T(8,128)(2,1)}, u32[]{:S(2)}) copy-start(bf16[2,64,1,96,128]{4,3,2,1,0:T(8,128)(2,1)} %param.23) | copy-start | bytes 9437188

commit v2 on v1

v2 whole, which is shorter than its diff:
```python
import jax
import jax.numpy as jnp
from jax import lax
from jax.experimental import pallas as pl
from jax.experimental.pallas import tpu as pltpu
from jax.sharding import PartitionSpec as P

D = 14848
R = 64
GROUPS_PER_COMPLETION = 4
VMEM_BYTES = 48 * 1024 * 1024

rate_a = 0.5
rate_b = 0.05

f32 = jnp.float32
bf16 = jnp.bfloat16


def pick(array, index, axis=0):
    return lax.dynamic_index_in_dim(array, index, axis, keepdims=False)


def split3(x):
    hi = lax.reduce_precision(x, 8, 7)
    mid = lax.reduce_precision(x - hi, 8, 7)
    lo = lax.reduce_precision(x - hi - mid, 8, 7)
    return hi, mid, lo


def nt_dot(a, b):
    return lax.dot_general(a, b, (((1,), (1,)), ((), ())), preferred_element_type=f32)


def project_kernel(core, factors, act, far_act, cot, far_cot, out):
    r = factors.shape[0] // 2
    tokens = act.shape[2]
    for half, sources in enumerate(((act, far_act), (cot, far_cot))):
        factor = factors[half * r : (half + 1) * r]
        for place, source in enumerate(sources):
            part = jnp.dot(factor, source[0], preferred_element_type=f32).astype(bf16)
            for peer in range(out.shape[0]):
                out[
                    peer, half * r : (half + 1) * r, place * tokens : (place + 1) * tokens
                ] = part


def grad_kernel(core, parts, adv, act, far_act, cot, far_cot, out):
    r = parts.shape[1] // 2
    tokens = act.shape[2]
    total = jnp.sum(parts[...].astype(f32), axis=0)
    low = (total[:r] * D**-0.5).astype(bf16).astype(f32)
    low = (low * adv[...]).astype(bf16)
    back = (total[r:] * (adv[...] * R**-0.5)).astype(bf16)
    for half, (rank, sources) in enumerate(((back, (act, far_act)), (low, (cot, far_cot)))):
        grad = nt_dot(rank[:, :tokens], sources[0][0]) + nt_dot(rank[:, tokens:], sources[1][0])
        out[half * r : (half + 1) * r] = grad.astype(bf16)


def decode_kernel(core, fresh, dec, far_dec, out):
    steps, _, rows, width = dec.shape
    for place, source in enumerate((dec, far_dec)):
        part = nt_dot(fresh[...], source[:, 0].reshape(steps * rows, width)).astype(bf16)
        for peer in range(out.shape[0]):
            out[peer, :, place * steps * rows : (place + 1) * steps * rows] = part


def attend_kernel(rank_ref, up_ref, frozen_ref, kv_ref, new_ref, valid_ref, out_ref, query, result):
    steps, _, rows, width = frozen_ref.shape
    half = query.shape[2] // 2
    heads = width // half
    pad = (query.shape[1] - 8) // steps
    rank = rank_ref[:, 0].reshape(steps * rows, -1)
    change = jnp.dot(rank, up_ref[0], preferred_element_type=f32)
    q = frozen_ref[:, 0].reshape(steps * rows, width).astype(f32) + change * R**-0.5
    q = q.astype(bf16).astype(f32) * (half**-0.5)
    lane = lax.broadcasted_iota(jnp.int32, (steps * rows, 2 * half), 1)
    for pair in range(heads // 2 + heads % 2):
        x = q[:, 2 * half * pair : 2 * half * (pair + 1)]
        if x.shape[1] < 2 * half:
            x = jnp.concatenate([x, jnp.zeros_like(x)], axis=1)
        for odd in range(2):
            head = 2 * pair + odd
            if head >= heads:
                break
            y = jnp.where(lane < half, pltpu.roll(x, half, 1) if odd else x, 0.0)
            for s in range(steps):
                query[:, pad * s + head, :] = y[s * rows : (s + 1) * rows]
    for s in range(steps):
        for head in range(heads, pad):
            query[:, pad * s + head, :] = jnp.zeros((rows, 2 * half), f32)
    place = lax.broadcasted_iota(jnp.int32, (rows, 16, 2 * half), 1)
    tail = jnp.zeros((rows, 16, 2 * half), f32)
    for t in range(steps):
        tail = jnp.where(place == t, new_ref[t, 0].astype(f32)[:, None, :], tail)
    kv = jnp.concatenate([kv_ref[0], tail.astype(bf16)], axis=1)
    scores = jnp.einsum(
        "bqd,bkd->bqk", query[:, : steps * pad].astype(bf16), kv, preferred_element_type=f32
    )
    weights = []
    for s in range(steps):
        mine = scores[:, pad * s : pad * (s + 1)]
        ok = valid_ref[:, s : s + 1, : kv.shape[1]] > 0
        mine = jnp.where(ok, mine, -jnp.inf)
        e = jnp.exp(mine - jnp.max(mine, axis=2, keepdims=True))
        weights.append((e / jnp.sum(e, axis=2, keepdims=True)).astype(bf16))
    weights = jnp.concatenate(weights, axis=1)
    result[:, : steps * pad] = jnp.einsum(
        "bqk,bkd->bqd", weights, kv, preferred_element_type=f32
    )
    low = lax.broadcasted_iota(jnp.int32, (rows, 2 * half), 1) < half
    for s in range(steps):
        for pair in range(heads // 2 + heads % 2):
            head = pad * s + 2 * pair
            even = pltpu.roll(result[:, head, :], half, 1)
            at = 2 * half * pair
            if 2 * pair + 1 < heads:
                both = jnp.where(low, even, result[:, head + 1, :])
                out_ref[s, 0, :, at : at + 2 * half] = both.astype(bf16)
            else:
                out_ref[s, 0, :, at : at + half] = even[:, :half].astype(bf16)


def attend(rank_low, up, frozen, kv, new_kv, valid, rows=32):
    steps, layers, rows_dev, width = frozen.shape
    slots, lanes = kv.shape[2:]
    pad = -(-(width // (lanes // 2)) // 8) * 8
    return pl.pallas_call(
        attend_kernel,
        grid=(layers, rows_dev // rows),
        in_specs=[
            pl.BlockSpec((steps, 1, rows, rank_low.shape[3]), lambda l, r: (0, l, r, 0)),
            pl.BlockSpec((1,) + up.shape[1:], lambda l, r: (l, 0, 0)),
            pl.BlockSpec((steps, 1, rows, width), lambda l, r: (0, l, r, 0)),
            pl.BlockSpec((1, rows, slots, lanes), lambda l, r: (l, r, 0, 0)),
            pl.BlockSpec((steps, 1, rows, lanes), lambda l, r: (0, l, r, 0)),
            pl.BlockSpec((rows, steps, lanes), lambda l, r: (r, 0, 0)),
        ],
        out_specs=pl.BlockSpec((steps, 1, rows, width), lambda l, r: (0, l, r, 0)),
        out_shape=jax.ShapeDtypeStruct(frozen.shape, bf16),
        scratch_shapes=[pltpu.VMEM((rows, steps * pad + 8, lanes), f32)] * 2,
        compiler_params=pltpu.CompilerParams(vmem_limit_bytes=VMEM_BYTES),
        name="attend",
    )(rank_low, up, frozen, kv, new_kv, valid)


def layer_call(kernel, name, core, arrays, layered, out):
    def whole(x):
        return pl.BlockSpec(x.shape, lambda i, c, n=x.ndim: (0,) * n)

    def layer(x, axis):
        shape = tuple(1 if d == axis else n for d, n in enumerate(x.shape))
        return pl.BlockSpec(
            shape, lambda i, c, n=x.ndim: tuple(c[0] if d == axis else 0 for d in range(n))
        )

    return pl.pallas_call(
        kernel,
        grid_spec=pltpu.PrefetchScalarGridSpec(
            num_scalar_prefetch=1,
            grid=(1,),
            in_specs=[whole(x) for x in arrays] + [layer(x, axis) for x, axis in layered],
            out_specs=whole(out),
        ),
        out_shape=out,
        compiler_params=pltpu.CompilerParams(vmem_limit_bytes=VMEM_BYTES),
        name=name,
    )(core.reshape(1), *arrays, *[x for x, _ in layered])


def shards(
    activations,
    cotangent,
    rewards,
    group_of,
    layer_owner,
    adapter_a,
    adapter_b,
    frozen_query_part,
    decode_in,
    kv_cache,
    new_kv,
    lengths,
):
    n_dp = lax.axis_size("dp")
    n_tensor = lax.axis_size("tensor")
    chips = n_dp // 2
    index = lax.axis_index("dp")
    core = index % 2
    chip = index // 2
    swap = [(i, i ^ 1) for i in range(n_dp)]
    same_core = [[i for i in range(n_dp) if i % 2 == c] for c in range(2)]
    layers, tokens, width = activations.shape
    completions = rewards.shape[0]
    steps, _, rows_dev, _ = decode_in.shape
    slots, lanes = kv_cache.shape[3:]

    def core_swap(x):
        return lax.ppermute(x, "dp", swap)

    def across_chips(x):
        return lax.all_to_all(x, "dp", 0, 0, axis_index_groups=same_core)

    def across_tensor(x):
        return lax.all_to_all(x, "tensor", 0, 0)

    own_info = jnp.stack([rewards, group_of.astype(f32)])
    far_a = core_swap(adapter_a)
    far_b = core_swap(adapter_b)
    far_info = core_swap(own_info)
    owner = pick(layer_owner, core)
    is_mine = owner % 2 == core
    candidate = jnp.concatenate(
        [
            jnp.where(is_mine, pick(adapter_a[0], core), pick(far_a[0], core)),
            jnp.where(is_mine, pick(adapter_b[0], core), pick(far_b[0], core)),
        ]
    )

    info = jnp.concatenate([own_info, far_info], axis=1)
    packed = jnp.concatenate([*split3(info[0]), info[1]]).astype(bf16)
    rows = candidate.shape[0] // chips
    tail = jnp.zeros((rows, 64), bf16).at[0, : packed.shape[0]].set(packed)
    message = jnp.concatenate(
        [candidate.reshape(chips, rows, width), jnp.broadcast_to(tail, (chips, rows, 64))], axis=2
    )
    message, act_out, cot_out, dec_out = lax.optimization_barrier(
        (message, activations, cotangent, decode_in)
    )
    arrived = across_chips(message)
    act = jnp.swapaxes(activations, 1, 2)
    cot = jnp.swapaxes(cotangent, 1, 2)
    far_act = core_swap(jnp.swapaxes(act_out, 1, 2))
    far_cot = core_swap(jnp.swapaxes(cot_out, 1, 2))
    far_dec = core_swap(dec_out)
    piece = pick(arrived, owner // 2)[:, :width]
    infos = arrived[:, 0, width : width + packed.shape[0]].astype(f32)
    infos = infos.reshape(chips, 4, 2 * completions)
    all_rewards = (infos[:, 0] + infos[:, 1] + infos[:, 2]).reshape(-1)
    all_groups = infos[:, 3].reshape(-1)
    labels = jnp.arange(n_dp * completions // GROUPS_PER_COMPLETION, dtype=f32)
    member = (all_groups[:, None] == labels[None, :]).astype(f32)
    group_mean = jnp.sum(member * all_rewards[:, None], axis=0) / jnp.maximum(
        jnp.sum(member, axis=0), 1.0
    )
    mine = (info[1][:, None] == labels[None, :]).astype(f32)
    advantage = info[0] - jnp.sum(mine * group_mean[None, :], axis=1)
    tok_adv = jnp.repeat(advantage, tokens // completions)

    factors = across_chips(jnp.broadcast_to(piece, (chips, rows, width)))
    factors = factors.reshape(chips * rows, width)

    token_arrays = [(act, 0), (far_act, 0), (cot, 0), (far_cot, 0)]
    parts = layer_call(
        project_kernel,
        "project",
        core,
        [factors],
        token_arrays,
        jax.ShapeDtypeStruct((n_tensor, 2 * R, 2 * tokens), bf16),
    )
    parts = across_tensor(parts)
    grads = layer_call(
        grad_kernel,
        "grads",
        core,
        [parts, tok_adv.reshape(1, -1)],
        token_arrays,
        jax.ShapeDtypeStruct((2 * R, width), bf16),
    )
    arrived = across_chips(grads.reshape(chips, rows, width))
    step = jnp.where(chip * rows < R, rate_a * D**-0.5, rate_b * R**-0.5)
    fresh = (piece.astype(f32) - step * jnp.sum(arrived.astype(f32), axis=0)).astype(bf16)
    fresh = across_chips(jnp.broadcast_to(fresh, (chips, rows, width)))
    fresh = fresh.reshape(chips * rows, width)

    ranks = layer_call(
        decode_kernel,
        "decode_rank",
        core,
        [fresh[:R]],
        [(decode_in, 1), (far_dec, 1)],
        jax.ShapeDtypeStruct((n_tensor, R, 2 * steps * rows_dev), bf16),
    )
    far_fresh = core_swap(fresh)
    first = jnp.where(core == 0, fresh, far_fresh)
    second = jnp.where(core == 0, far_fresh, fresh)
    new_a = jnp.stack([first[:R], second[:R]])
    new_b = jnp.stack([first[R:], second[R:]])
    ranks = across_tensor(ranks)
    rank_low = (jnp.sum(ranks.astype(f32), axis=0) * D**-0.5).astype(bf16)
    rank_low = rank_low.reshape(R, 2, steps, rows_dev)
    own_rank = rank_low[:, 0]
    far_rank = core_swap(rank_low[:, 1])
    rank_all = jnp.stack(
        [jnp.where(core == 0, own_rank, far_rank), jnp.where(core == 0, far_rank, own_rank)]
    )
    rank_all = jnp.transpose(rank_all, (2, 0, 3, 1))

    column = jnp.arange(lanes)[None, None, :]
    step_of = jnp.arange(steps)[None, :, None]
    valid = column < lengths[:, None, None]
    valid = valid | ((column >= slots) & (column <= slots + step_of))
    attended = attend(
        rank_all,
        new_b,
        frozen_query_part,
        kv_cache.reshape(layers, rows_dev, slots, lanes),
        new_kv.reshape(steps, layers, rows_dev, lanes),
        valid.astype(f32),
    )
    return (new_a, new_b, attended)


def solution(mesh):
    return jax.shard_map(
        shards,
        mesh=mesh,
        in_specs=(
            P(None, "dp", "tensor"),
            P(None, "dp", "tensor"),
            P("dp"),
            P("dp"),
            P(),
            P("dp", None, None, "tensor"),
            P("dp", None, None, "tensor"),
            P(None, None, "dp", "tensor"),
            P(None, None, "dp", "tensor"),
            P(None, "dp", "tensor", None, None),
            P(None, None, "dp", "tensor", None),
            P("dp"),
        ),
        out_specs=(P(None, None, "tensor"), P(None, None, "tensor"), P(None, None, "dp", "tensor")),
        check_vma=False,
    )
```

time: 179 us -> 157 us (0.88)
  matrix products: 25.9 us -> 0 us
  local copies, waits for them, and re-layouts: 22.7 us -> 6.09 us
  Pallas kernels: 0 us -> 16.5 us
  waiting for transfers between devices: 63.9 us -> 71.5 us
  other arithmetic: 10.1 us -> 6.8 us
    dot_general x14 -> x0, matrix products: 25.9 us -> none  [the longest x1 6.31 us: shards(): jnp.einsum('slrkgp,lrkpd->slrkgd', old_weight, cache_values, preferred_el...]
    pallas_call x0 -> x4, Pallas kernels: none -> 16.5 us  [the longest x1 9.01 us: attend(): pl.pallas_call(attend_kernel, grid=(layers, rows_dev // rows), in_specs=[...]
    all_to_all x4, waiting for transfers between devices: 44.1 us -> 53.4 us  [across_chips(): return lax.all_to_all(x, 'dp', 0, 0, axis_index_groups=same_core)]
    reshape x3 -> x0, local copies, waits for them, and re-layouts: 4.81 us -> none  [the longest x2 4.74 us: shards(): attended = combined.astype(bf16).reshape(steps, layers, rows_dev, width)]
    squeeze x4 -> x1, local copies, waits for them, and re-layouts: 4.7 us -> 0.01 us  [pick(): return lax.dynamic_index_in_dim(array, index, axis, keepdims=False)]
    another operation x2 -> x0, local copies, waits for them, and re-layouts: 4.46 us -> none
    reduce_sum x4 -> x1, other arithmetic: 3.33 us -> 0.04 us  [shards(): rank_low = (jnp.sum(ranks.astype(f32), axis=0) * D ** (-0.5)).astype(bf16)]
    select_n x0 -> x2, other arithmetic: none -> 2.09 us  [the longest x1 1.11 us: shards(): jnp.where(is_mine, pick(adapter_b[0], core), pick(far_b[0], core))]
  transfers between devices with their start and end apart: 13 -> 14, of which waited for: 8 -> 7; matrix products, arithmetic and copies ran while one was open for 7% -> 4% of each run, Pallas kernels for 0% -> 0%
where the time goes in v2:
time: 157 us; the launch traced here: 156 us
  waiting for transfers between devices  71.5 us (46%)
  starting transfers between devices  51.2 us (33%)
  Pallas kernels  16.5 us (11%)
  other arithmetic  6.8 us (4%)
  local copies, waits for them, and re-layouts  6.09 us (4%)
  between operations  3.59 us (2%)
    all_to_all x4, waiting for transfers between devices, across_chips(): return lax.all_to_all(x, 'dp', 0, 0, axis_index_groups=same_core)  53.4 us
    all_to_all x4, starting transfers between devices, across_chips(): return lax.all_to_all(x, 'dp', 0, 0, axis_index_groups=same_core)  30 us
    all_to_all x2, waiting for transfers between devices, across_tensor(): return lax.all_to_all(x, 'tensor', 0, 0)  17.2 us
    ppermute x8, starting transfers between devices, core_swap(): return lax.ppermute(x, 'dp', swap)  13.7 us
    pallas_call x1, Pallas kernels, attend(): pl.pallas_call(attend_kernel, grid=(layers, rows_dev // rows), in_specs=[...  9.01 us
    all_to_all x2, starting transfers between devices, across_tensor(): return lax.all_to_all(x, 'tensor', 0, 0)  7.54 us
    pallas_call x3, Pallas kernels, layer_call(): pl.pallas_call(kernel, grid_spec=pltpu.PrefetchScalarGridSpec(num_scalar_...  7.5 us
  transfers between devices with their start and end apart: 14, of which 7 were waited for; matrix products, arithmetic and copies ran while one was open for 4% of the time, Pallas kernels for 0%

profile of v2, /device:TPU:1, one launch (start us, length us, event | category | flops | bytes accessed | tf_op | source)
XLA Modules:
  0.0 155.7 jit_solution(16006130136854777005)
XLA Ops:
  0.6 3.3 %collective-permute-start = (bf16[1,2,64,1856]{3,2,1,0:T(8,128)(2,1)}, bf16[1,2,64,1856]{3,2,1,0:T(8,128)(2,1)S(1)}, u32[]{:S(2)}, u32[]{:S(2)}) collective-permute-start(bf16[1,2,64,1856]{3,2,1,0:T(8,128)(2,1)} %param.19), channel_id=1, source_target_pairs={{0,8},{8,0},{16,24},{24,16},{32,40},{40,32},{48,56},{56,48},{64,72... | collective-permute-start | bytes 1425416 | tf_op jit(solution)/shard_map/ppermute | solution.py:199
  4.0 0.1 collective-permute-start.1
  4.1 0.7 convert_bitcast_fusion
  4.7 0.7 pad_maximum_fusion.3
  5.4 0.4 collective-permute-start.2
  5.8 1.2 dynamic_slice.21
  9.0 0.7 pad_maximum_fusion.4
  9.7 0.1 fusion.8
  9.8 1.0 select_bitcast_fusion.1
  10.8 1.1 select_bitcast_fusion
  12.0 0.9 pad_maximum_fusion
  12.9 9.2 %all-to-all-start = ((bf16[16,8,1920]{2,1,0:T(8,128)(2,1)}), bf16[16,8,1920]{2,1,0:T(8,128)(2,1)S(1)}, u32[]{:S(2)}, u32[]{:S(2)}) async-start(bf16[16,8,1920]{2,1,0:T(8,128)(2,1)} %pad_maximum_fusion), calls=%async_computation | async-start | bytes 983040 | tf_op jit(solution)/shard_map/all_to_all | solution.py:202
  22.1 0.4 collective-permute-start.3
  22.6 0.1 collective-permute-start.4
  23.4 13.6 %all-to-all-done = bf16[16,8,1920]{2,1,0:T(8,128)(2,1)S(1)} async-done(((bf16[16,8,1920]{2,1,0:T(8,128)(2,1)}), bf16[16,8,1920]{2,1,0:T(8,128)(2,1)S(1)}, u32[]{:S(2)}, u32[]{:S(2)}) %all-to-all-start) | async-done | bytes 491552 | tf_op jit(solution)/shard_map/all_to_all | solution.py:202
  37.0 0.8 broadcast_in_dim.9
  37.8 6.4 %all-to-all-start.1 = ((bf16[16,8,1856]{2,1,0:T(8,128)(2,1)}), bf16[16,8,1856]{2,1,0:T(8,128)(2,1)S(1)}, u32[]{:S(2)}, u32[]{:S(2)}) async-start(bf16[16,8,1856]{2,1,0:T(8,128)(2,1)} %broadcast_in_dim.9), calls=%async_computation.1 | async-start | bytes 983040 | tf_op jit(solution)/shard_map/all_to_all | solution.py:202
  44.1 0.1 slice.83
  44.2 14.1 %all-to-all-done.1 = bf16[16,8,1856]{2,1,0:T(8,128)(2,1)S(1)} async-done(((bf16[16,8,1856]{2,1,0:T(8,128)(2,1)}), bf16[16,8,1856]{2,1,0:T(8,128)(2,1)S(1)}, u32[]{:S(2)}, u32[]{:S(2)}) %all-to-all-start.1) | async-done | bytes 475168 | tf_op jit(solution)/shard_map/all_to_all | solution.py:202
  58.4 2.6 %project.1 = bf16[8,128,512]{2,1,0:T(8,128)(2,1)S(1)} custom-call(s32[1]{0:T(128)} %bitcast.7.core, bf16[128,1856]{1,0:T(8,128)(2,1)S(1)} %bitcast.66, bf16[2,1856,256]{2,1,0:T(8,128)(2,1)S(1)} %bitcast.63, bf16[2,1856,256]{2,1,0:T(8,128)(2,1)} %collective-permute-done.3.far_act, bf16[2,1856,256]{2,1,0:T(8,128)(2,1)} %bitcast.70, ...), custom_call_target="tpu_custom_call" | custom-call | tf_op jit(solution)/shard_map/project/pallas_call | solution.py:157
  60.9 1.0 copy-done.1
  61.9 4.1 %all-to-all-start.2 = ((bf16[8,128,512]{2,1,0:T(8,128)(2,1)}), bf16[8,128,512]{2,1,0:T(8,128)(2,1)S(1)}, u32[]{:S(2)}, u32[]{:S(2)}) async-start(bf16[8,128,512]{2,1,0:T(8,128)(2,1)} %copy-done.1), calls=%async_computation.2 | async-start | bytes 2097152 | tf_op jit(solution)/shard_map/all_to_all | solution.py:205
  66.1 0.1 copy.42
  66.2 0.1 add.58
  66.3 0.1 copy.41
  66.4 0.1 eq.45
  66.5 0.1 convert_reduce_fusion.2
  66.6 0.2 select_reduce_fusion.1
  66.8 14.4 %all-to-all-done.2.parts = bf16[8,128,512]{2,1,0:T(8,128)(2,1)S(1)} async-done(((bf16[8,128,512]{2,1,0:T(8,128)(2,1)}), bf16[8,128,512]{2,1,0:T(8,128)(2,1)S(1)}, u32[]{:S(2)}, u32[]{:S(2)}) %all-to-all-start.2) | async-done | bytes 1048608 | tf_op jit(solution)/shard_map/all_to_all | solution.py:205
  81.3 3.7 %grads.1 = bf16[128,1856]{1,0:T(8,128)(2,1)} custom-call(s32[1]{0:T(128)} %bitcast.7.core, bf16[8,128,512]{2,1,0:T(8,128)(2,1)S(1)} %all-to-all-done.2.parts, f32[1,512]{1,0:T(1,128)S(1)} %bitcast.68, bf16[2,1856,256]{2,1,0:T(8,128)(2,1)S(1)} %bitcast.64, bf16[2,1856,256]{2,1,0:T(8,128)(2,1)} %collective-permute-done.3.far_act, ...), custom_call_target="tpu_custom_call" | custom-call | tf_op jit(solution)/shard_map/grads/pallas_call | solution.py:157
  85.0 7.8 %all-to-all-start.3 = ((bf16[16,8,1856]{2,1,0:T(8,128)(2,1)}), bf16[16,8,1856]{2,1,0:T(8,128)(2,1)S(1)}, u32[]{:S(2)}, u32[]{:S(2)}) async-start(bf16[16,8,1856]{2,1,0:T(8,128)(2,1)} %bitcast.17), calls=%async_computation.3 | async-start | bytes 983040 | tf_op jit(solution)/shard_map/all_to_all | solution.py:202
  92.9 13.7 %all-to-all-done.3 = bf16[16,8,1856]{2,1,0:T(8,128)(2,1)S(1)} async-done(((bf16[16,8,1856]{2,1,0:T(8,128)(2,1)}), bf16[16,8,1856]{2,1,0:T(8,128)(2,1)S(1)}, u32[]{:S(2)}, u32[]{:S(2)}) %all-to-all-start.3) | async-done | bytes 475168 | tf_op jit(solution)/shard_map/all_to_all | solution.py:202
  106.7 0.8 broadcast_in_dim.22
  107.5 6.6 %all-to-all-start.4 = ((bf16[16,8,1856]{2,1,0:T(8,128)(2,1)}), bf16[16,8,1856]{2,1,0:T(8,128)(2,1)S(1)}, u32[]{:S(2)}, u32[]{:S(2)}) async-start(bf16[16,8,1856]{2,1,0:T(8,128)(2,1)} %broadcast_in_dim.22), calls=%async_computation.4 | async-start | bytes 983040 | tf_op jit(solution)/shard_map/all_to_all | solution.py:202
  114.1 1.8 %collective-permute-start.6 = (bf16[2,2,64,1856]{3,2,1,0:T(8,128)(2,1)S(1)}, bf16[2,2,64,1856]{3,2,1,0:T(8,128)(2,1)S(1)}, u32[]{:S(2)}, u32[]{:S(2)}) collective-permute-start(bf16[2,2,64,1856]{3,2,1,0:T(8,128)(2,1)S(1)} %copy-done.4), channel_id=1, source_target_pairs={{0,8},{8,0},{16,24},{24,16},{32,40},{40,32},{48,56},{56,48},{64,72... | collective-permute-start | bytes 2850824 | tf_op jit(solution)/shard_map/ppermute | solution.py:199
  115.9 12.0 %all-to-all-done.4 = bf16[16,8,1856]{2,1,0:T(8,128)(2,1)S(1)} async-done(((bf16[16,8,1856]{2,1,0:T(8,128)(2,1)}), bf16[16,8,1856]{2,1,0:T(8,128)(2,1)S(1)}, u32[]{:S(2)}, u32[]{:S(2)}) %all-to-all-start.4) | async-done | bytes 475168 | tf_op jit(solution)/shard_map/all_to_all | solution.py:202
  128.0 1.2 decode_rank.1
  129.2 3.4 %all-to-all-start.5 = ((bf16[8,64,256]{2,1,0:T(8,128)(2,1)}), bf16[8,64,256]{2,1,0:T(8,128)(2,1)S(1)}, u32[]{:S(2)}, u32[]{:S(2)}) async-start(bf16[8,64,256]{2,1,0:T(8,128)(2,1)} %decode_rank.1), calls=%async_computation.5 | async-start | bytes 524288 | tf_op jit(solution)/shard_map/all_to_all | solution.py:205
  132.6 0.1 compare_and_fusion
  132.8 3.1 %collective-permute-start.5 = (bf16[128,1856]{1,0:T(8,128)(2,1)S(1)}, bf16[128,1856]{1,0:T(8,128)(2,1)S(1)}, u32[]{:S(2)}, u32[]{:S(2)}) collective-permute-start(bf16[128,1856]{1,0:T(8,128)(2,1)S(1)} %bitcast.72), channel_id=1, source_target_pairs={{0,8},{8,0},{16,24},{24,16},{32,40},{40,32},{48,56},{56,48},{64,72... | collective-permute-start | bytes 1425416 | tf_op jit(solution)/shard_map/ppermute | solution.py:199
  135.9 2.8 %all-to-all-done.5 = bf16[8,64,256]{2,1,0:T(8,128)(2,1)S(1)} async-done(((bf16[8,64,256]{2,1,0:T(8,128)(2,1)}), bf16[8,64,256]{2,1,0:T(8,128)(2,1)S(1)}, u32[]{:S(2)}, u32[]{:S(2)}) %all-to-all-start.5) | async-done | bytes 262176 | tf_op jit(solution)/shard_map/all_to_all | solution.py:205
  138.7 0.1 copy.43
  138.9 4.3 %collective-permute-start.7 = (bf16[64,2,64]{0,2,1:T(8,128)(2,1)S(1)}, bf16[64,2,64]{0,2,1:T(8,128)(2,1)S(1)}, u32[]{:S(2)}, u32[]{:S(2)}) collective-permute-start(bf16[64,2,64]{0,2,1:T(8,128)(2,1)S(1)} %slice_bitcast_fusion.5), channel_id=1, source_target_pairs={{0,8},{8,0},{16,24},{24,16},{32,40},{40,32},{48,56},{56,48},{64,72... | collective-permute-start | bytes 49160 | tf_op jit(solution)/shard_map/ppermute | solution.py:199
  143.2 0.8 collective-permute-done.7
  144.1 0.1 broadcast_select_fusion.1
  144.4 0.8 pad_maximum_fusion.1
  145.3 1.4 copy-done.2
  146.6 9.0 %attend.1 = bf16[2,2,64,1856]{3,2,1,0:T(8,128)(2,1)} custom-call(bf16[2,2,64,64]{3,2,1,0:T(8,128)(2,1)S(1)} %maximum_bitcast_fusion.1.rank_ref, bf16[2,64,1856]{2,1,0:T(8,128)(2,1)S(1)} %pad_maximum_fusion.2.up_ref, bf16[2,2,64,1856]{3,2,1,0:T(8,128)(2,1)S(1)} %copy-done.5, bf16[2,64,96,128]{3,2,1,0:T(8,128)(2,1)S(1)} %bitcast.65, ...), custom_call_target="tpu_custom_call" | custom-call | tf_op jit(solution)/shard_map/attend/pallas_call | solution.py:128
  (46 shorter events, 0.8 us)
Async XLA Ops:
  0.6 9.2 %collective-permute-start = (bf16[1,2,64,1856]{3,2,1,0:T(8,128)(2,1)}, bf16[1,2,64,1856]{3,2,1,0:T(8,128)(2,1)S(1)}, u32[]{:S(2)}, u32[]{:S(2)}) collective-permute-start(bf16[1,2,64,1856]{3,2,1,0:T(8,128)(2,1)} %param.19), channel_id=1, source_target_pairs={{0,8},{8,0},{16,24},{24,16},{32,40},{40,32},{48,56},{56,48},{64,72... | collective-permute-start | bytes 1425416 | tf_op jit(solution)/shard_map/ppermute | solution.py:199
  4.0 6.9 %collective-permute-start.1 = (bf16[1,2,64,1856]{3,2,1,0:T(8,128)(2,1)}, bf16[1,2,64,1856]{3,2,1,0:T(8,128)(2,1)S(1)}, u32[]{:S(2)}, u32[]{:S(2)}) collective-permute-start(bf16[1,2,64,1856]{3,2,1,0:T(8,128)(2,1)} %param.20), channel_id=1, source_target_pairs={{0,8},{8,0},{16,24},{24,16},{32,40},{40,32},{48,56},{56,48},{64,72... | collective-permute-start | bytes 1425416 | tf_op jit(solution)/shard_map/ppermute | solution.py:199
  5.4 3.6 %collective-permute-start.2 = (f32[2,2]{1,0:T(2,128)S(1)}, f32[2,2]{1,0:T(2,128)S(1)}, u32[]{:S(2)}, u32[]{:S(2)}) collective-permute-start(f32[2,2]{1,0:T(2,128)S(1)} %pad_maximum_fusion.3), channel_id=1, source_target_pairs={{0,8},{8,0},{16,24},{24,16},{32,40},{40,32},{48,56},{56,48},{64,72... | collective-permute-start | bytes 56 | tf_op jit(solution)/shard_map/ppermute | solution.py:199
  10.8 11.3 %copy-start = (bf16[2,256,1856]{1,2,0:T(8,128)(2,1)S(1)}, bf16[2,256,1856]{1,2,0:T(8,128)(2,1)}, u32[]{:S(2)}) copy-start(bf16[2,256,1856]{1,2,0:T(8,128)(2,1)} %param.14) | copy-start | bytes 5701636
  12.9 24.1 %all-to-all-start = ((bf16[16,8,1920]{2,1,0:T(8,128)(2,1)}), bf16[16,8,1920]{2,1,0:T(8,128)(2,1)S(1)}, u32[]{:S(2)}, u32[]{:S(2)}) async-start(bf16[16,8,1920]{2,1,0:T(8,128)(2,1)} %pad_maximum_fusion), calls=%async_computation | async-start | bytes 983040 | tf_op jit(solution)/shard_map/all_to_all | solution.py:202
  22.1 36.2 %collective-permute-start.3 = (bf16[2,1856,256]{2,1,0:T(8,128)(2,1)S(1)}, bf16[2,1856,256]{2,1,0:T(8,128)(2,1)}, u32[]{:S(2)}, u32[]{:S(2)}) collective-permute-start(bf16[2,1856,256]{2,1,0:T(8,128)(2,1)S(1)} %bitcast.62), channel_id=1, source_target_pairs={{0,8},{8,0},{16,24},{24,16},{32,40},{40,32},{48,56},{56,48},{64,72... | collective-permute-start | bytes 5701640 | tf_op jit(solution)/shard_map/ppermute | solution.py:199
  22.6 35.8 %collective-permute-start.4 = (bf16[2,1856,256]{2,1,0:T(8,128)(2,1)}, bf16[2,1856,256]{2,1,0:T(8,128)(2,1)}, u32[]{:S(2)}, u32[]{:S(2)}) collective-permute-start(bf16[2,1856,256]{2,1,0:T(8,128)(2,1)} %bitcast.69), channel_id=1, source_target_pairs={{0,8},{8,0},{16,24},{24,16},{32,40},{40,32},{48,56},{56,48},{64,72... | collective-permute-start | bytes 5701640 | tf_op jit(solution)/shard_map/ppermute | solution.py:199
  37.8 20.6 %all-to-all-start.1 = ((bf16[16,8,1856]{2,1,0:T(8,128)(2,1)}), bf16[16,8,1856]{2,1,0:T(8,128)(2,1)S(1)}, u32[]{:S(2)}, u32[]{:S(2)}) async-start(bf16[16,8,1856]{2,1,0:T(8,128)(2,1)} %broadcast_in_dim.9), calls=%async_computation.1 | async-start | bytes 983040 | tf_op jit(solution)/shard_map/all_to_all | solution.py:202
  60.9 1.0 copy-start.1
  61.9 19.3 %all-to-all-start.2 = ((bf16[8,128,512]{2,1,0:T(8,128)(2,1)}), bf16[8,128,512]{2,1,0:T(8,128)(2,1)S(1)}, u32[]{:S(2)}, u32[]{:S(2)}) async-start(bf16[8,128,512]{2,1,0:T(8,128)(2,1)} %copy-done.1), calls=%async_computation.2 | async-start | bytes 2097152 | tf_op jit(solution)/shard_map/all_to_all | solution.py:205
  85.0 29.0 %copy-start.4 = (bf16[2,2,64,1856]{3,2,1,0:T(8,128)(2,1)S(1)}, bf16[2,2,64,1856]{3,2,1,0:T(8,128)(2,1)}, u32[]{:S(2)}) copy-start(bf16[2,2,64,1856]{3,2,1,0:T(8,128)(2,1)} %dec.1) | copy-start | bytes 2850820
  85.0 21.6 %all-to-all-start.3 = ((bf16[16,8,1856]{2,1,0:T(8,128)(2,1)}), bf16[16,8,1856]{2,1,0:T(8,128)(2,1)S(1)}, u32[]{:S(2)}, u32[]{:S(2)}) async-start(bf16[16,8,1856]{2,1,0:T(8,128)(2,1)} %bitcast.17), calls=%async_computation.3 | async-start | bytes 983040 | tf_op jit(solution)/shard_map/all_to_all | solution.py:202
  107.5 20.5 %all-to-all-start.4 = ((bf16[16,8,1856]{2,1,0:T(8,128)(2,1)}), bf16[16,8,1856]{2,1,0:T(8,128)(2,1)S(1)}, u32[]{:S(2)}, u32[]{:S(2)}) async-start(bf16[16,8,1856]{2,1,0:T(8,128)(2,1)} %broadcast_in_dim.22), calls=%async_computation.4 | async-start | bytes 983040 | tf_op jit(solution)/shard_map/all_to_all | solution.py:202
  114.1 18.6 %copy-start.7 = (s32[64]{0:T(128)S(1)}, s32[64]{0:T(128)}, u32[]{:S(2)}) copy-start(s32[64]{0:T(128)} %param.25) | copy-start | bytes 772
  114.1 13.9 %collective-permute-start.6 = (bf16[2,2,64,1856]{3,2,1,0:T(8,128)(2,1)S(1)}, bf16[2,2,64,1856]{3,2,1,0:T(8,128)(2,1)S(1)}, u32[]{:S(2)}, u32[]{:S(2)}) collective-permute-start(bf16[2,2,64,1856]{3,2,1,0:T(8,128)(2,1)S(1)} %copy-done.4), channel_id=1, source_target_pairs={{0,8},{8,0},{16,24},{24,16},{32,40},{40,32},{48,56},{56,48},{64,72... | collective-permute-start | bytes 2850824 | tf_op jit(solution)/shard_map/ppermute | solution.py:199
  129.2 9.5 %all-to-all-start.5 = ((bf16[8,64,256]{2,1,0:T(8,128)(2,1)}), bf16[8,64,256]{2,1,0:T(8,128)(2,1)S(1)}, u32[]{:S(2)}, u32[]{:S(2)}) async-start(bf16[8,64,256]{2,1,0:T(8,128)(2,1)} %decode_rank.1), calls=%async_computation.5 | async-start | bytes 524288 | tf_op jit(solution)/shard_map/all_to_all | solution.py:205
  132.8 11.3 %collective-permute-start.5 = (bf16[128,1856]{1,0:T(8,128)(2,1)S(1)}, bf16[128,1856]{1,0:T(8,128)(2,1)S(1)}, u32[]{:S(2)}, u32[]{:S(2)}) collective-permute-start(bf16[128,1856]{1,0:T(8,128)(2,1)S(1)} %bitcast.72), channel_id=1, source_target_pairs={{0,8},{8,0},{16,24},{24,16},{32,40},{40,32},{48,56},{56,48},{64,72... | collective-permute-start | bytes 1425416 | tf_op jit(solution)/shard_map/ppermute | solution.py:199
  138.9 5.2 %collective-permute-start.7 = (bf16[64,2,64]{0,2,1:T(8,128)(2,1)S(1)}, bf16[64,2,64]{0,2,1:T(8,128)(2,1)S(1)}, u32[]{:S(2)}, u32[]{:S(2)}) collective-permute-start(bf16[64,2,64]{0,2,1:T(8,128)(2,1)S(1)} %slice_bitcast_fusion.5), channel_id=1, source_target_pairs={{0,8},{8,0},{16,24},{24,16},{32,40},{40,32},{48,56},{56,48},{64,72... | collective-permute-start | bytes 49160 | tf_op jit(solution)/shard_map/ppermute | solution.py:199
  144.1 1.2 copy-start.5
  144.2 2.5 %copy-start.2 = (bf16[2,64,1,96,128]{4,3,2,1,0:T(8,128)(2,1)S(1)}, bf16[2,64,1,96,128]{4,3,2,1,0:T(8,128)(2,1)}, u32[]{:S(2)}) copy-start(bf16[2,64,1,96,128]{4,3,2,1,0:T(8,128)(2,1)} %param.23) | copy-start | bytes 9437188
  144.2 2.5 %copy-start.6 = (bf16[2,2,64,1,128]{4,2,3,1,0:T(8,128)(2,1)S(1)}, bf16[2,2,64,1,128]{4,2,3,1,0:T(8,128)(2,1)}, u32[]{:S(2)}) copy-start(bf16[2,2,64,1,128]{4,2,3,1,0:T(8,128)(2,1)} %param.24) | copy-start | bytes 196612
  144.3 11.3 %copy-start.3 = (bf16[2,64,1856]{2,1,0:T(8,128)(2,1)}, bf16[2,64,1856]{2,1,0:T(8,128)(2,1)S(1)}, u32[]{:S(2)}) copy-start(bf16[2,64,1856]{2,1,0:T(8,128)(2,1)S(1)} %pad_maximum_fusion.2.up_ref) | copy-start | bytes 1425412

commit v3 on v2

v3 whole, which is shorter than its diff:
```python
import jax
import jax.numpy as jnp
from jax import lax
from jax.experimental import pallas as pl
from jax.experimental.pallas import tpu as pltpu
from jax.sharding import PartitionSpec as P

D = 14848
R = 64
GROUPS_PER_COMPLETION = 4
VMEM_BYTES = 32 * 1024 * 1024

rate_a = 0.5
rate_b = 0.05

f32 = jnp.float32
bf16 = jnp.bfloat16


def pick(array, index, axis=0):
    return lax.dynamic_index_in_dim(array, index, axis, keepdims=False)


def split3(x):
    hi = lax.reduce_precision(x, 8, 7)
    mid = lax.reduce_precision(x - hi, 8, 7)
    lo = lax.reduce_precision(x - hi - mid, 8, 7)
    return hi, mid, lo


def nt_dot(a, b):
    return lax.dot_general(a, b, (((1,), (1,)), ((), ())), preferred_element_type=f32)


def in_hbm(x):
    return pltpu.with_memory_space_constraint(x, pltpu.HBM)


def start_all(copies):
    for copy in copies:
        copy.start()
    return copies


def message_kernel(core, owner, own_a, own_b, far_a, far_b, out, both, sems):
    r = own_a.shape[2]

    def run(sources):
        arriving = start_all(
            [
                pltpu.make_async_copy(
                    source.at[0, core[0]], both.at[pl.ds(half * r, r)], sems.at[half]
                )
                for half, source in enumerate(sources)
            ]
        )
        leaving = []
        for half, copy in enumerate(arriving):
            rows = pl.ds(half * r, r)
            copy.wait()
            leaving += start_all(
                [pltpu.make_async_copy(both.at[rows], out.at[rows], sems.at[2 + half])]
            )
        for copy in leaving:
            copy.wait()

    is_mine = owner[core[0]] % 2 == core[0]

    @pl.when(is_mine)
    def _():
        run((own_a, own_b))

    @pl.when(jnp.logical_not(is_mine))
    def _():
        run((far_a, far_b))


def load_tokens(core, sources, held, sems):
    return start_all(
        [
            pltpu.make_async_copy(source.at[core[0]], held.at[i], sems.at[i])
            for i, source in enumerate(sources)
        ]
    )


def project_kernel(core, factors, act, far_act, cot, far_cot, out, held, part, sems, out_sems):
    r = factors.shape[0] // 2
    _, width, tokens = held.shape
    arriving = load_tokens(core, (act, far_act, cot, far_cot), held, sems)
    leaving = []
    for half in range(2):
        rows = pl.ds(half * r, r)
        factor = factors[half * r : (half + 1) * r, :width]
        for place in range(2):
            arriving[2 * half + place].wait()
            part[rows, place * tokens : (place + 1) * tokens] = jnp.dot(
                factor, held[2 * half + place], preferred_element_type=f32
            ).astype(bf16)
        leaving += start_all(
            [
                pltpu.make_async_copy(part.at[rows], out.at[peer, rows], out_sems.at[half, peer])
                for peer in range(out.shape[0])
            ]
        )
    for copy in leaving:
        copy.wait()


def grad_kernel(core, advantage, parts, act, far_act, cot, far_cot, out, held, sems):
    r = parts.shape[1] // 2
    _, width, tokens = held.shape
    arriving = load_tokens(core, (act, far_act, cot, far_cot), held, sems)
    count = advantage.shape[0]
    sequence = lax.broadcasted_iota(jnp.int32, (1, 2 * tokens), 1) // (2 * tokens // count)
    adv = jnp.zeros(sequence.shape, f32)
    for i in range(count):
        adv = jnp.where(sequence == i, advantage[i], adv)
    total = jnp.sum(parts[...].astype(f32), axis=0)
    low = (total[:r] * D**-0.5).astype(bf16).astype(f32)
    low = (low * adv).astype(bf16)
    back = (total[r:] * (adv * R**-0.5)).astype(bf16)
    for half, rank in enumerate((back, low)):
        arriving[2 * half].wait()
        grad = nt_dot(rank[:, :tokens], held[2 * half])
        arriving[2 * half + 1].wait()
        grad += nt_dot(rank[:, tokens:], held[2 * half + 1])
        out[half * r : (half + 1) * r] = grad.astype(bf16)


def decode_kernel(core, fresh, dec, far_dec, out):
    steps, _, rows, width = dec.shape
    mine, other = core[0], 1 - core[0]
    for place, source in ((mine, dec), (other, far_dec)):
        part = nt_dot(fresh[: out.shape[2]], source[:, 0].reshape(steps * rows, width)).astype(bf16)
        for peer in range(out.shape[0]):
            out[peer, place] = part


def attend_kernel(
    core,
    rank_ref,
    fresh,
    far_fresh,
    frozen_ref,
    kv_ref,
    new_ref,
    valid_ref,
    new_a,
    new_b,
    out_ref,
    change,
):
    steps, _, rows, width = frozen_ref.shape
    half = kv_ref.shape[3] // 2
    heads = width // half
    pad = -(-heads // 8) * 8
    layer, block = pl.program_id(0), pl.program_id(1)

    def begin(source):
        new_a[0] = source[:R]
        new_b[0] = source[R:]
        rank = (jnp.sum(rank_ref[:, 0].astype(f32), axis=0) * D**-0.5).astype(bf16)
        change[...] = lax.dot_general(
            rank, source[R:], (((0,), (0,)), ((), ())), preferred_element_type=f32
        ).reshape(change.shape)

    @pl.when((block == 0) & (layer == core[0]))
    def _():
        begin(fresh)

    @pl.when((block == 0) & (layer != core[0]))
    def _():
        begin(far_fresh)

    delta = change[:, pl.ds(block * rows, rows)].reshape(steps * rows, width)
    q = frozen_ref[:, 0].reshape(steps * rows, width).astype(f32) + delta * R**-0.5
    q = q.astype(bf16).astype(f32) * (half**-0.5)
    lane = lax.broadcasted_iota(jnp.int32, (steps * rows, 2 * half), 1)
    pieces = [[jnp.zeros((rows, 2 * half), f32)] * pad for _ in range(steps)]
    for pair in range(heads // 2 + heads % 2):
        x = q[:, 2 * half * pair : 2 * half * (pair + 1)]
        if x.shape[1] < 2 * half:
            x = jnp.concatenate([x, jnp.zeros_like(x)], axis=1)
        for odd in range(2):
            head = 2 * pair + odd
            if head >= heads:
                break
            y = jnp.where(lane < half, pltpu.roll(x, half, 1) if odd else x, 0.0)
            for s in range(steps):
                pieces[s][head] = y[s * rows : (s + 1) * rows]
    query = jnp.transpose(jnp.stack(sum(pieces, [])), (1, 0, 2)).astype(bf16)
    place = lax.broadcasted_iota(jnp.int32, (rows, 16, 2 * half), 1)
    tail = jnp.zeros((rows, 16, 2 * half), f32)
    for t in range(steps):
        tail = jnp.where(place == t, new_ref[t, 0].astype(f32)[:, None, :], tail)
    kv = jnp.concatenate([kv_ref[0], tail.astype(bf16)], axis=1)
    scores = jnp.einsum("bqd,bkd->bqk", query, kv, preferred_element_type=f32)
    weights = []
    for s in range(steps):
        mine = scores[:, pad * s : pad * (s + 1)]
        ok = valid_ref[:, s : s + 1, : kv.shape[1]] > 0
        mine = jnp.where(ok, mine, -jnp.inf)
        e = jnp.exp(mine - jnp.max(mine, axis=2, keepdims=True))
        weights.append((e / jnp.sum(e, axis=2, keepdims=True)).astype(bf16))
    weights = jnp.concatenate(weights, axis=1)
    result = jnp.einsum("bqk,bkd->bqd", weights, kv, preferred_element_type=f32)
    result = jnp.transpose(result, (1, 0, 2))
    low = lax.broadcasted_iota(jnp.int32, (rows, 2 * half), 1) < half
    for s in range(steps):
        for pair in range(heads // 2 + heads % 2):
            head = pad * s + 2 * pair
            even = pltpu.roll(result[head], half, 1)
            at = 2 * half * pair
            if 2 * pair + 1 < heads:
                both = jnp.where(low, even, result[head + 1])
                out_ref[s, 0, :, at : at + 2 * half] = both.astype(bf16)
            else:
                out_ref[s, 0, :, at : at + half] = even[:, :half].astype(bf16)


def attend(core, ranks, fresh, far_fresh, frozen, kv, new_kv, valid, rows=32):
    steps, layers, rows_dev, width = frozen.shape
    slots, lanes = kv.shape[2:]
    factor = jax.ShapeDtypeStruct((layers, R, width), bf16)
    return pl.pallas_call(
        attend_kernel,
        grid_spec=pltpu.PrefetchScalarGridSpec(
            num_scalar_prefetch=1,
            grid=(layers, rows_dev // rows),
            in_specs=[
                pl.BlockSpec((ranks.shape[0], 1) + ranks.shape[2:], lambda l, r, c: (0, l, 0, 0)),
                pl.BlockSpec(fresh.shape, lambda l, r, c: (0, 0)),
                pl.BlockSpec(fresh.shape, lambda l, r, c: (0, 0)),
                pl.BlockSpec((steps, 1, rows, width), lambda l, r, c: (0, l, r, 0)),
                pl.BlockSpec((1, rows, slots, lanes), lambda l, r, c: (l, r, 0, 0)),
                pl.BlockSpec((steps, 1, rows, lanes), lambda l, r, c: (0, l, r, 0)),
                pl.BlockSpec((rows, steps, lanes), lambda l, r, c: (r, 0, 0)),
            ],
            out_specs=[
                pl.BlockSpec((1, R, width), lambda l, r, c: (l, 0, 0)),
                pl.BlockSpec((1, R, width), lambda l, r, c: (l, 0, 0)),
                pl.BlockSpec((steps, 1, rows, width), lambda l, r, c: (0, l, r, 0)),
            ],
            scratch_shapes=[pltpu.VMEM((steps, rows_dev, width), f32)],
        ),
        out_shape=[factor, factor, jax.ShapeDtypeStruct(frozen.shape, bf16)],
        compiler_params=pltpu.CompilerParams(vmem_limit_bytes=VMEM_BYTES),
        name="attend",
    )(core.reshape(1), ranks, fresh, far_fresh, frozen, kv, new_kv, valid)


def layer_call(kernel, name, core, arrays, layered, out):
    def whole(x):
        return pl.BlockSpec(x.shape, lambda i, c, n=len(x.shape): (0,) * n)

    def layer(x, axis):
        shape = tuple(1 if d == axis else n for d, n in enumerate(x.shape))
        return pl.BlockSpec(
            shape, lambda i, c, n=x.ndim: tuple(c[0] if d == axis else 0 for d in range(n))
        )

    return pl.pallas_call(
        kernel,
        grid_spec=pltpu.PrefetchScalarGridSpec(
            num_scalar_prefetch=1,
            grid=(1,),
            in_specs=[whole(x) for x in arrays] + [layer(x, axis) for x, axis in layered],
            out_specs=whole(out),
        ),
        out_shape=pltpu.HBM(out.shape, out.dtype),
        compiler_params=pltpu.CompilerParams(vmem_limit_bytes=VMEM_BYTES),
        name=name,
    )(core.reshape(1), *arrays, *[x for x, _ in layered])


def local_call(kernel, name, scalars, whole, streamed, out, scratch, by_copy=True):
    def block(shape):
        return pl.BlockSpec(shape, lambda i, *_: (0,) * len(shape))

    return pl.pallas_call(
        kernel,
        grid_spec=pltpu.PrefetchScalarGridSpec(
            num_scalar_prefetch=len(scalars),
            grid=(1,),
            in_specs=[block(x.shape) for x in whole]
            + [pl.BlockSpec(memory_space=pl.ANY)] * len(streamed),
            out_specs=pl.BlockSpec(memory_space=pl.ANY) if by_copy else block(out),
            scratch_shapes=scratch,
        ),
        out_shape=pltpu.HBM(out, bf16),
        compiler_params=pltpu.CompilerParams(vmem_limit_bytes=VMEM_BYTES),
        name=name,
    )(*scalars, *whole, *streamed)


def shards(
    activations,
    cotangent,
    rewards,
    group_of,
    layer_owner,
    adapter_a,
    adapter_b,
    frozen_query_part,
    decode_in,
    kv_cache,
    new_kv,
    lengths,
):
    n_dp = lax.axis_size("dp")
    n_tensor = lax.axis_size("tensor")
    chips = n_dp // 2
    index = lax.axis_index("dp")
    core = index % 2
    chip = index // 2
    swap = [(i, i ^ 1) for i in range(n_dp)]
    same_core = [[i for i in range(n_dp) if i % 2 == c] for c in range(2)]
    layers, tokens, width = activations.shape
    completions = rewards.shape[0]
    steps, _, rows_dev, _ = decode_in.shape
    slots, lanes = kv_cache.shape[3:]

    def core_swap(x):
        return lax.ppermute(x, "dp", swap)

    def across_chips(x):
        return lax.all_to_all(x, "dp", 0, 0, axis_index_groups=same_core)

    def across_tensor(x):
        return lax.all_to_all(x, "tensor", 0, 0)

    far_a = core_swap(adapter_a)
    far_b = core_swap(adapter_b)
    scalars = [core.reshape(1)]
    candidate = local_call(
        message_kernel,
        "message",
        scalars + [in_hbm(layer_owner)],
        [],
        [in_hbm(adapter_a), in_hbm(adapter_b), far_a, far_b],
        (2 * R, width),
        [pltpu.VMEM((2 * R, width), bf16), pltpu.SemaphoreType.DMA((4,))],
    )
    rows = candidate.shape[0] // chips

    message, act_out, cot_out, dec_out, rewards, group_of = lax.optimization_barrier(
        (
            candidate.reshape(chips, rows, width),
            activations,
            cotangent,
            decode_in,
            rewards,
            group_of,
        )
    )
    arrived = across_chips(message)
    act = jnp.swapaxes(activations, 1, 2)
    cot = jnp.swapaxes(cotangent, 1, 2)
    own_info = jnp.stack([rewards, group_of.astype(f32)])
    far_info = core_swap(own_info)
    far_act = core_swap(jnp.swapaxes(act_out, 1, 2))
    far_cot = core_swap(jnp.swapaxes(cot_out, 1, 2))
    far_dec = core_swap(dec_out)
    piece = pick(arrived, pick(layer_owner, core) // 2)

    info = jnp.concatenate([own_info, far_info], axis=1)
    packed = jnp.concatenate([*split3(info[0]), info[1]]).astype(bf16)
    tail = jnp.zeros((rows, 64), bf16).at[0, : packed.shape[0]].set(packed)
    message = jnp.concatenate([piece, tail], axis=1)
    factors = across_chips(jnp.broadcast_to(message, (chips,) + message.shape))
    infos = factors[:, 0, width : width + packed.shape[0]].astype(f32)
    infos = infos.reshape(chips, 4, 2 * completions)
    all_rewards = (infos[:, 0] + infos[:, 1] + infos[:, 2]).reshape(-1)
    all_groups = infos[:, 3].reshape(-1)
    labels = jnp.arange(n_dp * completions // GROUPS_PER_COMPLETION, dtype=f32)
    member = (all_groups[:, None] == labels[None, :]).astype(f32)
    group_mean = jnp.sum(member * all_rewards[:, None], axis=0) / jnp.maximum(
        jnp.sum(member, axis=0), 1.0
    )
    mine = (info[1][:, None] == labels[None, :]).astype(f32)
    advantage = info[0] - jnp.sum(mine * group_mean[None, :], axis=1)
    factors = factors.reshape(chips * rows, -1)

    token_arrays = [in_hbm(act), far_act, in_hbm(cot), far_cot]
    token_scratch = [pltpu.VMEM((4, width, tokens), bf16), pltpu.SemaphoreType.DMA((4,))]
    parts = local_call(
        project_kernel,
        "project",
        scalars,
        [factors],
        token_arrays,
        (n_tensor, 2 * R, 2 * tokens),
        token_scratch[:1]
        + [pltpu.VMEM((2 * R, 2 * tokens), bf16)]
        + token_scratch[1:]
        + [pltpu.SemaphoreType.DMA((2, n_tensor))],
    )
    parts = across_tensor(parts)
    grads = local_call(
        grad_kernel,
        "grads",
        scalars + [advantage],
        [parts],
        token_arrays,
        (2 * R, width),
        token_scratch,
        by_copy=False,
    )
    arrived = across_chips(grads.reshape(chips, rows, width))
    step = jnp.where(chip * rows < R, rate_a * D**-0.5, rate_b * R**-0.5)
    fresh = (piece.astype(f32) - step * jnp.sum(arrived.astype(f32), axis=0)).astype(bf16)
    fresh = across_chips(jnp.broadcast_to(fresh, (chips, rows, width)))
    fresh = fresh.reshape(chips * rows, width)

    ranks = layer_call(
        decode_kernel,
        "decode_rank",
        core,
        [fresh],
        [(decode_in, 1), (far_dec, 1)],
        jax.ShapeDtypeStruct((n_tensor, 2, R, steps * rows_dev), bf16),
    )
    far_fresh = core_swap(fresh)
    ranks = lax.all_to_all(
        ranks.reshape(n_tensor * 2, R, steps * rows_dev),
        ("dp", "tensor"),
        0,
        0,
        axis_index_groups=[
            [(pair * 2 + c) * n_tensor + t for t in range(n_tensor) for c in range(2)]
            for pair in range(chips)
        ],
    ).reshape(n_tensor, 2, R, steps * rows_dev)

    column = jnp.arange(lanes)[None, None, :]
    step_of = jnp.arange(steps)[None, :, None]
    valid = column < lengths[:, None, None]
    valid = valid | ((column >= slots) & (column <= slots + step_of))
    return attend(
        core,
        ranks,
        fresh,
        far_fresh,
        in_hbm(frozen_query_part),
        in_hbm(kv_cache.reshape(layers, rows_dev, slots, lanes)),
        new_kv.reshape(steps, layers, rows_dev, lanes),
        valid.astype(f32),
    )


def solution(mesh):
    return jax.shard_map(
        shards,
        mesh=mesh,
        in_specs=(
            P(None, "dp", "tensor"),
            P(None, "dp", "tensor"),
            P("dp"),
            P("dp"),
            P(),
            P("dp", None, None, "tensor"),
            P("dp", None, None, "tensor"),
            P(None, None, "dp", "tensor"),
            P(None, None, "dp", "tensor"),
            P(None, "dp", "tensor", None, None),
            P(None, None, "dp", "tensor", None),
            P("dp"),
        ),
        out_specs=(P(None, None, "tensor"), P(None, None, "tensor"), P(None, None, "dp", "tensor")),
        check_vma=False,
    )
```

time: 157 us -> 148 us (0.943)
  blocking collectives: 0 us -> 20 us
  waiting for transfers between devices: 71.5 us -> 58 us
  starting transfers between devices: 51.2 us -> 41.3 us
  other arithmetic: 6.8 us -> 1.61 us
  Pallas kernels: 16.5 us -> 20 us
  local copies, waits for them, and re-layouts: 6.09 us -> 2.77 us
    all_to_all x4 -> x3, waiting for transfers between devices: 53.4 us -> 30.1 us  [across_chips(): return lax.all_to_all(x, 'dp', 0, 0, axis_index_groups=same_core)]
    all_to_all x0 -> x1, blocking collectives: none -> 20 us  [across_chips(): return lax.all_to_all(x, 'dp', 0, 0, axis_index_groups=same_core)]
    pallas_call x1 -> x4, Pallas kernels: 9.01 us -> 18.8 us  [the longest x3 10.2 us: local_call(): pl.pallas_call(kernel, grid_spec=pltpu.PrefetchScalarGridSpec(num_scalar_...]
    all_to_all x0 -> x1, waiting for transfers between devices: none -> 7.02 us  [shards(): lax.all_to_all(ranks.reshape(n_tensor * 2, R, steps * rows_dev), ('dp', '...]
    pallas_call x3 -> x1, Pallas kernels: 7.5 us -> 1.19 us  [layer_call(): pl.pallas_call(kernel, grid_spec=pltpu.PrefetchScalarGridSpec(num_scalar_...]
    all_to_all x4 -> x3, starting transfers between devices: 30 us -> 23.8 us  [across_chips(): return lax.all_to_all(x, 'dp', 0, 0, axis_index_groups=same_core)]
    ppermute x8 -> x7, waiting for transfers between devices: 0.84 us -> 6.9 us  [core_swap(): return lax.ppermute(x, 'dp', swap)]
    ppermute x8 -> x7, starting transfers between devices: 13.7 us -> 9.96 us  [core_swap(): return lax.ppermute(x, 'dp', swap)]
  transfers between devices with their start and end apart: 14 -> 12, of which waited for: 7 -> 8; matrix products, arithmetic and copies ran while one was open for 4% -> 1% of each run, Pallas kernels for 0% -> 1%
where the time goes in v3:
time: 148 us; the launch traced here: 147 us
  waiting for transfers between devices  58 us (39%)
  starting transfers between devices  41.3 us (28%)
  Pallas kernels  20 us (14%)
  blocking collectives  20 us (14%)
  between operations  3.45 us (2%)
  local copies, waits for them, and re-layouts  2.77 us (2%)
  other arithmetic  1.61 us (1%)
    all_to_all x3, waiting for transfers between devices, across_chips(): return lax.all_to_all(x, 'dp', 0, 0, axis_index_groups=same_core)  30.1 us
    all_to_all x3, starting transfers between devices, across_chips(): return lax.all_to_all(x, 'dp', 0, 0, axis_index_groups=same_core)  23.8 us
    all_to_all x1, blocking collectives, across_chips(): return lax.all_to_all(x, 'dp', 0, 0, axis_index_groups=same_core)  20 us
    all_to_all x1, waiting for transfers between devices, across_tensor(): return lax.all_to_all(x, 'tensor', 0, 0)  14.1 us
    pallas_call x3, Pallas kernels, local_call(): pl.pallas_call(kernel, grid_spec=pltpu.PrefetchScalarGridSpec(num_scalar_...  10.2 us
    ppermute x7, starting transfers between devices, core_swap(): return lax.ppermute(x, 'dp', swap)  9.96 us
    pallas_call x1, Pallas kernels, attend(): pl.pallas_call(attend_kernel, grid_spec=pltpu.PrefetchScalarGridSpec(num_...  8.62 us
    all_to_all x1, waiting for transfers between devices, shards(): lax.all_to_all(ranks.reshape(n_tensor * 2, R, steps * rows_dev), ('dp', '...  7.02 us
  transfers between devices with their start and end apart: 12, of which 8 were waited for; matrix products, arithmetic and copies ran while one was open for 1% of the time, Pallas kernels for 1%

profile of v3, /device:TPU:1, one launch (start us, length us, event | category | flops | bytes accessed | tf_op | source)
XLA Modules:
  0.0 147.2 jit_solution(9789927825623537318)
XLA Ops:
  0.7 3.3 %collective-permute-start = (bf16[1,2,64,1856]{3,2,1,0:T(8,128)(2,1)}, bf16[1,2,64,1856]{3,2,1,0:T(8,128)(2,1)S(1)}, u32[]{:S(2)}, u32[]{:S(2)}) collective-permute-start(bf16[1,2,64,1856]{3,2,1,0:T(8,128)(2,1)} %own_a.1), channel_id=1, source_target_pairs={{0,8},{8,0},{16,24},{24,16},{32,40},{40,32},{48,56},{56,48},{64,72... | collective-permute-start | bytes 1425416 | tf_op jit(solution)/shard_map/ppermute | solution.py:325
  4.0 0.1 collective-permute-start.1
  4.1 1.6 %collective-permute-done.far_a = bf16[1,2,64,1856]{3,2,1,0:T(8,128)(2,1)S(1)} collective-permute-done((bf16[1,2,64,1856]{3,2,1,0:T(8,128)(2,1)}, bf16[1,2,64,1856]{3,2,1,0:T(8,128)(2,1)S(1)}, u32[]{:S(2)}, u32[]{:S(2)}) %collective-permute-start) | collective-permute-done | bytes 475168 | tf_op jit(solution)/shard_map/ppermute | solution.py:325
  5.7 0.7 collective-permute-done.1.far_b
  6.4 2.1 %message.1 = bf16[128,1856]{1,0:T(8,128)(2,1)} custom-call(s32[1]{0:T(128)} %bitcast.core, s32[2]{0:T(128)} %owner.1, bf16[1,2,64,1856]{3,2,1,0:T(8,128)(2,1)} %own_a.1, bf16[1,2,64,1856]{3,2,1,0:T(8,128)(2,1)} %own_b.1, bf16[1,2,64,1856]{3,2,1,0:T(8,128)(2,1)S(1)} %collective-permute-done.far_a, bf16[1,2,64,1856]{3,2,1,0:T(8,128)(2,1)S(1)} %collective-permute-done.1.far_b), custom_call_target="tpu_custom_call" | custom-call | tf_op jit(solution)/shard_map/message/pallas_call | solution.py:281
  8.5 9.2 %all-to-all-start = ((bf16[16,8,1856]{2,1,0:T(8,128)(2,1)}), bf16[16,8,1856]{2,1,0:T(8,128)(2,1)S(1)}, u32[]{:S(2)}, u32[]{:S(2)}) async-start(bf16[16,8,1856]{2,1,0:T(8,128)(2,1)} %bitcast.44), calls=%async_computation | async-start | bytes 983040 | tf_op jit(solution)/shard_map/all_to_all | solution.py:328
  17.7 0.6 dynamic_slice.8
  20.9 1.1 collective-permute-start.3
  22.0 0.1 collective-permute-start.4
  22.1 0.5 collective-permute-start.2
  22.6 4.6 %collective-permute-done.2 = f32[2,2]{1,0:T(2,128)S(1)} collective-permute-done((f32[2,2]{1,0:T(2,128)S(1)}, f32[2,2]{1,0:T(2,128)S(1)}, u32[]{:S(2)}, u32[]{:S(2)}) %collective-permute-start.2) | collective-permute-done | bytes 48 | tf_op jit(solution)/shard_map/ppermute | solution.py:325
  27.2 0.1 pad_maximum_fusion.2
  27.3 0.1 fusion.8
  27.4 4.4 %all-to-all-done = bf16[16,8,1856]{2,1,0:T(8,128)(2,1)S(1)} async-done(((bf16[16,8,1856]{2,1,0:T(8,128)(2,1)}), bf16[16,8,1856]{2,1,0:T(8,128)(2,1)S(1)}, u32[]{:S(2)}, u32[]{:S(2)}) %all-to-all-start) | async-done | bytes 475168 | tf_op jit(solution)/shard_map/all_to_all | solution.py:328
  31.8 0.8 copy-done.2
  32.6 0.1 pad_maximum_fusion
  32.7 20.0 %all_to_all.30 = bf16[16,8,1920]{2,1,0:T(8,128)(2,1)S(1)} all-to-all(bf16[16,8,1920]{2,1,0:T(8,128)(2,1)S(1)} %broadcast_in_dim.4), channel_id=1, replica_groups={{0,16,32,48,64,80,96,112,128,144,160,176,192,208,224,240},{8,24,40,56,7..., dimensions={0} | all-to-all | bytes 983040 | tf_op jit(solution)/shard_map/all_to_all | solution.py:328
  52.7 0.0 collective-permute-done.3.far_act
  52.7 3.9 %project.1 = bf16[8,128,512]{2,1,0:T(8,128)(2,1)} custom-call(s32[1]{0:T(128)} %bitcast.core, bf16[128,1920]{1,0:T(8,128)(2,1)S(1)} %bitcast.34, bf16[2,1856,256]{2,1,0:T(8,128)(2,1)} %bitcast.38, bf16[2,1856,256]{2,1,0:T(8,128)(2,1)S(1)} %collective-permute-done.3.far_act, bf16[2,1856,256]{2,1,0:T(8,128)(2,1)} %bitcast.41, ...), custom_call_target="tpu_custom_call" | custom-call | tf_op jit(solution)/shard_map/project/pallas_call | solution.py:281
  56.6 4.1 %all-to-all-start.2 = ((bf16[8,128,512]{2,1,0:T(8,128)(2,1)}), bf16[8,128,512]{2,1,0:T(8,128)(2,1)S(1)}, u32[]{:S(2)}, u32[]{:S(2)}) async-start(bf16[8,128,512]{2,1,0:T(8,128)(2,1)} %project.1), calls=%async_computation.2 | async-start | bytes 2097152 | tf_op jit(solution)/shard_map/all_to_all | solution.py:331
  60.7 0.1 slice.46
  60.8 0.1 copy.24
  60.9 0.1 copy.22
  61.0 0.1 eq.36
  61.1 0.1 copy.23
  61.2 0.1 add.49
  61.3 0.1 convert_reduce_fusion.1
  61.4 0.2 select_reduce_fusion.1
  61.6 14.1 %all-to-all-done.2.parts = bf16[8,128,512]{2,1,0:T(8,128)(2,1)S(1)} async-done(((bf16[8,128,512]{2,1,0:T(8,128)(2,1)}), bf16[8,128,512]{2,1,0:T(8,128)(2,1)S(1)}, u32[]{:S(2)}, u32[]{:S(2)}) %all-to-all-start.2) | async-done | bytes 1048608 | tf_op jit(solution)/shard_map/all_to_all | solution.py:331
  75.7 4.2 %grads.1 = bf16[128,1856]{1,0:T(8,128)(2,1)} custom-call(s32[1]{0:T(128)} %bitcast.core, f32[4]{0:T(128)S(1)} %bitcast_subtract_fusion.advantage, bf16[8,128,512]{2,1,0:T(8,128)(2,1)S(1)} %all-to-all-done.2.parts, bf16[2,1856,256]{2,1,0:T(8,128)(2,1)} %bitcast.39, bf16[2,1856,256]{2,1,0:T(8,128)(2,1)S(1)} %collective-permute-done.3.far_act, ...), custom_call_target="tpu_custom_call" | custom-call | tf_op jit(solution)/shard_map/grads/pallas_call | solution.py:281
  79.9 0.0 copy-start
  79.9 0.0 copy-start.5
  79.9 8.0 %all-to-all-start.3 = ((bf16[16,8,1856]{2,1,0:T(8,128)(2,1)}), bf16[16,8,1856]{2,1,0:T(8,128)(2,1)S(1)}, u32[]{:S(2)}, u32[]{:S(2)}) async-start(bf16[16,8,1856]{2,1,0:T(8,128)(2,1)} %bitcast.45), calls=%async_computation.3 | async-start | bytes 983040 | tf_op jit(solution)/shard_map/all_to_all | solution.py:328
  87.9 13.7 %all-to-all-done.3 = bf16[16,8,1856]{2,1,0:T(8,128)(2,1)S(1)} async-done(((bf16[16,8,1856]{2,1,0:T(8,128)(2,1)}), bf16[16,8,1856]{2,1,0:T(8,128)(2,1)S(1)}, u32[]{:S(2)}, u32[]{:S(2)}) %all-to-all-start.3) | async-done | bytes 475168 | tf_op jit(solution)/shard_map/all_to_all | solution.py:328
  101.6 0.1 convert_reduce_fusion
  101.7 0.8 subtract_convert_fusion
  102.5 0.8 broadcast_in_dim.5
  103.3 6.6 %all-to-all-start.4 = ((bf16[16,8,1856]{2,1,0:T(8,128)(2,1)}), bf16[16,8,1856]{2,1,0:T(8,128)(2,1)S(1)}, u32[]{:S(2)}, u32[]{:S(2)}) async-start(bf16[16,8,1856]{2,1,0:T(8,128)(2,1)} %broadcast_in_dim.5), calls=%async_computation.4 | async-start | bytes 983040 | tf_op jit(solution)/shard_map/all_to_all | solution.py:328
  109.9 0.0 copy-start.1
  109.9 1.8 %collective-permute-start.5 = (bf16[2,2,64,1856]{3,2,1,0:T(8,128)(2,1)S(1)}, bf16[2,2,64,1856]{3,2,1,0:T(8,128)(2,1)S(1)}, u32[]{:S(2)}, u32[]{:S(2)}) collective-permute-start(bf16[2,2,64,1856]{3,2,1,0:T(8,128)(2,1)S(1)} %copy-done), channel_id=1, source_target_pairs={{0,8},{8,0},{16,24},{24,16},{32,40},{40,32},{48,56},{56,48},{64,72... | collective-permute-start | bytes 2850824 | tf_op jit(solution)/shard_map/ppermute | solution.py:325
  111.7 0.1 iota_compare_fusion
  111.8 12.0 %all-to-all-done.4 = bf16[16,8,1856]{2,1,0:T(8,128)(2,1)S(1)} async-done(((bf16[16,8,1856]{2,1,0:T(8,128)(2,1)}), bf16[16,8,1856]{2,1,0:T(8,128)(2,1)S(1)}, u32[]{:S(2)}, u32[]{:S(2)}) %all-to-all-start.4) | async-done | bytes 475168 | tf_op jit(solution)/shard_map/all_to_all | solution.py:328
  123.7 3.1 %collective-permute-start.6 = (bf16[128,1856]{1,0:T(8,128)(2,1)S(1)}, bf16[128,1856]{1,0:T(8,128)(2,1)S(1)}, u32[]{:S(2)}, u32[]{:S(2)}) collective-permute-start(bf16[128,1856]{1,0:T(8,128)(2,1)S(1)} %bitcast.31), channel_id=1, source_target_pairs={{0,8},{8,0},{16,24},{24,16},{32,40},{40,32},{48,56},{56,48},{64,72... | collective-permute-start | bytes 1425416 | tf_op jit(solution)/shard_map/ppermute | solution.py:325
  126.8 1.2 decode_rank.1
  128.0 3.4 %all-to-all-start.5 = ((bf16[16,64,128]{2,1,0:T(8,128)(2,1)}), bf16[16,64,128]{2,1,0:T(8,128)(2,1)S(1)}, u32[]{:S(2)}, u32[]{:S(2)}) async-start(bf16[16,64,128]{2,1,0:T(8,128)(2,1)} %bitcast.46), calls=%async_computation.5 | async-start | bytes 524288 | tf_op jit(solution)/shard_map/all_to_all | solution.py:425
  131.4 0.1 compare_and_fusion
  131.5 7.0 %all-to-all-done.5 = bf16[16,64,128]{2,1,0:T(8,128)(2,1)S(1)} async-done(((bf16[16,64,128]{2,1,0:T(8,128)(2,1)}), bf16[16,64,128]{2,1,0:T(8,128)(2,1)S(1)}, u32[]{:S(2)}, u32[]{:S(2)}) %all-to-all-start.5) | async-done | bytes 262176 | tf_op jit(solution)/shard_map/all_to_all | solution.py:425
  138.6 8.6 %attend.1 = (bf16[2,64,1856]{2,1,0:T(8,128)(2,1)}, bf16[2,64,1856]{2,1,0:T(8,128)(2,1)}, bf16[2,2,64,1856]{3,2,1,0:T(8,128)(2,1)}) custom-call(s32[1]{0:T(128)} %bitcast.core, bf16[8,2,64,128]{3,2,1,0:T(8,128)(2,1)S(1)} %bitcast.35, bf16[128,1856]{1,0:T(8,128)(2,1)S(1)} %bitcast.33, bf16[128,1856]{1,0:T(8,128)(2,1)S(1)} %collective-permute-done.6.far_fresh, ...), custom_call_target="tpu_custom_call" | custom-call | tf_op jit(solution)/shard_map/attend/pallas_call | solution.py:226
  (27 shorter events, 0.2 us)
Async XLA Ops:
  0.6 17.1 %copy-start.4 = (s32[2]{0:T(128)S(1)}, s32[2]{0:T(128)}, u32[]{:S(2)}) copy-start(s32[2]{0:T(128)} %owner.1) | copy-start | bytes 28
  0.6 21.5 %copy-start.3 = (f32[2]{0:T(128)S(1)}, f32[2]{0:T(128)}, u32[]{:S(2)}) copy-start(f32[2]{0:T(128)} %param.16) | copy-start | bytes 28
  0.7 21.5 %copy-start.6 = (s32[2]{0:T(128)S(1)}, s32[2]{0:T(128)}, u32[]{:S(2)}) copy-start(s32[2]{0:T(128)} %param.17) | copy-start | bytes 28
  0.7 5.0 %collective-permute-start = (bf16[1,2,64,1856]{3,2,1,0:T(8,128)(2,1)}, bf16[1,2,64,1856]{3,2,1,0:T(8,128)(2,1)S(1)}, u32[]{:S(2)}, u32[]{:S(2)}) collective-permute-start(bf16[1,2,64,1856]{3,2,1,0:T(8,128)(2,1)} %own_a.1), channel_id=1, source_target_pairs={{0,8},{8,0},{16,24},{24,16},{32,40},{40,32},{48,56},{56,48},{64,72... | collective-permute-start | bytes 1425416 | tf_op jit(solution)/shard_map/ppermute | solution.py:325
  4.0 2.4 %collective-permute-start.1 = (bf16[1,2,64,1856]{3,2,1,0:T(8,128)(2,1)}, bf16[1,2,64,1856]{3,2,1,0:T(8,128)(2,1)S(1)}, u32[]{:S(2)}, u32[]{:S(2)}) collective-permute-start(bf16[1,2,64,1856]{3,2,1,0:T(8,128)(2,1)} %own_b.1), channel_id=1, source_target_pairs={{0,8},{8,0},{16,24},{24,16},{32,40},{40,32},{48,56},{56,48},{64,72... | collective-permute-start | bytes 1425416 | tf_op jit(solution)/shard_map/ppermute | solution.py:325
  8.5 23.3 %all-to-all-start = ((bf16[16,8,1856]{2,1,0:T(8,128)(2,1)}), bf16[16,8,1856]{2,1,0:T(8,128)(2,1)S(1)}, u32[]{:S(2)}, u32[]{:S(2)}) async-start(bf16[16,8,1856]{2,1,0:T(8,128)(2,1)} %bitcast.44), calls=%async_computation | async-start | bytes 983040 | tf_op jit(solution)/shard_map/all_to_all | solution.py:328
  20.9 31.8 %collective-permute-start.3 = (bf16[2,1856,256]{2,1,0:T(8,128)(2,1)}, bf16[2,1856,256]{2,1,0:T(8,128)(2,1)S(1)}, u32[]{:S(2)}, u32[]{:S(2)}) collective-permute-start(bf16[2,1856,256]{2,1,0:T(8,128)(2,1)} %bitcast.37), channel_id=1, source_target_pairs={{0,8},{8,0},{16,24},{24,16},{32,40},{40,32},{48,56},{56,48},{64,72... | collective-permute-start | bytes 5701640 | tf_op jit(solution)/shard_map/ppermute | solution.py:325
  22.0 30.7 %collective-permute-start.4 = (bf16[2,1856,256]{2,1,0:T(8,128)(2,1)}, bf16[2,1856,256]{2,1,0:T(8,128)(2,1)}, u32[]{:S(2)}, u32[]{:S(2)}) collective-permute-start(bf16[2,1856,256]{2,1,0:T(8,128)(2,1)} %bitcast.40), channel_id=1, source_target_pairs={{0,8},{8,0},{16,24},{24,16},{32,40},{40,32},{48,56},{56,48},{64,72... | collective-permute-start | bytes 5701640 | tf_op jit(solution)/shard_map/ppermute | solution.py:325
  22.1 5.1 %collective-permute-start.2 = (f32[2,2]{1,0:T(2,128)S(1)}, f32[2,2]{1,0:T(2,128)S(1)}, u32[]{:S(2)}, u32[]{:S(2)}) collective-permute-start(f32[2,2]{1,0:T(2,128)S(1)} %pad_maximum_fusion.1), channel_id=1, source_target_pairs={{0,8},{8,0},{16,24},{24,16},{32,40},{40,32},{48,56},{56,48},{64,72... | collective-permute-start | bytes 56 | tf_op jit(solution)/shard_map/ppermute | solution.py:325
  31.8 0.8 copy-start.2
  56.6 19.1 %all-to-all-start.2 = ((bf16[8,128,512]{2,1,0:T(8,128)(2,1)}), bf16[8,128,512]{2,1,0:T(8,128)(2,1)S(1)}, u32[]{:S(2)}, u32[]{:S(2)}) async-start(bf16[8,128,512]{2,1,0:T(8,128)(2,1)} %project.1), calls=%async_computation.2 | async-start | bytes 2097152 | tf_op jit(solution)/shard_map/all_to_all | solution.py:331
  79.9 30.0 %copy-start = (bf16[2,2,64,1856]{3,2,1,0:T(8,128)(2,1)S(1)}, bf16[2,2,64,1856]{3,2,1,0:T(8,128)(2,1)}, u32[]{:S(2)}) copy-start(bf16[2,2,64,1856]{3,2,1,0:T(8,128)(2,1)} %dec.1) | copy-start | bytes 2850820
  79.9 31.8 %copy-start.5 = (s32[64]{0:T(128)S(1)}, s32[64]{0:T(128)}, u32[]{:S(2)}) copy-start(s32[64]{0:T(128)} %param.25) | copy-start | bytes 772
  79.9 21.7 %all-to-all-start.3 = ((bf16[16,8,1856]{2,1,0:T(8,128)(2,1)}), bf16[16,8,1856]{2,1,0:T(8,128)(2,1)S(1)}, u32[]{:S(2)}, u32[]{:S(2)}) async-start(bf16[16,8,1856]{2,1,0:T(8,128)(2,1)} %bitcast.45), calls=%async_computation.3 | async-start | bytes 983040 | tf_op jit(solution)/shard_map/all_to_all | solution.py:328
  103.3 20.5 %all-to-all-start.4 = ((bf16[16,8,1856]{2,1,0:T(8,128)(2,1)}), bf16[16,8,1856]{2,1,0:T(8,128)(2,1)S(1)}, u32[]{:S(2)}, u32[]{:S(2)}) async-start(bf16[16,8,1856]{2,1,0:T(8,128)(2,1)} %broadcast_in_dim.5), calls=%async_computation.4 | async-start | bytes 983040 | tf_op jit(solution)/shard_map/all_to_all | solution.py:328
  109.9 28.7 %copy-start.1 = (bf16[2,2,64,1,128]{4,2,3,1,0:T(8,128)(2,1)S(1)}, bf16[2,2,64,1,128]{4,2,3,1,0:T(8,128)(2,1)}, u32[]{:S(2)}) copy-start(bf16[2,2,64,1,128]{4,2,3,1,0:T(8,128)(2,1)} %param.24) | copy-start | bytes 196612
  109.9 16.9 %collective-permute-start.5 = (bf16[2,2,64,1856]{3,2,1,0:T(8,128)(2,1)S(1)}, bf16[2,2,64,1856]{3,2,1,0:T(8,128)(2,1)S(1)}, u32[]{:S(2)}, u32[]{:S(2)}) collective-permute-start(bf16[2,2,64,1856]{3,2,1,0:T(8,128)(2,1)S(1)} %copy-done), channel_id=1, source_target_pairs={{0,8},{8,0},{16,24},{24,16},{32,40},{40,32},{48,56},{56,48},{64,72... | collective-permute-start | bytes 2850824 | tf_op jit(solution)/shard_map/ppermute | solution.py:325
  123.7 14.8 %collective-permute-start.6 = (bf16[128,1856]{1,0:T(8,128)(2,1)S(1)}, bf16[128,1856]{1,0:T(8,128)(2,1)S(1)}, u32[]{:S(2)}, u32[]{:S(2)}) collective-permute-start(bf16[128,1856]{1,0:T(8,128)(2,1)S(1)} %bitcast.31), channel_id=1, source_target_pairs={{0,8},{8,0},{16,24},{24,16},{32,40},{40,32},{48,56},{56,48},{64,72... | collective-permute-start | bytes 1425416 | tf_op jit(solution)/shard_map/ppermute | solution.py:325
  128.0 10.6 %all-to-all-start.5 = ((bf16[16,64,128]{2,1,0:T(8,128)(2,1)}), bf16[16,64,128]{2,1,0:T(8,128)(2,1)S(1)}, u32[]{:S(2)}, u32[]{:S(2)}) async-start(bf16[16,64,128]{2,1,0:T(8,128)(2,1)} %bitcast.46), calls=%async_computation.5 | async-start | bytes 524288 | tf_op jit(solution)/shard_map/all_to_all | solution.py:425

commit v4 on v3

--- a/solution.py
+++ b/solution.py
@@ -7,7 +7,8 @@
 
 D = 14848
 R = 64
-GROUPS_PER_COMPLETION = 4
+ROWS = 8
+TAIL = D // 8 % 128
 VMEM_BYTES = 32 * 1024 * 1024
 
 rate_a = 0.5
@@ -84,10 +85,35 @@
     )
 
 
-def project_kernel(core, factors, act, far_act, cot, far_cot, out, held, part, sems, out_sems):
+def token_advantage(info, tails, count, tokens):
+    lanes = tails.shape[1]
+
+    def lane_shifted(x, by):
+        return pltpu.roll(x, lanes - by, 1)
+
+    rewards = tails + lane_shifted(tails, count) + lane_shifted(tails, 2 * count)
+    groups = lane_shifted(tails, 3 * count)
+    row = lax.broadcasted_iota(jnp.int32, tails.shape, 0)
+    lane = lax.broadcasted_iota(jnp.int32, tails.shape, 1)
+    used = (row % ROWS == 0) & (lane >= TAIL) & (lane < TAIL + count)
+    sequence = lax.broadcasted_iota(jnp.int32, (1, tokens), 1) // (tokens // count)
+    adv = jnp.zeros(sequence.shape, f32)
+    for i in range(count):
+        same = used & (groups == info[count + i])
+        total = jnp.sum(jnp.where(same, rewards, 0.0), keepdims=True)
+        members = jnp.sum(jnp.where(same, 1.0, 0.0), keepdims=True)
+        adv = jnp.where(sequence == i, info[i] - total / jnp.maximum(members, 1.0), adv)
+    return adv
+
+
+def project_kernel(
+    core, info, factors, act, far_act, cot, far_cot, out, adv, held, part, sems, out_sems
+):
     r = factors.shape[0] // 2
     _, width, tokens = held.shape
     arriving = load_tokens(core, (act, far_act, cot, far_cot), held, sems)
+    tails = factors[:, width // 128 * 128 :].astype(f32)
+    adv[...] = token_advantage(info, tails, info.shape[0] // 2, 2 * tokens)
     leaving = []
     for half in range(2):
         rows = pl.ds(half * r, r)
@@ -107,15 +133,11 @@
         copy.wait()
 
 
-def grad_kernel(core, advantage, parts, act, far_act, cot, far_cot, out, held, sems):
+def grad_kernel(core, parts, adv_ref, act, far_act, cot, far_cot, out, held, sems):
     r = parts.shape[1] // 2
     _, width, tokens = held.shape
     arriving = load_tokens(core, (act, far_act, cot, far_cot), held, sems)
-    count = advantage.shape[0]
-    sequence = lax.broadcasted_iota(jnp.int32, (1, 2 * tokens), 1) // (2 * tokens // count)
-    adv = jnp.zeros(sequence.shape, f32)
-    for i in range(count):
-        adv = jnp.where(sequence == i, advantage[i], adv)
+    adv = adv_ref[...]
     total = jnp.sum(parts[...].astype(f32), axis=0)
     low = (total[:r] * D**-0.5).astype(bf16).astype(f32)
     low = (low * adv).astype(bf16)
@@ -128,11 +150,19 @@
         out[half * r : (half + 1) * r] = grad.astype(bf16)
 
 
+def update_kernel(chip, arrived, piece, out):
+    total = jnp.sum(arrived[...].astype(f32), axis=0)
+    step = jnp.where(chip[0] * ROWS < R, rate_a * D**-0.5, rate_b * R**-0.5)
+    fresh = (piece[...].astype(f32) - step * total).astype(bf16)
+    for peer in range(out.shape[0]):
+        out[peer] = fresh
+
+
 def decode_kernel(core, fresh, dec, far_dec, out):
-    steps, _, rows, width = dec.shape
+    steps, rows, width = dec.shape
     mine, other = core[0], 1 - core[0]
     for place, source in ((mine, dec), (other, far_dec)):
-        part = nt_dot(fresh[: out.shape[2]], source[:, 0].reshape(steps * rows, width)).astype(bf16)
+        part = nt_dot(fresh[: out.shape[2]], source[...].reshape(steps * rows, width)).astype(bf16)
         for peer in range(out.shape[0]):
             out[peer, place] = part
 
@@ -250,34 +280,11 @@
     )(core.reshape(1), ranks, fresh, far_fresh, frozen, kv, new_kv, valid)
 
 
-def layer_call(kernel, name, core, arrays, layered, out):
-    def whole(x):
-        return pl.BlockSpec(x.shape, lambda i, c, n=len(x.shape): (0,) * n)
-
-    def layer(x, axis):
-        shape = tuple(1 if d == axis else n for d, n in enumerate(x.shape))
-        return pl.BlockSpec(
-            shape, lambda i, c, n=x.ndim: tuple(c[0] if d == axis else 0 for d in range(n))
-        )
-
-    return pl.pallas_call(
-        kernel,
-        grid_spec=pltpu.PrefetchScalarGridSpec(
-            num_scalar_prefetch=1,
-            grid=(1,),
-            in_specs=[whole(x) for x in arrays] + [layer(x, axis) for x, axis in layered],
-            out_specs=whole(out),
-        ),
-        out_shape=pltpu.HBM(out.shape, out.dtype),
-        compiler_params=pltpu.CompilerParams(vmem_limit_bytes=VMEM_BYTES),
-        name=name,
-    )(core.reshape(1), *arrays, *[x for x, _ in layered])
-
-
-def local_call(kernel, name, scalars, whole, streamed, out, scratch, by_copy=True):
+def local_call(kernel, name, scalars, whole, streamed, out, scratch, by_copy=True, beside=None):
     def block(shape):
         return pl.BlockSpec(shape, lambda i, *_: (0,) * len(shape))
 
+    out_spec = pl.BlockSpec(memory_space=pl.ANY) if by_copy else block(out)
     return pl.pallas_call(
         kernel,
         grid_spec=pltpu.PrefetchScalarGridSpec(
@@ -285,10 +292,10 @@
             grid=(1,),
             in_specs=[block(x.shape) for x in whole]
             + [pl.BlockSpec(memory_space=pl.ANY)] * len(streamed),
-            out_specs=pl.BlockSpec(memory_space=pl.ANY) if by_copy else block(out),
+            out_specs=(out_spec, block(beside.shape)) if beside else out_spec,
             scratch_shapes=scratch,
         ),
-        out_shape=pltpu.HBM(out, bf16),
+        out_shape=(pltpu.HBM(out, bf16), beside) if beside else pltpu.HBM(out, bf16),
         compiler_params=pltpu.CompilerParams(vmem_limit_bytes=VMEM_BYTES),
         name=name,
     )(*scalars, *whole, *streamed)
@@ -342,11 +349,12 @@
         (2 * R, width),
         [pltpu.VMEM((2 * R, width), bf16), pltpu.SemaphoreType.DMA((4,))],
     )
-    rows = candidate.shape[0] // chips
-
-    message, act_out, cot_out, dec_out, rewards, group_of = lax.optimization_barrier(
+    rows = ROWS
+
+    message, layer_owner, act_out, cot_out, dec_out, rewards, group_of = lax.optimization_barrier(
         (
             candidate.reshape(chips, rows, width),
+            layer_owner,
             activations,
             cotangent,
             decode_in,
@@ -361,33 +369,33 @@
     far_info = core_swap(own_info)
     far_act = core_swap(jnp.swapaxes(act_out, 1, 2))
     far_cot = core_swap(jnp.swapaxes(cot_out, 1, 2))
-    far_dec = core_swap(dec_out)
-    piece = pick(arrived, pick(layer_owner, core) // 2)
-
+    dec = pick(dec_out, core, 1)
+    far_dec = core_swap(pick(dec_out, 1 - core, 1))
+    column = jnp.arange(lanes)[None, None, :]
+    step_of = jnp.arange(steps)[None, :, None]
+    valid = column < lengths[:, None, None]
+    valid = valid | ((column >= slots) & (column <= slots + step_of))
     info = jnp.concatenate([own_info, far_info], axis=1)
     packed = jnp.concatenate([*split3(info[0]), info[1]]).astype(bf16)
     tail = jnp.zeros((rows, 64), bf16).at[0, : packed.shape[0]].set(packed)
+    owner_chip = pick(layer_owner, core) // 2
+    arrived, owner_chip, tail, info, valid, dec, far_dec, far_act, far_cot = (
+        lax.optimization_barrier(
+            (arrived, owner_chip, tail, info, valid.astype(f32), dec, far_dec, far_act, far_cot)
+        )
+    )
+    piece = pick(arrived, owner_chip)
+
     message = jnp.concatenate([piece, tail], axis=1)
     factors = across_chips(jnp.broadcast_to(message, (chips,) + message.shape))
-    infos = factors[:, 0, width : width + packed.shape[0]].astype(f32)
-    infos = infos.reshape(chips, 4, 2 * completions)
-    all_rewards = (infos[:, 0] + infos[:, 1] + infos[:, 2]).reshape(-1)
-    all_groups = infos[:, 3].reshape(-1)
-    labels = jnp.arange(n_dp * completions // GROUPS_PER_COMPLETION, dtype=f32)
-    member = (all_groups[:, None] == labels[None, :]).astype(f32)
-    group_mean = jnp.sum(member * all_rewards[:, None], axis=0) / jnp.maximum(
-        jnp.sum(member, axis=0), 1.0
-    )
-    mine = (info[1][:, None] == labels[None, :]).astype(f32)
-    advantage = info[0] - jnp.sum(mine * group_mean[None, :], axis=1)
     factors = factors.reshape(chips * rows, -1)
 
-    token_arrays = [in_hbm(act), far_act, in_hbm(cot), far_cot]
+    token_arrays = [act, far_act, in_hbm(cot), far_cot]
     token_scratch = [pltpu.VMEM((4, width, tokens), bf16), pltpu.SemaphoreType.DMA((4,))]
-    parts = local_call(
+    parts, advantage = local_call(
         project_kernel,
         "project",
-        scalars,
+        scalars + [info.reshape(-1)],
         [factors],
         token_arrays,
         (n_tensor, 2 * R, 2 * tokens),
@@ -395,31 +403,42 @@
         + [pltpu.VMEM((2 * R, 2 * tokens), bf16)]
         + token_scratch[1:]
         + [pltpu.SemaphoreType.DMA((2, n_tensor))],
+        beside=jax.ShapeDtypeStruct((1, 2 * tokens), f32),
     )
     parts = across_tensor(parts)
     grads = local_call(
         grad_kernel,
         "grads",
-        scalars + [advantage],
-        [parts],
+        scalars,
+        [parts, advantage],
         token_arrays,
         (2 * R, width),
         token_scratch,
         by_copy=False,
     )
     arrived = across_chips(grads.reshape(chips, rows, width))
-    step = jnp.where(chip * rows < R, rate_a * D**-0.5, rate_b * R**-0.5)
-    fresh = (piece.astype(f32) - step * jnp.sum(arrived.astype(f32), axis=0)).astype(bf16)
-    fresh = across_chips(jnp.broadcast_to(fresh, (chips, rows, width)))
+    fresh = local_call(
+        update_kernel,
+        "update",
+        [chip.reshape(1)],
+        [arrived, piece],
+        [],
+        (chips, rows, width),
+        [],
+        by_copy=False,
+    )
+    fresh = across_chips(fresh)
     fresh = fresh.reshape(chips * rows, width)
 
-    ranks = layer_call(
+    ranks = local_call(
         decode_kernel,
         "decode_rank",
-        core,
-        [fresh],
-        [(decode_in, 1), (far_dec, 1)],
-        jax.ShapeDtypeStruct((n_tensor, 2, R, steps * rows_dev), bf16),
+        scalars,
+        [fresh, dec, far_dec],
+        [],
+        (n_tensor, 2, R, steps * rows_dev),
+        [],
+        by_copy=False,
     )
     far_fresh = core_swap(fresh)
     ranks = lax.all_to_all(
@@ -433,10 +452,6 @@
         ],
     ).reshape(n_tensor, 2, R, steps * rows_dev)
 
-    column = jnp.arange(lanes)[None, None, :]
-    step_of = jnp.arange(steps)[None, :, None]
-    valid = column < lengths[:, None, None]
-    valid = valid | ((column >= slots) & (column <= slots + step_of))
     return attend(
         core,
         ranks,
@@ -445,7 +460,7 @@
         in_hbm(frozen_query_part),
         in_hbm(kv_cache.reshape(layers, rows_dev, slots, lanes)),
         new_kv.reshape(steps, layers, rows_dev, lanes),
-        valid.astype(f32),
+        valid,
     )
 
 

time: 148 us -> 148 us (level)
  blocking collectives: 20 us -> 46.9 us
  waiting for transfers between devices: 58 us -> 37.8 us
  starting transfers between devices: 41.3 us -> 33.7 us
    all_to_all x0 -> x2, blocking collectives: none -> 26.7 us  [the longest x1 16.1 us: across_tensor(): return lax.all_to_all(x, 'tensor', 0, 0)]
    all_to_all x2 -> x0, waiting for transfers between devices: 21.1 us -> none  [the longest x1 14.1 us: across_tensor(): return lax.all_to_all(x, 'tensor', 0, 0)]
    all_to_all x2 -> x0, starting transfers between devices: 7.57 us -> none  [the longest x1 4.14 us: across_tensor(): return lax.all_to_all(x, 'tensor', 0, 0)]
    all_to_all x3, waiting for transfers between devices: 30.1 us -> 34.4 us  [across_chips(): return lax.all_to_all(x, 'dp', 0, 0, axis_index_groups=same_core)]
    ppermute x7, waiting for transfers between devices: 6.9 us -> 3.43 us  [core_swap(): return lax.ppermute(x, 'dp', swap)]
    pallas_call x3 -> x5, Pallas kernels: 10.2 us -> 12.3 us  [local_call(): pl.pallas_call(kernel, grid_spec=pltpu.PrefetchScalarGridSpec(num_scalar_...]
    squeeze x1 -> x2, local copies, waits for them, and re-layouts: 0.01 us -> 2.04 us  [pick(): return lax.dynamic_index_in_dim(array, index, axis, keepdims=False)]
    ppermute x7, starting transfers between devices: 9.96 us -> 8 us  [core_swap(): return lax.ppermute(x, 'dp', swap)]
  transfers between devices with their start and end apart: 12 -> 10, of which waited for: 8 -> 6; matrix products, arithmetic and copies ran while one was open for 1% -> 2% of each run, Pallas kernels for 1% -> 1%
where the time goes in v4:
time: 148 us; the launch traced here: 147 us
  blocking collectives  46.9 us (32%)
  waiting for transfers between devices  37.8 us (26%)
  starting transfers between devices  33.7 us (23%)
  Pallas kernels  20.9 us (14%)
  local copies, waits for them, and re-layouts  3.57 us (2%)
  between operations  3.38 us (2%)
    all_to_all x3, waiting for transfers between devices, across_chips(): return lax.all_to_all(x, 'dp', 0, 0, axis_index_groups=same_core)  34.4 us
    all_to_all x3, starting transfers between devices, across_chips(): return lax.all_to_all(x, 'dp', 0, 0, axis_index_groups=same_core)  25.7 us
    all_to_all x1, blocking collectives, across_chips(): return lax.all_to_all(x, 'dp', 0, 0, axis_index_groups=same_core)  20.2 us
    all_to_all x1, blocking collectives, across_tensor(): return lax.all_to_all(x, 'tensor', 0, 0)  16.1 us
    pallas_call x5, Pallas kernels, local_call(): pl.pallas_call(kernel, grid_spec=pltpu.PrefetchScalarGridSpec(num_scalar_...  12.3 us
    all_to_all x1, blocking collectives, shards(): lax.all_to_all(ranks.reshape(n_tensor * 2, R, steps * rows_dev), ('dp', '...  10.5 us
    pallas_call x1, Pallas kernels, attend(): pl.pallas_call(attend_kernel, grid_spec=pltpu.PrefetchScalarGridSpec(num_...  8.61 us
    ppermute x7, starting transfers between devices, core_swap(): return lax.ppermute(x, 'dp', swap)  8 us
  transfers between devices with their start and end apart: 10, of which 6 were waited for; matrix products, arithmetic and copies ran while one was open for 2% of the time, Pallas kernels for 1%

profile of v4, /device:TPU:1, one launch (start us, length us, event | category | flops | bytes accessed | tf_op | source)
XLA Modules:
  0.0 146.7 jit_solution(15840996711375440135)
XLA Ops:
  0.6 0.0 copy-start
  0.6 0.0 copy-start.4
  0.7 3.3 %collective-permute-start = (bf16[1,2,64,1856]{3,2,1,0:T(8,128)(2,1)}, bf16[1,2,64,1856]{3,2,1,0:T(8,128)(2,1)S(1)}, u32[]{:S(2)}, u32[]{:S(2)}) collective-permute-start(bf16[1,2,64,1856]{3,2,1,0:T(8,128)(2,1)} %own_a.1), channel_id=1, source_target_pairs={{0,8},{8,0},{16,24},{24,16},{32,40},{40,32},{48,56},{56,48},{64,72... | collective-permute-start | bytes 1425416 | tf_op jit(solution)/shard_map/ppermute | solution.py:332
  4.0 0.1 collective-permute-start.1
  4.1 1.6 %collective-permute-done.far_a = bf16[1,2,64,1856]{3,2,1,0:T(8,128)(2,1)S(1)} collective-permute-done((bf16[1,2,64,1856]{3,2,1,0:T(8,128)(2,1)}, bf16[1,2,64,1856]{3,2,1,0:T(8,128)(2,1)S(1)}, u32[]{:S(2)}, u32[]{:S(2)}) %collective-permute-start) | collective-permute-done | bytes 475168 | tf_op jit(solution)/shard_map/ppermute | solution.py:332
  5.7 0.7 collective-permute-done.1.far_b
  6.4 2.1 %message.1 = bf16[128,1856]{1,0:T(8,128)(2,1)} custom-call(s32[1]{0:T(128)} %bitcast.core, s32[2]{0:T(128)} %owner.1, bf16[1,2,64,1856]{3,2,1,0:T(8,128)(2,1)} %own_a.1, bf16[1,2,64,1856]{3,2,1,0:T(8,128)(2,1)} %own_b.1, bf16[1,2,64,1856]{3,2,1,0:T(8,128)(2,1)S(1)} %collective-permute-done.far_a, bf16[1,2,64,1856]{3,2,1,0:T(8,128)(2,1)S(1)} %collective-permute-done.1.far_b), custom_call_target="tpu_custom_call" | custom-call | tf_op jit(solution)/shard_map/message/pallas_call | solution.py:288
  8.5 0.0 copy-start.5
  8.5 0.0 copy-start.2
  8.5 0.0 copy-start.3
  8.6 0.0 copy-done
  8.6 0.5 collective-permute-start.4
  9.0 0.1 collective-permute-start.5
  9.2 0.1 compare_and_fusion
  9.2 0.0 copy-done.4
  9.2 0.1 iota_compare_fusion
  9.4 9.2 %all-to-all-start = ((bf16[16,8,1856]{2,1,0:T(8,128)(2,1)}), bf16[16,8,1856]{2,1,0:T(8,128)(2,1)S(1)}, u32[]{:S(2)}, u32[]{:S(2)}) async-start(bf16[16,8,1856]{2,1,0:T(8,128)(2,1)} %bitcast.37), calls=%async_computation | async-start | bytes 983040 | tf_op jit(solution)/shard_map/all_to_all | solution.py:335
  18.6 2.0 %dynamic-slice_bitcast_fusion = (bf16[2,64,1856]{2,1,0:T(8,128)(2,1)}, bf16[2,64,1856]{2,1,0:T(8,128)(2,1)S(1)}) fusion(bf16[2,2,64,1856]{3,2,1,0:T(8,128)(2,1)} %param.22, s32[]{:T(128)S(6)} %select_n.31, s32[]{:T(128)S(6)} %select_n.29), kind=kLoop, calls=%fused_computation | loop fusion | bytes 1900552 | tf_op jit(solution)/shard_map/jit(dynamic_index_in_dim)/squeeze | solution.py:22
  20.6 0.7 collective-permute-start.3
  21.3 0.0 copy-done.5
  21.3 0.0 copy-done.2
  21.3 0.0 copy-done.3
  21.3 0.6 dynamic_slice.15
  24.5 0.1 collective-permute-start.2
  24.6 1.1 collective-permute-done.2
  25.7 0.1 fusion.14
  25.8 0.1 fusion.8
  25.9 0.0 collective-permute-done.3.far_dec
  25.9 6.9 %all-to-all-done = bf16[16,8,1856]{2,1,0:T(8,128)(2,1)S(1)} async-done(((bf16[16,8,1856]{2,1,0:T(8,128)(2,1)}), bf16[16,8,1856]{2,1,0:T(8,128)(2,1)S(1)}, u32[]{:S(2)}, u32[]{:S(2)}) %all-to-all-start) | async-done | bytes 475168 | tf_op jit(solution)/shard_map/all_to_all | solution.py:335
  32.8 0.0 collective-permute-done.4.far_act
  32.8 0.0 collective-permute-done.5.far_cot
  32.8 0.1 pad_maximum_fusion
  32.9 0.8 broadcast_in_dim.2
  33.7 6.9 %all-to-all-start.1 = ((bf16[16,8,1920]{2,1,0:T(8,128)(2,1)}), bf16[16,8,1920]{2,1,0:T(8,128)(2,1)S(1)}, u32[]{:S(2)}, u32[]{:S(2)}) async-start(bf16[16,8,1920]{2,1,0:T(8,128)(2,1)} %broadcast_in_dim.2), calls=%async_computation.1 | async-start | bytes 983040 | tf_op jit(solution)/shard_map/all_to_all | solution.py:335
  40.5 0.1 reshape.174.info
  40.6 14.1 %all-to-all-done.1 = bf16[16,8,1920]{2,1,0:T(8,128)(2,1)S(1)} async-done(((bf16[16,8,1920]{2,1,0:T(8,128)(2,1)}), bf16[16,8,1920]{2,1,0:T(8,128)(2,1)S(1)}, u32[]{:S(2)}, u32[]{:S(2)}) %all-to-all-start.1) | async-done | bytes 491552 | tf_op jit(solution)/shard_map/all_to_all | solution.py:335
  54.7 4.3 %project.1 = (bf16[8,128,512]{2,1,0:T(8,128)(2,1)}, f32[1,512]{1,0:T(1,128)S(1)}) custom-call(s32[1]{0:T(128)} %bitcast.core, f32[8]{0:T(128)S(1)} %reshape.174.info, bf16[128,1920]{1,0:T(8,128)(2,1)S(1)} %bitcast.30, bf16[2,1856,256]{2,1,0:T(8,128)(2,1)S(1)} %bitcast.25, bf16[2,1856,256]{2,1,0:T(8,128)(2,1)} %collective-permute-done.4.far_act, ...), custom_call_target="tpu_custom_call" | custom-call | tf_op jit(solution)/shard_map/project/pallas_call | solution.py:288
  59.0 16.1 %all_to_all.30.parts = bf16[8,128,512]{2,1,0:T(8,128)(2,1)S(1)} all-to-all(bf16[8,128,512]{2,1,0:T(8,128)(2,1)} %get-tuple-element.46), channel_id=1, replica_groups=mesh['dp'=32,'tensor'=8] {'tensor'}, dimensions={0} | all-to-all | bytes 2097152 | tf_op jit(solution)/shard_map/all_to_all | solution.py:338
  75.1 3.8 %grads.1 = bf16[128,1856]{1,0:T(8,128)(2,1)} custom-call(s32[1]{0:T(128)} %bitcast.core, bf16[8,128,512]{2,1,0:T(8,128)(2,1)S(1)} %all_to_all.30.parts, f32[1,512]{1,0:T(1,128)S(1)} %get-tuple-element.47.adv_ref, bf16[2,1856,256]{2,1,0:T(8,128)(2,1)S(1)} %bitcast.26, bf16[2,1856,256]{2,1,0:T(8,128)(2,1)} %collective-permute-done.4.far_act, ...), custom_call_target="tpu_custom_call" | custom-call | tf_op jit(solution)/shard_map/grads/pallas_call | solution.py:288
  79.0 9.7 %all-to-all-start.3 = ((bf16[16,8,1856]{2,1,0:T(8,128)(2,1)}), bf16[16,8,1856]{2,1,0:T(8,128)(2,1)S(1)}, u32[]{:S(2)}, u32[]{:S(2)}) async-start(bf16[16,8,1856]{2,1,0:T(8,128)(2,1)} %bitcast.38), calls=%async_computation.3 | async-start | bytes 983040 | tf_op jit(solution)/shard_map/all_to_all | solution.py:335
  88.6 13.5 %all-to-all-done.3.arrived = bf16[16,8,1856]{2,1,0:T(8,128)(2,1)S(1)} async-done(((bf16[16,8,1856]{2,1,0:T(8,128)(2,1)}), bf16[16,8,1856]{2,1,0:T(8,128)(2,1)S(1)}, u32[]{:S(2)}, u32[]{:S(2)}) %all-to-all-start.3) | async-done | bytes 475168 | tf_op jit(solution)/shard_map/all_to_all | solution.py:335
  102.1 0.9 update.1
  103.0 20.2 %all_to_all.31 = bf16[16,8,1856]{2,1,0:T(8,128)(2,1)S(1)} all-to-all(bf16[16,8,1856]{2,1,0:T(8,128)(2,1)} %update.1), channel_id=1, replica_groups={{0,16,32,48,64,80,96,112,128,144,160,176,192,208,224,240},{8,24,40,56,7..., dimensions={0} | all-to-all | bytes 950272 | tf_op jit(solution)/shard_map/all_to_all | solution.py:335
  123.1 3.2 %collective-permute-start.6 = (bf16[128,1856]{1,0:T(8,128)(2,1)S(1)}, bf16[128,1856]{1,0:T(8,128)(2,1)S(1)}, u32[]{:S(2)}, u32[]{:S(2)}) collective-permute-start(bf16[128,1856]{1,0:T(8,128)(2,1)S(1)} %bitcast.27), channel_id=1, source_target_pairs={{0,8},{8,0},{16,24},{24,16},{32,40},{40,32},{48,56},{56,48},{64,72... | collective-permute-start | bytes 1425416 | tf_op jit(solution)/shard_map/ppermute | solution.py:332
  126.4 1.2 decode_rank.1
  127.5 10.5 %all_to_all.32 = bf16[16,64,128]{2,1,0:T(8,128)(2,1)S(1)} all-to-all(bf16[16,64,128]{2,1,0:T(8,128)(2,1)} %bitcast.39), channel_id=1, replica_groups={{0,8,1,9,2,10,3,11,4,12,5,13,6,14,7,15},{16,24,17,25,18,26,19,27,20,28,..., dimensions={0} | all-to-all | bytes 524288 | tf_op jit(solution)/shard_map/all_to_all | solution.py:444
  138.1 0.0 collective-permute-done.6.far_fresh
  138.1 8.6 %attend.1 = (bf16[2,64,1856]{2,1,0:T(8,128)(2,1)}, bf16[2,64,1856]{2,1,0:T(8,128)(2,1)}, bf16[2,2,64,1856]{3,2,1,0:T(8,128)(2,1)}) custom-call(s32[1]{0:T(128)} %bitcast.core, bf16[8,2,64,128]{3,2,1,0:T(8,128)(2,1)S(1)} %bitcast.31, bf16[128,1856]{1,0:T(8,128)(2,1)S(1)} %bitcast.29, bf16[128,1856]{1,0:T(8,128)(2,1)S(1)} %collective-permute-done.6.far_fresh, ...), custom_call_target="tpu_custom_call" | custom-call | tf_op jit(solution)/shard_map/attend/pallas_call | solution.py:256
  (10 shorter events, 0.1 us)
Async XLA Ops:
  0.6 7.9 %copy-start = (bf16[2,256,1856]{1,2,0:T(8,128)(2,1)S(1)}, bf16[2,256,1856]{1,2,0:T(8,128)(2,1)}, u32[]{:S(2)}) copy-start(bf16[2,256,1856]{1,2,0:T(8,128)(2,1)} %param.14) | copy-start | bytes 5701636
  0.6 8.6 %copy-start.4 = (s32[64]{0:T(128)S(1)}, s32[64]{0:T(128)}, u32[]{:S(2)}) copy-start(s32[64]{0:T(128)} %param.25) | copy-start | bytes 772
  0.7 5.0 %collective-permute-start = (bf16[1,2,64,1856]{3,2,1,0:T(8,128)(2,1)}, bf16[1,2,64,1856]{3,2,1,0:T(8,128)(2,1)S(1)}, u32[]{:S(2)}, u32[]{:S(2)}) collective-permute-start(bf16[1,2,64,1856]{3,2,1,0:T(8,128)(2,1)} %own_a.1), channel_id=1, source_target_pairs={{0,8},{8,0},{16,24},{24,16},{32,40},{40,32},{48,56},{56,48},{64,72... | collective-permute-start | bytes 1425416 | tf_op jit(solution)/shard_map/ppermute | solution.py:332
  4.0 2.4 %collective-permute-start.1 = (bf16[1,2,64,1856]{3,2,1,0:T(8,128)(2,1)}, bf16[1,2,64,1856]{3,2,1,0:T(8,128)(2,1)S(1)}, u32[]{:S(2)}, u32[]{:S(2)}) collective-permute-start(bf16[1,2,64,1856]{3,2,1,0:T(8,128)(2,1)} %own_b.1), channel_id=1, source_target_pairs={{0,8},{8,0},{16,24},{24,16},{32,40},{40,32},{48,56},{56,48},{64,72... | collective-permute-start | bytes 1425416 | tf_op jit(solution)/shard_map/ppermute | solution.py:332
  8.5 12.8 %copy-start.5 = (s32[2]{0:T(128)S(1)}, s32[2]{0:T(128)}, u32[]{:S(2)}) copy-start(s32[2]{0:T(128)} %param.17) | copy-start | bytes 28
  8.5 12.7 %copy-start.2 = (f32[2]{0:T(128)S(1)}, f32[2]{0:T(128)}, u32[]{:S(2)}) copy-start(f32[2]{0:T(128)} %param.16) | copy-start | bytes 28
  8.5 12.7 %copy-start.3 = (s32[2]{0:T(128)S(1)}, s32[2]{0:T(128)}, u32[]{:S(2)}) copy-start(s32[2]{0:T(128)} %owner.1) | copy-start | bytes 28
  8.6 24.2 %collective-permute-start.4 = (bf16[2,1856,256]{2,1,0:T(8,128)(2,1)S(1)}, bf16[2,1856,256]{2,1,0:T(8,128)(2,1)}, u32[]{:S(2)}, u32[]{:S(2)}) collective-permute-start(bf16[2,1856,256]{2,1,0:T(8,128)(2,1)S(1)} %bitcast.24), channel_id=1, source_target_pairs={{0,8},{8,0},{16,24},{24,16},{32,40},{40,32},{48,56},{56,48},{64,72... | collective-permute-start | bytes 5701640 | tf_op jit(solution)/shard_map/ppermute | solution.py:332
  9.0 23.8 %collective-permute-start.5 = (bf16[2,1856,256]{2,1,0:T(8,128)(2,1)}, bf16[2,1856,256]{2,1,0:T(8,128)(2,1)}, u32[]{:S(2)}, u32[]{:S(2)}) collective-permute-start(bf16[2,1856,256]{2,1,0:T(8,128)(2,1)} %bitcast.33), channel_id=1, source_target_pairs={{0,8},{8,0},{16,24},{24,16},{32,40},{40,32},{48,56},{56,48},{64,72... | collective-permute-start | bytes 5701640 | tf_op jit(solution)/shard_map/ppermute | solution.py:332
  9.4 23.4 %all-to-all-start = ((bf16[16,8,1856]{2,1,0:T(8,128)(2,1)}), bf16[16,8,1856]{2,1,0:T(8,128)(2,1)S(1)}, u32[]{:S(2)}, u32[]{:S(2)}) async-start(bf16[16,8,1856]{2,1,0:T(8,128)(2,1)} %bitcast.37), calls=%async_computation | async-start | bytes 983040 | tf_op jit(solution)/shard_map/all_to_all | solution.py:335
  20.6 5.3 %collective-permute-start.3 = (bf16[2,64,1856]{2,1,0:T(8,128)(2,1)}, bf16[2,64,1856]{2,1,0:T(8,128)(2,1)S(1)}, u32[]{:S(2)}, u32[]{:S(2)}) collective-permute-start(bf16[2,64,1856]{2,1,0:T(8,128)(2,1)} %get-tuple-element.53), channel_id=1, source_target_pairs={{0,8},{8,0},{16,24},{24,16},{32,40},{40,32},{48,56},{56,48},{64,72... | collective-permute-start | bytes 1425416 | tf_op jit(solution)/shard_map/ppermute | solution.py:332
  24.5 1.2 collective-permute-start.2
  33.7 21.0 %all-to-all-start.1 = ((bf16[16,8,1920]{2,1,0:T(8,128)(2,1)}), bf16[16,8,1920]{2,1,0:T(8,128)(2,1)S(1)}, u32[]{:S(2)}, u32[]{:S(2)}) async-start(bf16[16,8,1920]{2,1,0:T(8,128)(2,1)} %broadcast_in_dim.2), calls=%async_computation.1 | async-start | bytes 983040 | tf_op jit(solution)/shard_map/all_to_all | solution.py:335
  79.0 23.1 %all-to-all-start.3 = ((bf16[16,8,1856]{2,1,0:T(8,128)(2,1)}), bf16[16,8,1856]{2,1,0:T(8,128)(2,1)S(1)}, u32[]{:S(2)}, u32[]{:S(2)}) async-start(bf16[16,8,1856]{2,1,0:T(8,128)(2,1)} %bitcast.38), calls=%async_computation.3 | async-start | bytes 983040 | tf_op jit(solution)/shard_map/all_to_all | solution.py:335
  102.1 36.0 %copy-start.1 = (bf16[2,2,64,1,128]{4,2,3,1,0:T(8,128)(2,1)S(1)}, bf16[2,2,64,1,128]{4,2,3,1,0:T(8,128)(2,1)}, u32[]{:S(2)}) copy-start(bf16[2,2,64,1,128]{4,2,3,1,0:T(8,128)(2,1)} %param.24) | copy-start | bytes 196612
  123.1 14.9 %collective-permute-start.6 = (bf16[128,1856]{1,0:T(8,128)(2,1)S(1)}, bf16[128,1856]{1,0:T(8,128)(2,1)S(1)}, u32[]{:S(2)}, u32[]{:S(2)}) collective-permute-start(bf16[128,1856]{1,0:T(8,128)(2,1)S(1)} %bitcast.27), channel_id=1, source_target_pairs={{0,8},{8,0},{16,24},{24,16},{32,40},{40,32},{48,56},{56,48},{64,72... | collective-permute-start | bytes 1425416 | tf_op jit(solution)/shard_map/ppermute | solution.py:332

commit v5 on v4

--- a/solution.py
+++ b/solution.py
@@ -249,7 +249,7 @@
                 out_ref[s, 0, :, at : at + half] = even[:, :half].astype(bf16)
 
 
-def attend(core, ranks, fresh, far_fresh, frozen, kv, new_kv, valid, rows=32):
+def attend(core, ranks, fresh, far_fresh, frozen, kv, new_kv, valid, rows=64):
     steps, layers, rows_dev, width = frozen.shape
     slots, lanes = kv.shape[2:]
     factor = jax.ShapeDtypeStruct((layers, R, width), bf16)
@@ -379,6 +379,7 @@
     packed = jnp.concatenate([*split3(info[0]), info[1]]).astype(bf16)
     tail = jnp.zeros((rows, 64), bf16).at[0, : packed.shape[0]].set(packed)
     owner_chip = pick(layer_owner, core) // 2
+    info = info.reshape(-1)
     arrived, owner_chip, tail, info, valid, dec, far_dec, far_act, far_cot = (
         lax.optimization_barrier(
             (arrived, owner_chip, tail, info, valid.astype(f32), dec, far_dec, far_act, far_cot)
@@ -395,7 +396,7 @@
     parts, advantage = local_call(
         project_kernel,
         "project",
-        scalars + [info.reshape(-1)],
+        scalars + [info],
         [factors],
         token_arrays,
         (n_tensor, 2 * R, 2 * tokens),

time: 148 us -> 146 us (0.986)
  blocking collectives: 46.9 us -> 67.7 us
  waiting for transfers between devices: 37.8 us -> 23.7 us
  starting transfers between devices: 33.7 us -> 26.8 us
    all_to_all x1 -> x2, blocking collectives: 20.2 us -> 41 us  [across_chips(): return lax.all_to_all(x, 'dp', 0, 0, axis_index_groups=same_core)]
    all_to_all x3 -> x2, waiting for transfers between devices: 34.4 us -> 20.3 us  [across_chips(): return lax.all_to_all(x, 'dp', 0, 0, axis_index_groups=same_core)]
    all_to_all x3 -> x2, starting transfers between devices: 25.7 us -> 18.8 us  [across_chips(): return lax.all_to_all(x, 'dp', 0, 0, axis_index_groups=same_core)]
  transfers between devices with their start and end apart: 10 -> 9, of which waited for: 6 -> 5; matrix products, arithmetic and copies ran while one was open for 2% -> 2% of each run, Pallas kernels for 1% -> 1%
where the time goes in v5:
time: 146 us
  blocking collectives  67.7 us (46%)
  starting transfers between devices  26.8 us (18%)
  waiting for transfers between devices  23.7 us (16%)
  Pallas kernels  20.7 us (14%)
  between operations  3.38 us (2%)
  local copies, waits for them, and re-layouts  2.79 us (2%)
    all_to_all x2, blocking collectives, across_chips(): return lax.all_to_all(x, 'dp', 0, 0, axis_index_groups=same_core)  41 us
    all_to_all x2, waiting for transfers between devices, across_chips(): return lax.all_to_all(x, 'dp', 0, 0, axis_index_groups=same_core)  20.3 us
    all_to_all x2, starting transfers between devices, across_chips(): return lax.all_to_all(x, 'dp', 0, 0, axis_index_groups=same_core)  18.8 us
    all_to_all x1, blocking collectives, across_tensor(): return lax.all_to_all(x, 'tensor', 0, 0)  16.1 us
    pallas_call x5, Pallas kernels, local_call(): pl.pallas_call(kernel, grid_spec=pltpu.PrefetchScalarGridSpec(num_scalar_...  12.6 us
    all_to_all x1, blocking collectives, shards(): lax.all_to_all(ranks.reshape(n_tensor * 2, R, steps * rows_dev), ('dp', '...  10.5 us
    pallas_call x1, Pallas kernels, attend(): pl.pallas_call(attend_kernel, grid_spec=pltpu.PrefetchScalarGridSpec(num_...  8.11 us
    ppermute x7, starting transfers between devices, core_swap(): return lax.ppermute(x, 'dp', swap)  8 us
  transfers between devices with their start and end apart: 9, of which 5 were waited for; matrix products, arithmetic and copies ran while one was open for 2% of the time, Pallas kernels for 1%

profile of v5, /device:TPU:1, one launch (start us, length us, event | category | flops | bytes accessed | tf_op | source)
XLA Modules:
  0.0 145.6 jit_solution(15661672858926855644)
XLA Ops:
  0.6 0.0 copy-start
  0.6 0.0 copy-start.4
  0.7 3.3 %collective-permute-start = (bf16[1,2,64,1856]{3,2,1,0:T(8,128)(2,1)}, bf16[1,2,64,1856]{3,2,1,0:T(8,128)(2,1)S(1)}, u32[]{:S(2)}, u32[]{:S(2)}) collective-permute-start(bf16[1,2,64,1856]{3,2,1,0:T(8,128)(2,1)} %own_a.1), channel_id=1, source_target_pairs={{0,8},{8,0},{16,24},{24,16},{32,40},{40,32},{48,56},{56,48},{64,72... | collective-permute-start | bytes 1425416 | tf_op jit(solution)/shard_map/ppermute | solution.py:332
  4.0 0.1 collective-permute-start.1
  4.1 1.6 %collective-permute-done.far_a = bf16[1,2,64,1856]{3,2,1,0:T(8,128)(2,1)S(1)} collective-permute-done((bf16[1,2,64,1856]{3,2,1,0:T(8,128)(2,1)}, bf16[1,2,64,1856]{3,2,1,0:T(8,128)(2,1)S(1)}, u32[]{:S(2)}, u32[]{:S(2)}) %collective-permute-start) | collective-permute-done | bytes 475168 | tf_op jit(solution)/shard_map/ppermute | solution.py:332
  5.7 0.7 collective-permute-done.1.far_b
  6.4 2.5 %message.1 = bf16[128,1856]{1,0:T(8,128)(2,1)} custom-call(s32[1]{0:T(128)} %bitcast.core, s32[2]{0:T(128)} %owner.1, bf16[1,2,64,1856]{3,2,1,0:T(8,128)(2,1)} %own_a.1, bf16[1,2,64,1856]{3,2,1,0:T(8,128)(2,1)} %own_b.1, bf16[1,2,64,1856]{3,2,1,0:T(8,128)(2,1)S(1)} %collective-permute-done.far_a, bf16[1,2,64,1856]{3,2,1,0:T(8,128)(2,1)S(1)} %collective-permute-done.1.far_b), custom_call_target="tpu_custom_call" | custom-call | tf_op jit(solution)/shard_map/message/pallas_call | solution.py:288
  8.8 0.0 copy-start.5
  8.9 0.0 copy-start.2
  8.9 0.0 copy-start.3
  8.9 0.0 copy-done
  8.9 0.5 collective-permute-start.4
  9.4 0.1 collective-permute-start.5
  9.5 0.1 compare_and_fusion
  9.6 0.0 copy-done.4
  9.6 0.1 iota_compare_fusion
  9.7 9.2 %all-to-all-start = ((bf16[16,8,1856]{2,1,0:T(8,128)(2,1)}), bf16[16,8,1856]{2,1,0:T(8,128)(2,1)S(1)}, u32[]{:S(2)}, u32[]{:S(2)}) async-start(bf16[16,8,1856]{2,1,0:T(8,128)(2,1)} %bitcast.37), calls=%async_computation | async-start | bytes 983040 | tf_op jit(solution)/shard_map/all_to_all | solution.py:335
  18.9 2.0 %dynamic-slice_bitcast_fusion = (bf16[2,64,1856]{2,1,0:T(8,128)(2,1)}, bf16[2,64,1856]{2,1,0:T(8,128)(2,1)S(1)}) fusion(bf16[2,2,64,1856]{3,2,1,0:T(8,128)(2,1)} %param.22, s32[]{:T(128)S(6)} %select_n.31, s32[]{:T(128)S(6)} %select_n.29), kind=kLoop, calls=%fused_computation | loop fusion | bytes 1900552 | tf_op jit(solution)/shard_map/jit(dynamic_index_in_dim)/squeeze | solution.py:22
  20.9 0.7 collective-permute-start.3
  21.6 0.0 copy-done.5
  21.6 0.0 copy-done.2
  21.6 0.0 copy-done.3
  21.6 0.6 dynamic_slice.15
  24.8 0.1 collective-permute-start.2
  24.9 1.1 collective-permute-done.2
  26.0 0.1 fusion.14
  26.1 0.1 reshape.174.info
  26.2 0.1 fusion.8
  26.3 0.0 collective-permute-done.3.far_dec
  26.3 6.8 %all-to-all-done = bf16[16,8,1856]{2,1,0:T(8,128)(2,1)S(1)} async-done(((bf16[16,8,1856]{2,1,0:T(8,128)(2,1)}), bf16[16,8,1856]{2,1,0:T(8,128)(2,1)S(1)}, u32[]{:S(2)}, u32[]{:S(2)}) %all-to-all-start) | async-done | bytes 475168 | tf_op jit(solution)/shard_map/all_to_all | solution.py:335
  33.1 0.0 collective-permute-done.4.far_act
  33.1 0.0 collective-permute-done.5.far_cot
  33.1 0.1 pad_maximum_fusion
  33.2 20.8 %all_to_all.30 = bf16[16,8,1920]{2,1,0:T(8,128)(2,1)S(1)} all-to-all(bf16[16,8,1920]{2,1,0:T(8,128)(2,1)S(1)} %broadcast_in_dim.2), channel_id=1, replica_groups={{0,16,32,48,64,80,96,112,128,144,160,176,192,208,224,240},{8,24,40,56,7..., dimensions={0} | all-to-all | bytes 983040 | tf_op jit(solution)/shard_map/all_to_all | solution.py:335
  54.0 4.3 %project.1 = (bf16[8,128,512]{2,1,0:T(8,128)(2,1)}, f32[1,512]{1,0:T(1,128)S(1)}) custom-call(s32[1]{0:T(128)} %bitcast.core, f32[8]{0:T(128)S(1)} %reshape.174.info, bf16[128,1920]{1,0:T(8,128)(2,1)S(1)} %bitcast.30, bf16[2,1856,256]{2,1,0:T(8,128)(2,1)S(1)} %bitcast.25, bf16[2,1856,256]{2,1,0:T(8,128)(2,1)} %collective-permute-done.4.far_act, ...), custom_call_target="tpu_custom_call" | custom-call | tf_op jit(solution)/shard_map/project/pallas_call | solution.py:288
  58.4 16.1 %all_to_all.31.parts = bf16[8,128,512]{2,1,0:T(8,128)(2,1)S(1)} all-to-all(bf16[8,128,512]{2,1,0:T(8,128)(2,1)} %get-tuple-element.46), channel_id=1, replica_groups=mesh['dp'=32,'tensor'=8] {'tensor'}, dimensions={0} | all-to-all | bytes 2097152 | tf_op jit(solution)/shard_map/all_to_all | solution.py:338
  74.5 3.8 %grads.1 = bf16[128,1856]{1,0:T(8,128)(2,1)} custom-call(s32[1]{0:T(128)} %bitcast.core, bf16[8,128,512]{2,1,0:T(8,128)(2,1)S(1)} %all_to_all.31.parts, f32[1,512]{1,0:T(1,128)S(1)} %get-tuple-element.47.adv_ref, bf16[2,1856,256]{2,1,0:T(8,128)(2,1)S(1)} %bitcast.26, bf16[2,1856,256]{2,1,0:T(8,128)(2,1)} %collective-permute-done.4.far_act, ...), custom_call_target="tpu_custom_call" | custom-call | tf_op jit(solution)/shard_map/grads/pallas_call | solution.py:288
  78.3 9.7 %all-to-all-start.3 = ((bf16[16,8,1856]{2,1,0:T(8,128)(2,1)}), bf16[16,8,1856]{2,1,0:T(8,128)(2,1)S(1)}, u32[]{:S(2)}, u32[]{:S(2)}) async-start(bf16[16,8,1856]{2,1,0:T(8,128)(2,1)} %bitcast.38), calls=%async_computation.3 | async-start | bytes 983040 | tf_op jit(solution)/shard_map/all_to_all | solution.py:335
  88.0 13.5 %all-to-all-done.3.arrived = bf16[16,8,1856]{2,1,0:T(8,128)(2,1)S(1)} async-done(((bf16[16,8,1856]{2,1,0:T(8,128)(2,1)}), bf16[16,8,1856]{2,1,0:T(8,128)(2,1)S(1)}, u32[]{:S(2)}, u32[]{:S(2)}) %all-to-all-start.3) | async-done | bytes 475168 | tf_op jit(solution)/shard_map/all_to_all | solution.py:335
  101.5 0.0 copy-start.1
  101.5 0.9 update.1
  102.3 20.2 %all_to_all.32 = bf16[16,8,1856]{2,1,0:T(8,128)(2,1)S(1)} all-to-all(bf16[16,8,1856]{2,1,0:T(8,128)(2,1)} %update.1), channel_id=1, replica_groups={{0,16,32,48,64,80,96,112,128,144,160,176,192,208,224,240},{8,24,40,56,7..., dimensions={0} | all-to-all | bytes 950272 | tf_op jit(solution)/shard_map/all_to_all | solution.py:335
  122.5 3.2 %collective-permute-start.6 = (bf16[128,1856]{1,0:T(8,128)(2,1)S(1)}, bf16[128,1856]{1,0:T(8,128)(2,1)S(1)}, u32[]{:S(2)}, u32[]{:S(2)}) collective-permute-start(bf16[128,1856]{1,0:T(8,128)(2,1)S(1)} %bitcast.27), channel_id=1, source_target_pairs={{0,8},{8,0},{16,24},{24,16},{32,40},{40,32},{48,56},{56,48},{64,72... | collective-permute-start | bytes 1425416 | tf_op jit(solution)/shard_map/ppermute | solution.py:332
  125.7 1.2 decode_rank.1
  126.9 10.5 %all_to_all.33 = bf16[16,64,128]{2,1,0:T(8,128)(2,1)S(1)} all-to-all(bf16[16,64,128]{2,1,0:T(8,128)(2,1)} %bitcast.39), channel_id=1, replica_groups={{0,8,1,9,2,10,3,11,4,12,5,13,6,14,7,15},{16,24,17,25,18,26,19,27,20,28,..., dimensions={0} | all-to-all | bytes 524288 | tf_op jit(solution)/shard_map/all_to_all | solution.py:445
  137.5 0.0 collective-permute-done.6.far_fresh
  137.5 0.0 copy-done.1
  137.5 8.1 %attend.1 = (bf16[2,64,1856]{2,1,0:T(8,128)(2,1)}, bf16[2,64,1856]{2,1,0:T(8,128)(2,1)}, bf16[2,2,64,1856]{3,2,1,0:T(8,128)(2,1)}) custom-call(s32[1]{0:T(128)} %bitcast.core, bf16[8,2,64,128]{3,2,1,0:T(8,128)(2,1)S(1)} %bitcast.31, bf16[128,1856]{1,0:T(8,128)(2,1)S(1)} %bitcast.29, bf16[128,1856]{1,0:T(8,128)(2,1)S(1)} %collective-permute-done.6.far_fresh, ...), custom_call_target="tpu_custom_call" | custom-call | tf_op jit(solution)/shard_map/attend/pallas_call | solution.py:256
  (9 shorter events, 0.1 us)
Async XLA Ops:
  0.6 8.3 %copy-start = (bf16[2,256,1856]{1,2,0:T(8,128)(2,1)S(1)}, bf16[2,256,1856]{1,2,0:T(8,128)(2,1)}, u32[]{:S(2)}) copy-start(bf16[2,256,1856]{1,2,0:T(8,128)(2,1)} %param.14) | copy-start | bytes 5701636
  0.6 8.9 %copy-start.4 = (s32[64]{0:T(128)S(1)}, s32[64]{0:T(128)}, u32[]{:S(2)}) copy-start(s32[64]{0:T(128)} %param.25) | copy-start | bytes 772
  0.7 5.0 %collective-permute-start = (bf16[1,2,64,1856]{3,2,1,0:T(8,128)(2,1)}, bf16[1,2,64,1856]{3,2,1,0:T(8,128)(2,1)S(1)}, u32[]{:S(2)}, u32[]{:S(2)}) collective-permute-start(bf16[1,2,64,1856]{3,2,1,0:T(8,128)(2,1)} %own_a.1), channel_id=1, source_target_pairs={{0,8},{8,0},{16,24},{24,16},{32,40},{40,32},{48,56},{56,48},{64,72... | collective-permute-start | bytes 1425416 | tf_op jit(solution)/shard_map/ppermute | solution.py:332
  4.0 2.4 %collective-permute-start.1 = (bf16[1,2,64,1856]{3,2,1,0:T(8,128)(2,1)}, bf16[1,2,64,1856]{3,2,1,0:T(8,128)(2,1)S(1)}, u32[]{:S(2)}, u32[]{:S(2)}) collective-permute-start(bf16[1,2,64,1856]{3,2,1,0:T(8,128)(2,1)} %own_b.1), channel_id=1, source_target_pairs={{0,8},{8,0},{16,24},{24,16},{32,40},{40,32},{48,56},{56,48},{64,72... | collective-permute-start | bytes 1425416 | tf_op jit(solution)/shard_map/ppermute | solution.py:332
  8.8 12.8 %copy-start.5 = (s32[2]{0:T(128)S(1)}, s32[2]{0:T(128)}, u32[]{:S(2)}) copy-start(s32[2]{0:T(128)} %param.17) | copy-start | bytes 28
  8.9 12.7 %copy-start.2 = (f32[2]{0:T(128)S(1)}, f32[2]{0:T(128)}, u32[]{:S(2)}) copy-start(f32[2]{0:T(128)} %param.16) | copy-start | bytes 28
  8.9 12.7 %copy-start.3 = (s32[2]{0:T(128)S(1)}, s32[2]{0:T(128)}, u32[]{:S(2)}) copy-start(s32[2]{0:T(128)} %owner.1) | copy-start | bytes 28
  8.9 24.2 %collective-permute-start.4 = (bf16[2,1856,256]{2,1,0:T(8,128)(2,1)S(1)}, bf16[2,1856,256]{2,1,0:T(8,128)(2,1)}, u32[]{:S(2)}, u32[]{:S(2)}) collective-permute-start(bf16[2,1856,256]{2,1,0:T(8,128)(2,1)S(1)} %bitcast.24), channel_id=1, source_target_pairs={{0,8},{8,0},{16,24},{24,16},{32,40},{40,32},{48,56},{56,48},{64,72... | collective-permute-start | bytes 5701640 | tf_op jit(solution)/shard_map/ppermute | solution.py:332
  9.4 23.8 %collective-permute-start.5 = (bf16[2,1856,256]{2,1,0:T(8,128)(2,1)}, bf16[2,1856,256]{2,1,0:T(8,128)(2,1)}, u32[]{:S(2)}, u32[]{:S(2)}) collective-permute-start(bf16[2,1856,256]{2,1,0:T(8,128)(2,1)} %bitcast.33), channel_id=1, source_target_pairs={{0,8},{8,0},{16,24},{24,16},{32,40},{40,32},{48,56},{56,48},{64,72... | collective-permute-start | bytes 5701640 | tf_op jit(solution)/shard_map/ppermute | solution.py:332
  9.7 23.4 %all-to-all-start = ((bf16[16,8,1856]{2,1,0:T(8,128)(2,1)}), bf16[16,8,1856]{2,1,0:T(8,128)(2,1)S(1)}, u32[]{:S(2)}, u32[]{:S(2)}) async-start(bf16[16,8,1856]{2,1,0:T(8,128)(2,1)} %bitcast.37), calls=%async_computation | async-start | bytes 983040 | tf_op jit(solution)/shard_map/all_to_all | solution.py:335
  20.9 5.4 %collective-permute-start.3 = (bf16[2,64,1856]{2,1,0:T(8,128)(2,1)}, bf16[2,64,1856]{2,1,0:T(8,128)(2,1)S(1)}, u32[]{:S(2)}, u32[]{:S(2)}) collective-permute-start(bf16[2,64,1856]{2,1,0:T(8,128)(2,1)} %get-tuple-element.53), channel_id=1, source_target_pairs={{0,8},{8,0},{16,24},{24,16},{32,40},{40,32},{48,56},{56,48},{64,72... | collective-permute-start | bytes 1425416 | tf_op jit(solution)/shard_map/ppermute | solution.py:332
  24.8 1.2 collective-permute-start.2
  78.3 23.1 %all-to-all-start.3 = ((bf16[16,8,1856]{2,1,0:T(8,128)(2,1)}), bf16[16,8,1856]{2,1,0:T(8,128)(2,1)S(1)}, u32[]{:S(2)}, u32[]{:S(2)}) async-start(bf16[16,8,1856]{2,1,0:T(8,128)(2,1)} %bitcast.38), calls=%async_computation.3 | async-start | bytes 983040 | tf_op jit(solution)/shard_map/all_to_all | solution.py:335
  101.5 36.0 %copy-start.1 = (bf16[2,2,64,1,128]{4,2,3,1,0:T(8,128)(2,1)S(1)}, bf16[2,2,64,1,128]{4,2,3,1,0:T(8,128)(2,1)}, u32[]{:S(2)}) copy-start(bf16[2,2,64,1,128]{4,2,3,1,0:T(8,128)(2,1)} %param.24) | copy-start | bytes 196612
  122.5 14.9 %collective-permute-start.6 = (bf16[128,1856]{1,0:T(8,128)(2,1)S(1)}, bf16[128,1856]{1,0:T(8,128)(2,1)S(1)}, u32[]{:S(2)}, u32[]{:S(2)}) collective-permute-start(bf16[128,1856]{1,0:T(8,128)(2,1)S(1)} %bitcast.27), channel_id=1, source_target_pairs={{0,8},{8,0},{16,24},{24,16},{32,40},{40,32},{48,56},{56,48},{64,72... | collective-permute-start | bytes 1425416 | tf_op jit(solution)/shard_map/ppermute | solution.py:332

commit v6 on v5

--- a/solution.py
+++ b/solution.py
@@ -380,10 +380,8 @@
     tail = jnp.zeros((rows, 64), bf16).at[0, : packed.shape[0]].set(packed)
     owner_chip = pick(layer_owner, core) // 2
     info = info.reshape(-1)
-    arrived, owner_chip, tail, info, valid, dec, far_dec, far_act, far_cot = (
-        lax.optimization_barrier(
-            (arrived, owner_chip, tail, info, valid.astype(f32), dec, far_dec, far_act, far_cot)
-        )
+    arrived, owner_chip, tail, info, valid, dec, far_dec = lax.optimization_barrier(
+        (arrived, owner_chip, tail, info, valid.astype(f32), dec, far_dec)
     )
     piece = pick(arrived, owner_chip)
 

time: 146 us -> 146 us (level)
    all_to_all x2, waiting for transfers between devices: 20.3 us -> 17.9 us  [across_chips(): return lax.all_to_all(x, 'dp', 0, 0, axis_index_groups=same_core)]
  transfers between devices with their start and end apart: 9 -> 9, of which waited for: 5 -> 5; matrix products, arithmetic and copies ran while one was open for 2% -> 3% of each run, Pallas kernels for 1% -> 1%
where the time goes in v6:
time: 146 us; the launch traced here: 144 us
  blocking collectives  67.7 us (46%)
  starting transfers between devices  26.9 us (18%)
  waiting for transfers between devices  22.3 us (15%)
  Pallas kernels  20.3 us (14%)
  between operations  3.36 us (2%)
  local copies, waits for them, and re-layouts  2.79 us (2%)
    all_to_all x2, blocking collectives, across_chips(): return lax.all_to_all(x, 'dp', 0, 0, axis_index_groups=same_core)  41 us
    all_to_all x2, starting transfers between devices, across_chips(): return lax.all_to_all(x, 'dp', 0, 0, axis_index_groups=same_core)  19 us
    all_to_all x2, waiting for transfers between devices, across_chips(): return lax.all_to_all(x, 'dp', 0, 0, axis_index_groups=same_core)  17.9 us
    all_to_all x1, blocking collectives, across_tensor(): return lax.all_to_all(x, 'tensor', 0, 0)  16.1 us
    pallas_call x5, Pallas kernels, local_call(): pl.pallas_call(kernel, grid_spec=pltpu.PrefetchScalarGridSpec(num_scalar_...  12.2 us
    all_to_all x1, blocking collectives, shards(): lax.all_to_all(ranks.reshape(n_tensor * 2, R, steps * rows_dev), ('dp', '...  10.5 us
    pallas_call x1, Pallas kernels, attend(): pl.pallas_call(attend_kernel, grid_spec=pltpu.PrefetchScalarGridSpec(num_...  8.11 us
    ppermute x7, starting transfers between devices, core_swap(): return lax.ppermute(x, 'dp', swap)  7.91 us
  transfers between devices with their start and end apart: 9, of which 5 were waited for; matrix products, arithmetic and copies ran while one was open for 3% of the time, Pallas kernels for 1%

profile of v6, /device:TPU:1, one launch (start us, length us, event | category | flops | bytes accessed | tf_op | source)
XLA Modules:
  0.0 144.5 jit_solution(16063525589355963556)
XLA Ops:
  0.6 3.3 %collective-permute-start = (bf16[1,2,64,1856]{3,2,1,0:T(8,128)(2,1)}, bf16[1,2,64,1856]{3,2,1,0:T(8,128)(2,1)S(1)}, u32[]{:S(2)}, u32[]{:S(2)}) collective-permute-start(bf16[1,2,64,1856]{3,2,1,0:T(8,128)(2,1)} %own_a.1), channel_id=1, source_target_pairs={{0,8},{8,0},{16,24},{24,16},{32,40},{40,32},{48,56},{56,48},{64,72... | collective-permute-start | bytes 1425416 | tf_op jit(solution)/shard_map/ppermute | solution.py:332
  4.0 0.1 collective-permute-start.1
  4.1 0.1 compare_and_fusion
  4.1 0.7 iota_compare_fusion
  4.9 0.7 collective-permute-done.far_a
  5.7 0.7 collective-permute-done.1.far_b
  6.4 2.1 %message.1 = bf16[128,1856]{1,0:T(8,128)(2,1)} custom-call(s32[1]{0:T(128)} %bitcast.core, s32[2]{0:T(128)} %owner.1, bf16[1,2,64,1856]{3,2,1,0:T(8,128)(2,1)} %own_a.1, bf16[1,2,64,1856]{3,2,1,0:T(8,128)(2,1)} %own_b.1, bf16[1,2,64,1856]{3,2,1,0:T(8,128)(2,1)S(1)} %collective-permute-done.far_a, bf16[1,2,64,1856]{3,2,1,0:T(8,128)(2,1)S(1)} %collective-permute-done.1.far_b), custom_call_target="tpu_custom_call" | custom-call | tf_op jit(solution)/shard_map/message/pallas_call | solution.py:288
  8.5 0.0 copy-start
  8.5 0.0 copy-start.4
  8.5 0.0 copy-start.2
  8.5 0.0 copy-start.3
  8.5 9.3 %all-to-all-start = ((bf16[16,8,1856]{2,1,0:T(8,128)(2,1)}), bf16[16,8,1856]{2,1,0:T(8,128)(2,1)S(1)}, u32[]{:S(2)}, u32[]{:S(2)}) async-start(bf16[16,8,1856]{2,1,0:T(8,128)(2,1)} %bitcast.37), calls=%async_computation | async-start | bytes 983040 | tf_op jit(solution)/shard_map/all_to_all | solution.py:335
  17.9 2.0 %dynamic-slice_bitcast_fusion = (bf16[2,64,1856]{2,1,0:T(8,128)(2,1)}, bf16[2,64,1856]{2,1,0:T(8,128)(2,1)S(1)}) fusion(bf16[2,2,64,1856]{3,2,1,0:T(8,128)(2,1)} %param.22, s32[]{:T(128)S(6)} %select_n.31, s32[]{:T(128)S(6)} %select_n.29), kind=kLoop, calls=%fused_computation | loop fusion | bytes 1900552 | tf_op jit(solution)/shard_map/jit(dynamic_index_in_dim)/squeeze | solution.py:22
  19.9 0.7 collective-permute-start.3
  20.6 0.0 copy-done
  20.6 0.0 collective-permute-start.4
  20.6 0.5 collective-permute-start.5
  21.1 0.0 copy-done.4
  21.1 0.0 copy-done.2
  21.1 0.0 copy-done.3
  21.1 0.6 dynamic_slice.15
  24.3 0.1 collective-permute-start.2
  24.4 2.9 %collective-permute-done.2 = f32[2,2]{1,0:T(2,128)S(1)} collective-permute-done((f32[2,2]{1,0:T(2,128)S(1)}, f32[2,2]{1,0:T(2,128)S(1)}, u32[]{:S(2)}, u32[]{:S(2)}) %collective-permute-start.2) | collective-permute-done | bytes 48 | tf_op jit(solution)/shard_map/ppermute | solution.py:332
  27.3 0.1 fusion.14
  27.4 0.1 reshape.174.info
  27.5 0.1 fusion.8
  27.6 0.0 collective-permute-done.3.far_dec
  27.6 4.5 %all-to-all-done = bf16[16,8,1856]{2,1,0:T(8,128)(2,1)S(1)} async-done(((bf16[16,8,1856]{2,1,0:T(8,128)(2,1)}), bf16[16,8,1856]{2,1,0:T(8,128)(2,1)S(1)}, u32[]{:S(2)}, u32[]{:S(2)}) %all-to-all-start) | async-done | bytes 475168 | tf_op jit(solution)/shard_map/all_to_all | solution.py:335
  32.1 0.1 pad_maximum_fusion
  32.2 20.8 %all_to_all.30 = bf16[16,8,1920]{2,1,0:T(8,128)(2,1)S(1)} all-to-all(bf16[16,8,1920]{2,1,0:T(8,128)(2,1)S(1)} %broadcast_in_dim.2), channel_id=1, replica_groups={{0,16,32,48,64,80,96,112,128,144,160,176,192,208,224,240},{8,24,40,56,7..., dimensions={0} | all-to-all | bytes 983040 | tf_op jit(solution)/shard_map/all_to_all | solution.py:335
  53.0 0.0 collective-permute-done.4.far_act
  53.0 0.0 collective-permute-done.5.far_cot
  53.0 4.2 %project.1 = (bf16[8,128,512]{2,1,0:T(8,128)(2,1)}, f32[1,512]{1,0:T(1,128)S(1)}) custom-call(s32[1]{0:T(128)} %bitcast.core, f32[8]{0:T(128)S(1)} %reshape.174.info, bf16[128,1920]{1,0:T(8,128)(2,1)S(1)} %bitcast.30, bf16[2,1856,256]{2,1,0:T(8,128)(2,1)S(1)} %bitcast.25, bf16[2,1856,256]{2,1,0:T(8,128)(2,1)} %collective-permute-done.4.far_act, ...), custom_call_target="tpu_custom_call" | custom-call | tf_op jit(solution)/shard_map/project/pallas_call | solution.py:288
  57.3 16.1 %all_to_all.31.parts = bf16[8,128,512]{2,1,0:T(8,128)(2,1)S(1)} all-to-all(bf16[8,128,512]{2,1,0:T(8,128)(2,1)} %get-tuple-element.42), channel_id=1, replica_groups=mesh['dp'=32,'tensor'=8] {'tensor'}, dimensions={0} | all-to-all | bytes 2097152 | tf_op jit(solution)/shard_map/all_to_all | solution.py:338
  73.4 3.8 %grads.1 = bf16[128,1856]{1,0:T(8,128)(2,1)} custom-call(s32[1]{0:T(128)} %bitcast.core, bf16[8,128,512]{2,1,0:T(8,128)(2,1)S(1)} %all_to_all.31.parts, f32[1,512]{1,0:T(1,128)S(1)} %get-tuple-element.43.adv_ref, bf16[2,1856,256]{2,1,0:T(8,128)(2,1)S(1)} %bitcast.26, bf16[2,1856,256]{2,1,0:T(8,128)(2,1)} %collective-permute-done.4.far_act, ...), custom_call_target="tpu_custom_call" | custom-call | tf_op jit(solution)/shard_map/grads/pallas_call | solution.py:288
  77.2 9.7 %all-to-all-start.3 = ((bf16[16,8,1856]{2,1,0:T(8,128)(2,1)}), bf16[16,8,1856]{2,1,0:T(8,128)(2,1)S(1)}, u32[]{:S(2)}, u32[]{:S(2)}) async-start(bf16[16,8,1856]{2,1,0:T(8,128)(2,1)} %bitcast.38), calls=%async_computation.3 | async-start | bytes 983040 | tf_op jit(solution)/shard_map/all_to_all | solution.py:335
  86.9 13.5 %all-to-all-done.3.arrived = bf16[16,8,1856]{2,1,0:T(8,128)(2,1)S(1)} async-done(((bf16[16,8,1856]{2,1,0:T(8,128)(2,1)}), bf16[16,8,1856]{2,1,0:T(8,128)(2,1)S(1)}, u32[]{:S(2)}, u32[]{:S(2)}) %all-to-all-start.3) | async-done | bytes 475168 | tf_op jit(solution)/shard_map/all_to_all | solution.py:335
  100.4 0.0 copy-start.1
  100.4 0.9 update.1
  101.2 20.2 %all_to_all.32 = bf16[16,8,1856]{2,1,0:T(8,128)(2,1)S(1)} all-to-all(bf16[16,8,1856]{2,1,0:T(8,128)(2,1)} %update.1), channel_id=1, replica_groups={{0,16,32,48,64,80,96,112,128,144,160,176,192,208,224,240},{8,24,40,56,7..., dimensions={0} | all-to-all | bytes 950272 | tf_op jit(solution)/shard_map/all_to_all | solution.py:335
  121.4 3.2 %collective-permute-start.6 = (bf16[128,1856]{1,0:T(8,128)(2,1)S(1)}, bf16[128,1856]{1,0:T(8,128)(2,1)S(1)}, u32[]{:S(2)}, u32[]{:S(2)}) collective-permute-start(bf16[128,1856]{1,0:T(8,128)(2,1)S(1)} %bitcast.27), channel_id=1, source_target_pairs={{0,8},{8,0},{16,24},{24,16},{32,40},{40,32},{48,56},{56,48},{64,72... | collective-permute-start | bytes 1425416 | tf_op jit(solution)/shard_map/ppermute | solution.py:332
  124.6 1.2 decode_rank.1
  125.8 10.5 %all_to_all.33 = bf16[16,64,128]{2,1,0:T(8,128)(2,1)S(1)} all-to-all(bf16[16,64,128]{2,1,0:T(8,128)(2,1)} %bitcast.39), channel_id=1, replica_groups={{0,8,1,9,2,10,3,11,4,12,5,13,6,14,7,15},{16,24,17,25,18,26,19,27,20,28,..., dimensions={0} | all-to-all | bytes 524288 | tf_op jit(solution)/shard_map/all_to_all | solution.py:443
  136.4 0.0 collective-permute-done.6.far_fresh
  136.4 0.0 copy-done.1
  136.4 8.1 %attend.1 = (bf16[2,64,1856]{2,1,0:T(8,128)(2,1)}, bf16[2,64,1856]{2,1,0:T(8,128)(2,1)}, bf16[2,2,64,1856]{3,2,1,0:T(8,128)(2,1)}) custom-call(s32[1]{0:T(128)} %bitcast.core, bf16[8,2,64,128]{3,2,1,0:T(8,128)(2,1)S(1)} %bitcast.31, bf16[128,1856]{1,0:T(8,128)(2,1)S(1)} %bitcast.29, bf16[128,1856]{1,0:T(8,128)(2,1)S(1)} %collective-permute-done.6.far_fresh, ...), custom_call_target="tpu_custom_call" | custom-call | tf_op jit(solution)/shard_map/attend/pallas_call | solution.py:256
  (9 shorter events, 0.1 us)
Async XLA Ops:
  0.6 5.0 %collective-permute-start = (bf16[1,2,64,1856]{3,2,1,0:T(8,128)(2,1)}, bf16[1,2,64,1856]{3,2,1,0:T(8,128)(2,1)S(1)}, u32[]{:S(2)}, u32[]{:S(2)}) collective-permute-start(bf16[1,2,64,1856]{3,2,1,0:T(8,128)(2,1)} %own_a.1), channel_id=1, source_target_pairs={{0,8},{8,0},{16,24},{24,16},{32,40},{40,32},{48,56},{56,48},{64,72... | collective-permute-start | bytes 1425416 | tf_op jit(solution)/shard_map/ppermute | solution.py:332
  4.0 2.4 %collective-permute-start.1 = (bf16[1,2,64,1856]{3,2,1,0:T(8,128)(2,1)}, bf16[1,2,64,1856]{3,2,1,0:T(8,128)(2,1)S(1)}, u32[]{:S(2)}, u32[]{:S(2)}) collective-permute-start(bf16[1,2,64,1856]{3,2,1,0:T(8,128)(2,1)} %own_b.1), channel_id=1, source_target_pairs={{0,8},{8,0},{16,24},{24,16},{32,40},{40,32},{48,56},{56,48},{64,72... | collective-permute-start | bytes 1425416 | tf_op jit(solution)/shard_map/ppermute | solution.py:332
  8.5 12.1 %copy-start = (bf16[2,256,1856]{1,2,0:T(8,128)(2,1)S(1)}, bf16[2,256,1856]{1,2,0:T(8,128)(2,1)}, u32[]{:S(2)}) copy-start(bf16[2,256,1856]{1,2,0:T(8,128)(2,1)} %param.14) | copy-start | bytes 5701636
  8.5 12.6 %copy-start.4 = (s32[2]{0:T(128)S(1)}, s32[2]{0:T(128)}, u32[]{:S(2)}) copy-start(s32[2]{0:T(128)} %param.17) | copy-start | bytes 28
  8.5 12.6 %copy-start.2 = (f32[2]{0:T(128)S(1)}, f32[2]{0:T(128)}, u32[]{:S(2)}) copy-start(f32[2]{0:T(128)} %param.16) | copy-start | bytes 28
  8.5 12.6 %copy-start.3 = (s32[2]{0:T(128)S(1)}, s32[2]{0:T(128)}, u32[]{:S(2)}) copy-start(s32[2]{0:T(128)} %owner.1) | copy-start | bytes 28
  8.5 23.5 %all-to-all-start = ((bf16[16,8,1856]{2,1,0:T(8,128)(2,1)}), bf16[16,8,1856]{2,1,0:T(8,128)(2,1)S(1)}, u32[]{:S(2)}, u32[]{:S(2)}) async-start(bf16[16,8,1856]{2,1,0:T(8,128)(2,1)} %bitcast.37), calls=%async_computation | async-start | bytes 983040 | tf_op jit(solution)/shard_map/all_to_all | solution.py:335
  19.9 7.7 %collective-permute-start.3 = (bf16[2,64,1856]{2,1,0:T(8,128)(2,1)}, bf16[2,64,1856]{2,1,0:T(8,128)(2,1)S(1)}, u32[]{:S(2)}, u32[]{:S(2)}) collective-permute-start(bf16[2,64,1856]{2,1,0:T(8,128)(2,1)} %get-tuple-element.49), channel_id=1, source_target_pairs={{0,8},{8,0},{16,24},{24,16},{32,40},{40,32},{48,56},{56,48},{64,72... | collective-permute-start | bytes 1425416 | tf_op jit(solution)/shard_map/ppermute | solution.py:332
  20.6 32.4 %collective-permute-start.4 = (bf16[2,1856,256]{2,1,0:T(8,128)(2,1)S(1)}, bf16[2,1856,256]{2,1,0:T(8,128)(2,1)}, u32[]{:S(2)}, u32[]{:S(2)}) collective-permute-start(bf16[2,1856,256]{2,1,0:T(8,128)(2,1)S(1)} %bitcast.24), channel_id=1, source_target_pairs={{0,8},{8,0},{16,24},{24,16},{32,40},{40,32},{48,56},{56,48},{64,72... | collective-permute-start | bytes 5701640 | tf_op jit(solution)/shard_map/ppermute | solution.py:332
  20.6 32.4 %collective-permute-start.5 = (bf16[2,1856,256]{2,1,0:T(8,128)(2,1)}, bf16[2,1856,256]{2,1,0:T(8,128)(2,1)}, u32[]{:S(2)}, u32[]{:S(2)}) collective-permute-start(bf16[2,1856,256]{2,1,0:T(8,128)(2,1)} %bitcast.33), channel_id=1, source_target_pairs={{0,8},{8,0},{16,24},{24,16},{32,40},{40,32},{48,56},{56,48},{64,72... | collective-permute-start | bytes 5701640 | tf_op jit(solution)/shard_map/ppermute | solution.py:332
  24.3 3.0 %collective-permute-start.2 = (f32[2,2]{1,0:T(2,128)S(1)}, f32[2,2]{1,0:T(2,128)S(1)}, u32[]{:S(2)}, u32[]{:S(2)}) collective-permute-start(f32[2,2]{1,0:T(2,128)S(1)} %pad_maximum_fusion.1), channel_id=1, source_target_pairs={{0,8},{8,0},{16,24},{24,16},{32,40},{40,32},{48,56},{56,48},{64,72... | collective-permute-start | bytes 56 | tf_op jit(solution)/shard_map/ppermute | solution.py:332
  77.2 23.1 %all-to-all-start.3 = ((bf16[16,8,1856]{2,1,0:T(8,128)(2,1)}), bf16[16,8,1856]{2,1,0:T(8,128)(2,1)S(1)}, u32[]{:S(2)}, u32[]{:S(2)}) async-start(bf16[16,8,1856]{2,1,0:T(8,128)(2,1)} %bitcast.38), calls=%async_computation.3 | async-start | bytes 983040 | tf_op jit(solution)/shard_map/all_to_all | solution.py:335
  100.4 36.0 %copy-start.1 = (bf16[2,2,64,1,128]{4,2,3,1,0:T(8,128)(2,1)S(1)}, bf16[2,2,64,1,128]{4,2,3,1,0:T(8,128)(2,1)}, u32[]{:S(2)}) copy-start(bf16[2,2,64,1,128]{4,2,3,1,0:T(8,128)(2,1)} %param.24) | copy-start | bytes 196612
  121.4 14.9 %collective-permute-start.6 = (bf16[128,1856]{1,0:T(8,128)(2,1)S(1)}, bf16[128,1856]{1,0:T(8,128)(2,1)S(1)}, u32[]{:S(2)}, u32[]{:S(2)}) collective-permute-start(bf16[128,1856]{1,0:T(8,128)(2,1)S(1)} %bitcast.27), channel_id=1, source_target_pairs={{0,8},{8,0},{16,24},{24,16},{32,40},{40,32},{48,56},{56,48},{64,72... | collective-permute-start | bytes 1425416 | tf_op jit(solution)/shard_map/ppermute | solution.py:332
